TPU v7x, 32 devices: a whole 2x2x4 slice. The times are simulated.
32 devices in a mesh: ta: 4 (over z), gx: 2 (over core), gy: 4 (over y, x).
Axes of the slice: x: 2, y: 2, z: 4, core: 2. Of those that a mesh axis runs over, the one named last changes fastest.
Arguments:
- initial_state: float32 [2, 64, 4096], P(None, 'gx', 'gy'), may hold values from 0 to 1
- feed_rate: float32 [64, 4096], P('gx', 'gy'), may hold values from 0.02 to 0.1
- kill_rate: float32 [64, 4096], P('gx', 'gy'), may hold values from 0.03 to 0.09
Outputs:
- final_state: float32 [4, 2, 64, 4096], P('ta', None, 'gx', 'gy')
All inputs are finite; a program needn't handle non-finite values.
Results may differ from a plain program's by a relative error of at most 0.00002.
Values sent between devices are 32-bit elements; how exact they have to be, the bound alone decides.
No kernel may reach another device: no remote copies, remote signals or barrier semaphores. Data moves between devices by JAX's collectives and lax.ppermute only.
A program may use at most 64 MiB of HBM per device.

v0:
```python
import jax
import jax.numpy as jnp
from jax import lax
from jax.sharding import PartitionSpec as P

TURNS = 2


DIFF_U = 0.2
DIFF_V = 0.1
HALF_STEP = 0.5
NODE_WEIGHTS = ((5.0 / 24.0, 1.0 / 3.0, -1.0 / 24.0), (-1.0 / 24.0, 1.0 / 3.0, 5.0 / 24.0))


def padded_2(block, sides, width):
    for axis, dim in sides:
        count = lax.axis_size(axis)
        forward = [(i, i + 1) for i in range(count - 1)]
        backward = [(target, source) for source, target in forward]
        low = lax.ppermute(
            lax.slice_in_dim(block, block.shape[dim] - width, None, axis=dim), axis, forward
        )
        high = lax.ppermute(lax.slice_in_dim(block, 0, width, axis=dim), axis, backward)
        block = jnp.concatenate([low, block, high], axis=dim)
    return block


def shifted(block, axis, distance):
    devices = range(lax.axis_size(axis))
    route = [(i - distance, i) for i in devices if i - distance in devices]
    return lax.ppermute(block, axis, route)


def neighbours(padded, values_in):
    total = (
        padded[..., 2:, 1:-1]
        + padded[..., :-2, 1:-1]
        + padded[..., 1:-1, 2:]
        + padded[..., 1:-1, :-2]
    )
    return total - 4.0 * values_in


def react_rates(state, laplace_val, feed_rate, kill_rate, lap_scale):
    conc_u = state[:, 0]
    conc_v = state[:, 1]
    lap_u = lap_scale * laplace_val[:, 0]
    lap_v = lap_scale * laplace_val[:, 1]
    react_term = conc_u * conc_v * conc_v
    rate_u = DIFF_U * lap_u - react_term + feed_rate * (1.0 - conc_u)
    rate_v = DIFF_V * lap_v + react_term - (feed_rate + kill_rate) * conc_v
    return jnp.stack([rate_u, rate_v], axis=1)


def restrict(values_in):
    total = (
        values_in[..., 0::2, 0::2]
        + values_in[..., 1::2, 0::2]
        + values_in[..., 0::2, 1::2]
        + values_in[..., 1::2, 1::2]
    )
    return total * 0.25


def prolong(values_in):
    return jnp.repeat(jnp.repeat(values_in, 2, axis=-2), 2, axis=-1)


def integrals(rates_old):
    rows = []
    for weights in NODE_WEIGHTS:
        rows.append(
            weights[0] * rates_old[0] + weights[1] * rates_old[1] + weights[2] * rates_old[2]
        )
    return jnp.stack(rows)


def fine_sweep(node_vals, slice_start, rhs_fn):
    old_vals = jnp.concatenate([slice_start[None], node_vals[1:]], axis=0)
    rates_old = rhs_fn(old_vals)
    integ = integrals(rates_old)
    second = slice_start + integ[0]
    rates_new = rhs_fn(second[None])[0]
    third = second + HALF_STEP * (rates_new - rates_old[1]) + integ[1]
    return (jnp.stack([slice_start, second, third]), integ)


def coarse_sweep(start_value, rates_coarse, coarse_integ, rhs_fn):
    rate_first = rhs_fn(start_value[None])[0]
    second = start_value + HALF_STEP * (rate_first - rates_coarse[0]) + coarse_integ[0]
    rate_second = rhs_fn(second[None])[0]
    third = second + HALF_STEP * (rate_second - rates_coarse[1]) + coarse_integ[1]
    return jnp.stack([start_value, second, third])


def per_device(initial_state, feed_rate, kill_rate):
    pass_count = lax.axis_size("ta")
    slice_index = lax.axis_index("ta")
    is_first = slice_index == 0
    coarse_feed = restrict(feed_rate)
    coarse_kill = restrict(kill_rate)

    def fine_rhs(state):
        padded = padded_2(state, (("gx", 2), ("gy", 3)), 1)
        return react_rates(state, neighbours(padded, state), feed_rate, kill_rate, 1.0)

    def coarse_rhs(state):
        padded = padded_2(state, (("gx", 2), ("gy", 3)), 1)
        return react_rates(state, neighbours(padded, state), coarse_feed, coarse_kill, 0.25)

    coarse_start = restrict(initial_state)
    node_vals = jnp.stack([initial_state, initial_state, initial_state])
    slice_start = initial_state
    for sweep_turn in range(TURNS):
        node_vals, integ = fine_sweep(node_vals, slice_start, fine_rhs)
        coarse_old = restrict(node_vals)
        rates_coarse = coarse_rhs(coarse_old)
        coarse_integ = restrict(integ)

        def one_pass(pass_step, chain_state):
            received, coarse_vals, used_init = chain_state
            start_value = jnp.where(is_first, coarse_start, received)
            coarse_vals = coarse_sweep(start_value, rates_coarse, coarse_integ, coarse_rhs)
            received = shifted(coarse_vals[2], "ta", 1)
            return (received, coarse_vals, start_value)

        empty_start = jnp.zeros_like(coarse_start)
        received, coarse_vals, used_init = lax.fori_loop(
            0, pass_count, one_pass, (empty_start, coarse_old, empty_start)
        )
        node_vals = node_vals + prolong(coarse_vals - coarse_old)
        if sweep_turn + 1 < TURNS:
            passed_end = shifted(node_vals[2], "ta", 1)
            slice_start = jnp.where(is_first, initial_state, passed_end)
    return node_vals[2][None]


def solution(mesh):
    placed = (P(None, "gx", "gy"), P("gx", "gy"), P("gx", "gy"))
    return jax.shard_map(
        per_device, mesh=mesh, in_specs=placed, out_specs=P("ta", None, "gx", "gy"), check_vma=False
    )
```

profile of v0, /device:TPU:0, one launch (start us, length us, event | category | flops | bytes accessed | tf_op | source)
XLA Modules:
  0.0 510.3 jit_solution(12967297843783900833)
XLA Ops:
  23.1 5.7 %collective-permute-start.21 = (f32[3,2,34,1]{3,1,2,0:T(2,128)S(1)}, f32[3,2,34,1]{3,1,2,0:T(2,128)S(1)}, u32[]{:S(2)}, u32[]{:S(2)}) collective-permute-start(f32[3,2,34,1]{3,1,2,0:T(2,128)S(1)} %get-tuple-element.476), channel_id=1, source_target_pairs={{0,1},{1,2},{2,3},{4,5},{5,6},{6,7},{8,9},{9,10},{10,11},{12,13},{... | collective-permute-start | bytes 2456 | tf_op jit(solution)/shard_map/ppermute | solution.py:20
  38.1 5.5 %pad_maximum_fusion.57 = (f32[3,2,32,1024]{3,1,2,0:T(2,128)S(1)}, f32[3,2,32,1024]{3,1,2,0:T(2,128)S(1)}, f32[3,2,32,1024]{3,1,2,0:T(2,128)S(1)}, f32[3,2,32,1024]{3,1,2,0:T(2,128)S(1)}) fusion(f32[3,2,34,1]{3,1,2,0:T(2,128)S(1)} %collective-permute-done.20, f32[3,2,1,1024]{3,1,2,0:T(2,128)S(1)} %collective-permute-done.18, ...), kind=kLoop, calls=%fused_computation.148 | loop fusion | flops 1572864 | bytes 3982944 | tf_op jit(solution)/shard_map/concatenate | solution.py:24
  50.6 5.4 %collective-permute-start.25 = (f32[1,2,34,1]{3,1,2,0:T(2,128)S(1)}, f32[1,2,34,1]{3,1,2,0:T(2,128)S(1)}, u32[]{:S(2)}, u32[]{:S(2)}) collective-permute-start(f32[1,2,34,1]{3,1,2,0:T(2,128)S(1)} %get-tuple-element.497), channel_id=1, source_target_pairs={{0,1},{1,2},{2,3},{4,5},{5,6},{6,7},{8,9},{9,10},{10,11},{12,13},{... | collective-permute-start | bytes 824 | tf_op jit(solution)/shard_map/ppermute | solution.py:20
  59.5 7.0 %slice.807 = f32[3,2,16,512]{3,2,1,0:T(8,128)S(1)} slice(f32[3,2,32,1024]{3,2,1,0:T(8,128)S(1)} %pad_maximum_fusion.62), slice={[0:3:1], [0:2:1], [0:32:2], [0:1024:2]} | slice | bytes 393216 | tf_op jit(solution)/shard_map/slice | solution.py:57
  66.6 6.8 %slice.808 = f32[3,2,16,512]{3,2,1,0:T(8,128)S(1)} slice(f32[3,2,32,1024]{3,2,1,0:T(8,128)S(1)} %pad_maximum_fusion.62), slice={[0:3:1], [0:2:1], [1:32:2], [0:1024:2]} | slice | bytes 393216 | tf_op jit(solution)/shard_map/slice | solution.py:58
  73.3 6.8 %slice.809 = f32[3,2,16,512]{3,2,1,0:T(8,128)S(1)} slice(f32[3,2,32,1024]{3,2,1,0:T(8,128)S(1)} %pad_maximum_fusion.62), slice={[0:3:1], [0:2:1], [0:32:2], [1:1024:2]} | slice | bytes 393216 | tf_op jit(solution)/shard_map/slice | solution.py:59
  80.1 6.8 %slice.810 = f32[3,2,16,512]{3,2,1,0:T(8,128)S(1)} slice(f32[3,2,32,1024]{3,2,1,0:T(8,128)S(1)} %pad_maximum_fusion.62), slice={[0:3:1], [0:2:1], [1:32:2], [1:1024:2]} | slice | bytes 393216 | tf_op jit(solution)/shard_map/slice | solution.py:60
  88.3 5.0 slice.835
  111.4 5.4 %collective-permute-start.29 = (f32[3,2,18,1]{3,1,2,0:T(2,128)S(1)}, f32[3,2,18,1]{3,1,2,0:T(2,128)S(1)}, u32[]{:S(2)}, u32[]{:S(2)}) collective-permute-start(f32[3,2,18,1]{3,1,2,0:T(2,128)S(1)} %get-tuple-element.511), channel_id=1, source_target_pairs={{0,1},{1,2},{2,3},{4,5},{5,6},{6,7},{8,9},{9,10},{10,11},{12,13},{... | collective-permute-start | bytes 1304 | tf_op jit(solution)/shard_map/ppermute | solution.py:20
  119.4 141.5 %while.30 = (s32[]{:T(128)}, f32[2,16,512]{2,1,0:T(8,128)S(1)}, f32[3,2,16,512]{3,2,1,0:T(8,128)}, pred[]{:T(512)}, f32[2,16,512]{2,1,0:T(8,128)S(1)}, /*index=5...) while((s32[]{:T(128)}, f32[2,16,512]{2,1,0:T(8,128)S(1)}, ...), condition=%wide.region_1.2_spmd, body=%wide.region_0.1_spmd.sunk | while | flops 885026 | bytes 2690894 | solution.py:128
  124.8 5.1 %collective-permute-start.2 = (f32[1,2,18,1]{3,2,1,0:T(8,128)S(1)}, f32[1,2,18,1]{3,2,1,0:T(8,128)S(1)}, u32[]{:S(2)}, u32[]{:S(2)}) collective-permute-start(f32[1,2,18,1]{3,2,1,0:T(8,128)S(1)} %get-tuple-element.640), channel_id=1, source_target_pairs={{0,1},{1,2},{2,3},{4,5},{5,6},{6,7},{8,9},{9,10},{10,11},{12,13},{... | collective-permute-start | bytes 440 | tf_op jit(solution)/shard_map/while/body/eval_jaxpr/ppermute | solution.py:20
  131.4 5.5 %collective-permute-done.3 = f32[1,2,18,1]{3,2,1,0:T(8,128)S(1)} collective-permute-done((f32[1,2,18,1]{3,2,1,0:T(8,128)S(1)}, f32[1,2,18,1]{3,2,1,0:T(8,128)S(1)}, u32[]{:S(2)}, u32[]{:S(2)}) %collective-permute-start.3) | collective-permute-done | bytes 176 | tf_op jit(solution)/shard_map/while/body/eval_jaxpr/ppermute | solution.py:23
  142.3 4.8 collective-permute-start.6
  299.1 5.0 collective-permute-start.38
  306.8 7.0 %slice.868 = f32[3,2,16,512]{3,2,1,0:T(8,128)S(1)} slice(f32[3,2,32,1024]{3,2,1,0:T(8,128)S(1)} %fusion.48), slice={[0:3:1], [0:2:1], [0:32:2], [0:1024:2]} | slice | bytes 393216 | tf_op jit(solution)/shard_map/slice | solution.py:57
  313.8 6.8 %slice.869 = f32[3,2,16,512]{3,2,1,0:T(8,128)S(1)} slice(f32[3,2,32,1024]{3,2,1,0:T(8,128)S(1)} %fusion.48), slice={[0:3:1], [0:2:1], [1:32:2], [0:1024:2]} | slice | bytes 393216 | tf_op jit(solution)/shard_map/slice | solution.py:58
  320.6 6.8 %slice.870 = f32[3,2,16,512]{3,2,1,0:T(8,128)S(1)} slice(f32[3,2,32,1024]{3,2,1,0:T(8,128)S(1)} %fusion.48), slice={[0:3:1], [0:2:1], [0:32:2], [1:1024:2]} | slice | bytes 393216 | tf_op jit(solution)/shard_map/slice | solution.py:59
  327.3 6.8 %slice.871 = f32[3,2,16,512]{3,2,1,0:T(8,128)S(1)} slice(f32[3,2,32,1024]{3,2,1,0:T(8,128)S(1)} %fusion.48), slice={[0:3:1], [0:2:1], [1:32:2], [1:1024:2]} | slice | bytes 393216 | tf_op jit(solution)/shard_map/slice | solution.py:60
  335.6 4.8 slice.884
  358.4 5.4 %collective-permute-start.42 = (f32[3,2,18,1]{3,1,2,0:T(2,128)S(1)}, f32[3,2,18,1]{3,1,2,0:T(2,128)S(1)}, u32[]{:S(2)}, u32[]{:S(2)}) collective-permute-start(f32[3,2,18,1]{3,1,2,0:T(2,128)S(1)} %get-tuple-element.507), channel_id=1, source_target_pairs={{0,1},{1,2},{2,3},{4,5},{5,6},{6,7},{8,9},{9,10},{10,11},{12,13},{... | collective-permute-start | bytes 1304 | tf_op jit(solution)/shard_map/ppermute | solution.py:20
  366.4 139.4 %while.31 = (s32[]{:T(128)}, f32[2,16,512]{2,1,0:T(8,128)S(1)}, f32[3,2,16,512]{3,2,1,0:T(8,128)}, pred[]{:T(512)}, f32[2,16,512]{2,1,0:T(8,128)S(1)}, /*index=5...) while((s32[]{:T(128)}, f32[2,16,512]{2,1,0:T(8,128)S(1)}, ...), condition=%wide.region_3.4_spmd, body=%wide.region_2.3_spmd.sunk | while | flops 885026 | bytes 2690894 | solution.py:128
  371.2 5.1 %collective-permute-start.11 = (f32[1,2,18,1]{3,2,1,0:T(8,128)S(1)}, f32[1,2,18,1]{3,2,1,0:T(8,128)S(1)}, u32[]{:S(2)}, u32[]{:S(2)}) collective-permute-start(f32[1,2,18,1]{3,2,1,0:T(8,128)S(1)} %get-tuple-element.660), channel_id=1, source_target_pairs={{0,1},{1,2},{2,3},{4,5},{5,6},{6,7},{8,9},{9,10},{10,11},{12,13},{... | collective-permute-start | bytes 440 | tf_op jit(solution)/shard_map/while/body/eval_jaxpr/ppermute | solution.py:20
  377.8 5.5 %collective-permute-done.12 = f32[1,2,18,1]{3,2,1,0:T(8,128)S(1)} collective-permute-done((f32[1,2,18,1]{3,2,1,0:T(8,128)S(1)}, f32[1,2,18,1]{3,2,1,0:T(8,128)S(1)}, u32[]{:S(2)}, u32[]{:S(2)}) %collective-permute-start.12) | collective-permute-done | bytes 176 | tf_op jit(solution)/shard_map/while/body/eval_jaxpr/ppermute | solution.py:23
  388.7 4.8 collective-permute-start.15
  (427 shorter events, 379.3 us)
Async XLA Ops:
  1.0 20.4 %collective-permute-start.18 = (f32[3,2,1,1024]{3,1,2,0:T(2,128)S(1)}, f32[3,2,1,1024]{3,1,2,0:T(2,128)S(1)}, u32[]{:S(2)}, u32[]{:S(2)}) collective-permute-start(f32[3,2,1,1024]{3,1,2,0:T(2,128)S(1)} %concatenate.257), channel_id=1, source_target_pairs={{4,0},{5,1},{6,2},{7,3},{12,8},{13,9},{14,10},{15,11},{20,16},{21,... | collective-permute-start | bytes 73736 | tf_op jit(solution)/shard_map/ppermute | solution.py:23
  2.3 19.1 %collective-permute-start.19 = (f32[3,2,1,1024]{3,1,2,0:T(2,128)S(1)}, f32[3,2,1,1024]{3,1,2,0:T(2,128)S(1)}, u32[]{:S(2)}, u32[]{:S(2)}) collective-permute-start(f32[3,2,1,1024]{3,1,2,0:T(2,128)S(1)} %concatenate.259), channel_id=1, source_target_pairs={{0,4},{1,5},{2,6},{3,7},{8,12},{9,13},{10,14},{11,15},{16,20},{17,... | collective-permute-start | bytes 73736 | tf_op jit(solution)/shard_map/ppermute | solution.py:20
  21.8 16.3 %collective-permute-start.20 = (f32[3,2,34,1]{3,1,2,0:T(2,128)S(1)}, f32[3,2,34,1]{3,1,2,0:T(2,128)S(1)}, u32[]{:S(2)}, u32[]{:S(2)}) collective-permute-start(f32[3,2,34,1]{3,1,2,0:T(2,128)S(1)} %get-tuple-element.475), channel_id=1, source_target_pairs={{1,0},{2,1},{3,2},{5,4},{6,5},{7,6},{9,8},{10,9},{11,10},{13,12},{... | collective-permute-start | bytes 2456 | tf_op jit(solution)/shard_map/ppermute | solution.py:23
  23.1 15.0 %collective-permute-start.21 = (f32[3,2,34,1]{3,1,2,0:T(2,128)S(1)}, f32[3,2,34,1]{3,1,2,0:T(2,128)S(1)}, u32[]{:S(2)}, u32[]{:S(2)}) collective-permute-start(f32[3,2,34,1]{3,1,2,0:T(2,128)S(1)} %get-tuple-element.476), channel_id=1, source_target_pairs={{0,1},{1,2},{2,3},{4,5},{5,6},{6,7},{8,9},{9,10},{10,11},{12,13},{... | collective-permute-start | bytes 2456 | tf_op jit(solution)/shard_map/ppermute | solution.py:20
  49.3 6.8 %collective-permute-start.24 = (f32[1,2,34,1]{3,1,2,0:T(2,128)S(1)}, f32[1,2,34,1]{3,1,2,0:T(2,128)S(1)}, u32[]{:S(2)}, u32[]{:S(2)}) collective-permute-start(f32[1,2,34,1]{3,1,2,0:T(2,128)S(1)} %get-tuple-element.496), channel_id=1, source_target_pairs={{1,0},{2,1},{3,2},{5,4},{6,5},{7,6},{9,8},{10,9},{11,10},{13,12},{... | collective-permute-start | bytes 824 | tf_op jit(solution)/shard_map/ppermute | solution.py:23
  50.6 7.1 %collective-permute-start.25 = (f32[1,2,34,1]{3,1,2,0:T(2,128)S(1)}, f32[1,2,34,1]{3,1,2,0:T(2,128)S(1)}, u32[]{:S(2)}, u32[]{:S(2)}) collective-permute-start(f32[1,2,34,1]{3,1,2,0:T(2,128)S(1)} %get-tuple-element.497), channel_id=1, source_target_pairs={{0,1},{1,2},{2,3},{4,5},{5,6},{6,7},{8,9},{9,10},{10,11},{12,13},{... | collective-permute-start | bytes 824 | tf_op jit(solution)/shard_map/ppermute | solution.py:20
  87.0 21.2 %collective-permute-start.27 = (f32[3,2,1,512]{3,1,2,0:T(2,128)S(1)}, f32[3,2,1,512]{3,1,2,0:T(2,128)S(1)}, u32[]{:S(2)}, u32[]{:S(2)}) collective-permute-start(f32[3,2,1,512]{3,1,2,0:T(2,128)S(1)} %copy.303), channel_id=1, source_target_pairs={{0,4},{1,5},{2,6},{3,7},{8,12},{9,13},{10,14},{11,15},{16,20},{17,... | collective-permute-start | bytes 36872 | tf_op jit(solution)/shard_map/ppermute | solution.py:20
  110.1 7.0 %collective-permute-start.28 = (f32[3,2,18,1]{3,1,2,0:T(2,128)S(1)}, f32[3,2,18,1]{3,1,2,0:T(2,128)S(1)}, u32[]{:S(2)}, u32[]{:S(2)}) collective-permute-start(f32[3,2,18,1]{3,1,2,0:T(2,128)S(1)} %get-tuple-element.510), channel_id=1, source_target_pairs={{1,0},{2,1},{3,2},{5,4},{6,5},{7,6},{9,8},{10,9},{11,10},{13,12},{... | collective-permute-start | bytes 1304 | tf_op jit(solution)/shard_map/ppermute | solution.py:23
  111.4 7.2 %collective-permute-start.29 = (f32[3,2,18,1]{3,1,2,0:T(2,128)S(1)}, f32[3,2,18,1]{3,1,2,0:T(2,128)S(1)}, u32[]{:S(2)}, u32[]{:S(2)}) collective-permute-start(f32[3,2,18,1]{3,1,2,0:T(2,128)S(1)} %get-tuple-element.511), channel_id=1, source_target_pairs={{0,1},{1,2},{2,3},{4,5},{5,6},{6,7},{8,9},{9,10},{10,11},{12,13},{... | collective-permute-start | bytes 1304 | tf_op jit(solution)/shard_map/ppermute | solution.py:20
  124.8 6.6 %collective-permute-start.2 = (f32[1,2,18,1]{3,2,1,0:T(8,128)S(1)}, f32[1,2,18,1]{3,2,1,0:T(8,128)S(1)}, u32[]{:S(2)}, u32[]{:S(2)}) collective-permute-start(f32[1,2,18,1]{3,2,1,0:T(8,128)S(1)} %get-tuple-element.640), channel_id=1, source_target_pairs={{0,1},{1,2},{2,3},{4,5},{5,6},{6,7},{8,9},{9,10},{10,11},{12,13},{... | collective-permute-start | bytes 440 | tf_op jit(solution)/shard_map/while/body/eval_jaxpr/ppermute | solution.py:20
  129.9 7.0 %collective-permute-start.3 = (f32[1,2,18,1]{3,2,1,0:T(8,128)S(1)}, f32[1,2,18,1]{3,2,1,0:T(8,128)S(1)}, u32[]{:S(2)}, u32[]{:S(2)}) collective-permute-start(f32[1,2,18,1]{3,2,1,0:T(8,128)S(1)} %get-tuple-element.641), channel_id=1, source_target_pairs={{1,0},{2,1},{3,2},{5,4},{6,5},{7,6},{9,8},{10,9},{11,10},{13,12},{... | collective-permute-start | bytes 440 | tf_op jit(solution)/shard_map/while/body/eval_jaxpr/ppermute | solution.py:23
  142.3 6.3 %collective-permute-start.6 = (f32[1,2,18,1]{3,2,1,0:T(8,128)S(1)}, f32[1,2,18,1]{3,2,1,0:T(8,128)S(1)}, u32[]{:S(2)}, u32[]{:S(2)}) collective-permute-start(f32[1,2,18,1]{3,2,1,0:T(8,128)S(1)} %get-tuple-element.646), channel_id=1, source_target_pairs={{0,1},{1,2},{2,3},{4,5},{5,6},{6,7},{8,9},{9,10},{10,11},{12,13},{... | collective-permute-start | bytes 440 | tf_op jit(solution)/shard_map/while/body/eval_jaxpr/ppermute | solution.py:20
  269.5 8.1 %collective-permute-start.30 = (f32[2,32,1024]{2,1,0:T(8,128)S(1)}, f32[2,32,1024]{2,1,0:T(8,128)S(1)}, u32[]{:S(2)}, u32[]{:S(2)}) collective-permute-start(f32[2,32,1024]{2,1,0:T(8,128)S(1)} %slice_bitcast_fusion), channel_id=1, source_target_pairs={{0,8},{8,16},{16,24},{1,9},{9,17},{17,25},{2,10},{10,18},{18,26},{... | collective-permute-start | bytes 786440 | tf_op jit(solution)/shard_map/ppermute | solution.py:31
  282.5 6.9 %collective-permute-start.33 = (f32[3,2,34,1]{3,1,2,0:T(2,128)S(1)}, f32[3,2,34,1]{3,1,2,0:T(2,128)S(1)}, u32[]{:S(2)}, u32[]{:S(2)}) collective-permute-start(f32[3,2,34,1]{3,1,2,0:T(2,128)S(1)} %get-tuple-element.471), channel_id=1, source_target_pairs={{1,0},{2,1},{3,2},{5,4},{6,5},{7,6},{9,8},{10,9},{11,10},{13,12},{... | collective-permute-start | bytes 2456 | tf_op jit(solution)/shard_map/ppermute | solution.py:23
  283.8 6.8 %collective-permute-start.34 = (f32[3,2,34,1]{3,1,2,0:T(2,128)S(1)}, f32[3,2,34,1]{3,1,2,0:T(2,128)S(1)}, u32[]{:S(2)}, u32[]{:S(2)}) collective-permute-start(f32[3,2,34,1]{3,1,2,0:T(2,128)S(1)} %get-tuple-element.472), channel_id=1, source_target_pairs={{0,1},{1,2},{2,3},{4,5},{5,6},{6,7},{8,9},{9,10},{10,11},{12,13},{... | collective-permute-start | bytes 2456 | tf_op jit(solution)/shard_map/ppermute | solution.py:20
  297.8 6.3 %collective-permute-start.37 = (f32[1,2,34,1]{3,1,2,0:T(2,128)S(1)}, f32[1,2,34,1]{3,1,2,0:T(2,128)S(1)}, u32[]{:S(2)}, u32[]{:S(2)}) collective-permute-start(f32[1,2,34,1]{3,1,2,0:T(2,128)S(1)} %get-tuple-element.492), channel_id=1, source_target_pairs={{1,0},{2,1},{3,2},{5,4},{6,5},{7,6},{9,8},{10,9},{11,10},{13,12},{... | collective-permute-start | bytes 824 | tf_op jit(solution)/shard_map/ppermute | solution.py:23
  299.1 6.6 %collective-permute-start.38 = (f32[1,2,34,1]{3,1,2,0:T(2,128)S(1)}, f32[1,2,34,1]{3,1,2,0:T(2,128)S(1)}, u32[]{:S(2)}, u32[]{:S(2)}) collective-permute-start(f32[1,2,34,1]{3,1,2,0:T(2,128)S(1)} %get-tuple-element.493), channel_id=1, source_target_pairs={{0,1},{1,2},{2,3},{4,5},{5,6},{6,7},{8,9},{9,10},{10,11},{12,13},{... | collective-permute-start | bytes 824 | tf_op jit(solution)/shard_map/ppermute | solution.py:20
  334.2 21.0 %collective-permute-start.40 = (f32[3,2,1,512]{3,1,2,0:T(2,128)S(1)}, f32[3,2,1,512]{3,1,2,0:T(2,128)S(1)}, u32[]{:S(2)}, u32[]{:S(2)}) collective-permute-start(f32[3,2,1,512]{3,1,2,0:T(2,128)S(1)} %copy.327), channel_id=1, source_target_pairs={{0,4},{1,5},{2,6},{3,7},{8,12},{9,13},{10,14},{11,15},{16,20},{17,... | collective-permute-start | bytes 36872 | tf_op jit(solution)/shard_map/ppermute | solution.py:20
  357.1 7.0 %collective-permute-start.41 = (f32[3,2,18,1]{3,1,2,0:T(2,128)S(1)}, f32[3,2,18,1]{3,1,2,0:T(2,128)S(1)}, u32[]{:S(2)}, u32[]{:S(2)}) collective-permute-start(f32[3,2,18,1]{3,1,2,0:T(2,128)S(1)} %get-tuple-element.506), channel_id=1, source_target_pairs={{1,0},{2,1},{3,2},{5,4},{6,5},{7,6},{9,8},{10,9},{11,10},{13,12},{... | collective-permute-start | bytes 1304 | tf_op jit(solution)/shard_map/ppermute | solution.py:23
  358.4 7.2 %collective-permute-start.42 = (f32[3,2,18,1]{3,1,2,0:T(2,128)S(1)}, f32[3,2,18,1]{3,1,2,0:T(2,128)S(1)}, u32[]{:S(2)}, u32[]{:S(2)}) collective-permute-start(f32[3,2,18,1]{3,1,2,0:T(2,128)S(1)} %get-tuple-element.507), channel_id=1, source_target_pairs={{0,1},{1,2},{2,3},{4,5},{5,6},{6,7},{8,9},{9,10},{10,11},{12,13},{... | collective-permute-start | bytes 1304 | tf_op jit(solution)/shard_map/ppermute | solution.py:20
  371.2 6.6 %collective-permute-start.11 = (f32[1,2,18,1]{3,2,1,0:T(8,128)S(1)}, f32[1,2,18,1]{3,2,1,0:T(8,128)S(1)}, u32[]{:S(2)}, u32[]{:S(2)}) collective-permute-start(f32[1,2,18,1]{3,2,1,0:T(8,128)S(1)} %get-tuple-element.660), channel_id=1, source_target_pairs={{0,1},{1,2},{2,3},{4,5},{5,6},{6,7},{8,9},{9,10},{10,11},{12,13},{... | collective-permute-start | bytes 440 | tf_op jit(solution)/shard_map/while/body/eval_jaxpr/ppermute | solution.py:20
  376.3 7.0 %collective-permute-start.12 = (f32[1,2,18,1]{3,2,1,0:T(8,128)S(1)}, f32[1,2,18,1]{3,2,1,0:T(8,128)S(1)}, u32[]{:S(2)}, u32[]{:S(2)}) collective-permute-start(f32[1,2,18,1]{3,2,1,0:T(8,128)S(1)} %get-tuple-element.661), channel_id=1, source_target_pairs={{1,0},{2,1},{3,2},{5,4},{6,5},{7,6},{9,8},{10,9},{11,10},{13,12},{... | collective-permute-start | bytes 440 | tf_op jit(solution)/shard_map/while/body/eval_jaxpr/ppermute | solution.py:23
  388.7 6.3 %collective-permute-start.15 = (f32[1,2,18,1]{3,2,1,0:T(8,128)S(1)}, f32[1,2,18,1]{3,2,1,0:T(8,128)S(1)}, u32[]{:S(2)}, u32[]{:S(2)}) collective-permute-start(f32[1,2,18,1]{3,2,1,0:T(8,128)S(1)} %get-tuple-element.666), channel_id=1, source_target_pairs={{0,1},{1,2},{2,3},{4,5},{5,6},{6,7},{8,9},{9,10},{10,11},{12,13},{... | collective-permute-start | bytes 440 | tf_op jit(solution)/shard_map/while/body/eval_jaxpr/ppermute | solution.py:20
  399.4 6.3 %collective-permute-start.17 = (f32[2,16,512]{2,1,0:T(8,128)S(1)}, f32[2,16,512]{2,1,0:T(8,128)S(1)}, u32[]{:S(2)}, u32[]{:S(2)}) collective-permute-start(f32[2,16,512]{2,1,0:T(8,128)S(1)} %fusion.171), channel_id=1, source_target_pairs={{0,8},{8,16},{16,24},{1,9},{9,17},{17,25},{2,10},{10,18},{18,26},{... | collective-permute-start | bytes 196616 | tf_op jit(solution)/shard_map/while/body/eval_jaxpr/ppermute | solution.py:31
  (83 other events, 549.0 us)
where the time goes:
time: 520 us; the launch traced here: 510 us
  starting transfers between devices  231 us (44%)
  local copies, waits for them, and re-layouts  127 us (24%)
  waiting for transfers between devices  119 us (23%)
  other arithmetic  29.3 us (6%)
    ppermute x44, starting transfers between devices, padded_2(): lax.ppermute(lax.slice_in_dim(block, block.shape[dim] - width, None, axis...  136 us
    ppermute x44, waiting for transfers between devices, padded_2(): lax.ppermute(lax.slice_in_dim(block, 0, width, axis=dim), axis, backward)  85.6 us
    ppermute x44, starting transfers between devices, padded_2(): lax.ppermute(lax.slice_in_dim(block, 0, width, axis=dim), axis, backward)  56.8 us
    ppermute x9, starting transfers between devices, shifted(): return lax.ppermute(block, axis, route)  37.8 us
    slice x7, local copies, waits for them, and re-layouts, restrict(): values_in[..., 0::2, 0::2] + values_in[..., 1::2, 0::2]  29.2 us
    slice x7, local copies, waits for them, and re-layouts, restrict(): values_in[..., 0::2, 1::2]  28 us
    slice x7, local copies, waits for them, and re-layouts, restrict(): values_in[..., 1::2, 1::2]  28 us
    slice x7, local copies, waits for them, and re-layouts, restrict(): values_in[..., 1::2, 0::2]  28 us
  transfers between devices with their start and end apart: 97, of which 70 were waited for; matrix products, arithmetic and copies ran while one was open for 14% of the time, Pallas kernels for 0%

commit v1 on v0

v1 whole, which is shorter than its diff:
```python
import functools

import jax
import jax.numpy as jnp
from jax import lax
from jax.experimental import pallas as pl
from jax.experimental.pallas import tpu as pltpu
from jax.sharding import PartitionSpec as P

TURNS = 2

DIFF_U = 0.2
DIFF_V = 0.1
HALF_STEP = 0.5
W0 = (5.0 / 24.0, 1.0 / 3.0, -1.0 / 24.0)
W1 = (-1.0 / 24.0, 1.0 / 3.0, 5.0 / 24.0)
GUARD = 8
F32 = jnp.float32
BF16 = jnp.bfloat16
PHASES = ((0, 0), (0, 1), (1, 0), (1, 1))


def round_up(value, step):
    return -(-value // step) * step


def thirds(value):
    high = value.astype(BF16)
    rest = value - high.astype(F32)
    middle = rest.astype(BF16)
    low = (rest - middle.astype(F32)).astype(BF16)
    return high, middle, low


def permuted(value, matrix):
    rows = value.shape[0]
    parts = jnp.concatenate(thirds(value), axis=0)
    moved = jnp.dot(parts, matrix, preferred_element_type=F32)
    return (moved[2 * rows :] + moved[rows : 2 * rows]) + moved[:rows]


def split_matrix():
    source = lax.broadcasted_iota(jnp.int32, (256, 256), 0)
    target = lax.broadcasted_iota(jnp.int32, (256, 256), 1)
    wanted = jnp.where(target < 128, 2 * target, 2 * target - 255)
    return jnp.where(source == wanted, 1.0, 0.0).astype(BF16)


def merge_matrix():
    source = lax.broadcasted_iota(jnp.int32, (256, 256), 0)
    target = lax.broadcasted_iota(jnp.int32, (256, 256), 1)
    wanted = jnp.where(source < 128, 2 * source, 2 * source - 255)
    return jnp.where(target == wanted, 1.0, 0.0).astype(BF16)


C_X0, C_X1, C_X2, C_END, C_C1, C_Y1, C_NEW, C_NEW1, C_D1, C_D2 = (2 * i for i in range(10))
COARSE_STENCIL = 20 + 2
N_C1B, N_K0, N_K1, N_G0, N_RA, N_RB, N_RE, N_J0, N_J1, N_RF2 = (2 * i for i in range(10))
COARSE_PLAIN = 20
N_FEED, N_KILL = 0, 1


def scratch(rows, lanes):
    guarded = rows + 2 * GUARD
    return [
        pltpu.VMEM((4 * 8, guarded, lanes), F32),
        pltpu.VMEM((3 * 8, rows, lanes), F32),
        pltpu.VMEM((8, rows, lanes), F32),
        pltpu.VMEM((8, rows, lanes), F32),
        pltpu.VMEM((COARSE_STENCIL, guarded, lanes), F32),
        pltpu.VMEM((COARSE_PLAIN, rows, lanes), F32),
        pltpu.VMEM((2, rows, lanes), F32),
        pltpu.VMEM((8, rows, lanes), F32),
        pltpu.VMEM((24, rows, lanes), F32),
    ]


class Level:
    def __init__(self, refs, rows, lanes, mask):
        (self.fine, self.lin, self.coef, self.rest, self.cs, self.cp, self.cc, self.mom, self.tl) = refs
        self.rows, self.lanes, self.mask = rows, lanes, mask
        self.chunks = rows // 8

    def each(self, body):
        if self.chunks <= 4:
            for i in range(self.chunks):
                body(8 * i)
        else:
            pl.loop(0, self.chunks)(lambda i: body(pl.multiple_of(8 * i, 8)))

    def left(self, value):
        return pltpu.roll(value, 1, 1)

    def right(self, value):
        return pltpu.roll(value, self.lanes - 1, 1)

    def scaled(self, value, factor):
        if self.mask is None:
            return factor * value
        return (factor * self.mask) * value

    def at(self, ref, plane, row, shift=0):
        if shift and not isinstance(row, int):
            both = ref[plane, pl.ds(GUARD + row + 4 * (shift - 1), 16), :]
            return both[7:15] if shift < 0 else both[1:9]
        return ref[plane, pl.ds(GUARD + row + shift, 8), :]

    def put(self, ref, plane, row, value):
        ref[plane, pl.ds(GUARD + row, 8), :] = value

    def get(self, ref, plane, row):
        return ref[plane, pl.ds(row, 8), :]

    def set(self, ref, plane, row, value):
        ref[plane, pl.ds(row, 8), :] = value

    def clear_guards(self):
        for ref in (self.fine, self.cs):
            zeros = jnp.zeros((GUARD, self.lanes), F32)
            for plane in range(ref.shape[0]):
                ref[plane, pl.ds(0, GUARD), :] = zeros
                ref[plane, pl.ds(GUARD + self.rows, GUARD), :] = zeros

    def fine_rates(self, base, row):
        state = [[self.at(self.fine, base * 8 + s * 4 + p, row) for p in range(4)] for s in range(2)]
        linear, rates = [], []
        for p, (a, b) in enumerate(PHASES):
            laps = []
            for s in range(2):
                across = state[s][2 * a + 1 - b]
                along = state[s][2 * (1 - a) + b]
                moved = self.at(self.fine, base * 8 + s * 4 + 2 * (1 - a) + b, row, 1 if a else -1)
                side = self.right(across) if b else self.left(across)
                laps.append((along + moved) + (across + side) - 4.0 * state[s][p])
            u, v = state[0][p], state[1][p]
            feed = self.get(self.coef, p, row)
            both = self.get(self.coef, 4 + p, row)
            lin_u = self.scaled(laps[0], DIFF_U) + feed
            lin_v = self.scaled(laps[1], DIFF_V)
            linear.append((lin_u, lin_v))
            rates.append(self.reacted(u, v, lin_u, lin_v, feed, both))
        return state, linear, rates

    def reacted(self, u, v, lin_u, lin_v, feed, both):
        return lin_u - u * (feed + v * v), lin_v + v * (u * v - both)

    def neighbours(self, plane, row, value):
        rows = self.at(self.cs, plane, row, -1) + self.at(self.cs, plane, row, 1)
        return rows + (self.left(value) + self.right(value))

    def coarse_rates(self, first, row):
        u = self.at(self.cs, first, row)
        v = self.at(self.cs, first + 1, row)
        feed = self.get(self.cc, 0, row)
        both = self.get(self.cc, 1, row)
        lap_u = self.neighbours(first, row, u) - 4.0 * u
        lap_v = self.neighbours(first + 1, row, v) - 4.0 * v
        lin_u = self.scaled(lap_u, 0.25 * DIFF_U) + feed
        lin_v = self.scaled(lap_v, 0.25 * DIFF_V)
        return (u, v), self.reacted(u, v, lin_u, lin_v, feed, both)

    def moved_rates(self, first, row, which, base):
        a = self.at(self.cs, first, row)
        b = self.at(self.cs, first + 1, row)
        m_vv, m_uv = self.get(self.mom, 4 * which, row), self.get(self.mom, 4 * which + 1, row)
        m_u, m_v = self.get(self.mom, 4 * which + 2, row), self.get(self.mom, 4 * which + 3, row)
        react = a * (m_vv + b * (2.0 * m_v + b)) + b * (2.0 * m_uv + b * m_u)
        lap_a = self.neighbours(first, row, a) - 4.0 * a
        lap_b = self.neighbours(first + 1, row, b) - 4.0 * b
        feed = self.get(self.cc, 0, row)
        both = self.get(self.cc, 1, row)
        rate_u = self.get(self.cp, base, row) + (self.scaled(lap_a, 0.5 * DIFF_U) - (feed * a + react))
        rate_v = self.get(self.cp, base + 1, row) + (self.scaled(lap_b, 0.5 * DIFF_V) + (react - both * b))
        return rate_u, rate_v

    def block_mean(self, values):
        return 0.25 * ((values[0] + values[1]) + (values[2] + values[3]))

    def run(self, own):
        lv = self
        cs, cp = self.cs, self.cp

        def coefficients(row):
            for k in range(2):
                self.set(self.cc, k, row, self.block_mean([self.get(self.coef, 4 * k + p, row) for p in range(4)]))

        def first_sweep(row):
            state, linear, rates = lv.fine_rates(0, row)
            for s in range(2):
                for p in range(4):
                    lv.set(lv.lin, s * 4 + p, row, linear[p][s])
                    lv.put(lv.fine, 8 + s * 4 + p, row, state[s][p] + HALF_STEP * rates[p][s])
                mean = lv.block_mean([r[s] for r in rates])
                start = lv.block_mean(state[s])
                lv.set(cp, N_RA + s, row, mean)
                lv.put(cs, C_X0 + s, row, start)
                lv.put(cs, C_X1 + s, row, start + HALF_STEP * mean)
                lv.put(cs, C_END + s, row, start + mean)
                lv.put(cs, C_D1 + s, row, jnp.zeros_like(mean))
                lv.put(cs, C_D2 + s, row, jnp.zeros_like(mean))

        def moments(which, state, row):
            u, v = state
            lv.set(lv.mom, 4 * which, row, lv.block_mean([v[p] * v[p] for p in range(4)]))
            lv.set(lv.mom, 4 * which + 1, row, lv.block_mean([u[p] * v[p] for p in range(4)]))
            lv.set(lv.mom, 4 * which + 2, row, lv.block_mean(u))
            lv.set(lv.mom, 4 * which + 3, row, lv.block_mean(v))

        def second_sweep(row):
            state, linear, rates = lv.fine_rates(1, row)
            for s in range(2):
                for p in range(4):
                    lv.set(lv.lin, 8 + s * 4 + p, row, linear[p][s])
                    lv.put(lv.fine, 16 + s * 4 + p, row, state[s][p] + HALF_STEP * rates[p][s])
                mean = lv.block_mean([r[s] for r in rates])
                lv.set(cp, N_RB + s, row, mean)
                lv.put(cs, C_X2 + s, row, lv.at(cs, C_X1 + s, row) + HALF_STEP * mean)
            moments(0, state, row)
            _, g0 = lv.coarse_rates(C_X0, row)
            _, g1 = lv.coarse_rates(C_X1, row)
            for s in range(2):
                integral = HALF_STEP * lv.get(cp, N_RA + s, row)
                lv.set(cp, N_K0 + s, row, integral - HALF_STEP * g0[s])
                lv.set(cp, N_K1 + s, row, integral - HALF_STEP * g1[s])

        def third_sweep(row):
            state, linear, rates = lv.fine_rates(2, row)
            for s in range(2):
                for p in range(4):
                    lv.set(lv.lin, 16 + s * 4 + p, row, linear[p][s])
                mean = lv.block_mean([r[s] for r in rates])
                lv.set(cp, N_RE + s, row, mean)
                lv.put(cs, C_D2 + s, row, lv.at(cs, C_END + s, row) - lv.at(cs, C_X2 + s, row))
            moments(1, state, row)

        def first_slice(row):
            last = lv.moved_rates(C_D2, row, 1, N_RE)
            for s in range(2):
                f0, f1 = lv.get(cp, N_RA + s, row), lv.get(cp, N_RB + s, row)
                total = (W0[0] + W1[0]) * f0 + (W0[1] + W1[1]) * f1 + (W0[2] + W1[2]) * last[s]
                lv.put(cs, C_NEW + s, row, lv.at(cs, C_X0 + s, row) + total)
                lv.set(cp, N_RF2 + s, row, last[s])

        def chain(now, before):
            def stage_1(row):
                value, rate = lv.coarse_rates(C_END, row)
                for s in range(2):
                    half = HALF_STEP * rate[s]
                    lv.set(cp, N_G0 + s, row, half)
                    mid = value[s] + half + lv.get(cp, N_K0 + s, row)
                    lv.put(cs, C_C1 + s, row, mid)
                    lv.put(cs, C_D1 + s, row, mid - lv.at(cs, C_X1 + s, row))

            def stage_2(row):
                value, rate = lv.coarse_rates(C_C1, row)
                for s in range(2):
                    end = value[s] + HALF_STEP * rate[s] + lv.get(cp, N_K1 + s, row)
                    lv.set(cp, N_C1B + s, row, lv.at(cs, C_END + s, row))
                    lv.put(cs, C_END + s, row, end)
                    lv.put(cs, now + s, row, end - lv.at(cs, C_X2 + s, row))

            def stage_3(row):
                mid = lv.moved_rates(C_D1, row, 0, N_RB)
                last = lv.moved_rates(now, row, 1, N_RE)
                value, rate = lv.coarse_rates(C_NEW, row)
                for s in range(2):
                    f0 = lv.get(cp, N_RF2 + s, row)
                    j0 = W0[0] * f0 + W0[1] * mid[s] + W0[2] * last[s]
                    j1 = W1[0] * f0 + W1[1] * mid[s] + W1[2] * last[s]
                    lv.set(cp, N_RF2 + s, row, last[s])
                    lv.set(cp, N_J1 + s, row, j1)
                    lv.put(cs, C_Y1 + s, row, lv.get(cp, N_C1B + s, row) + j0)
                    lv.put(cs, C_NEW1 + s, row, value[s] + HALF_STEP * rate[s] - lv.get(cp, N_G0 + s, row) + j0)

            def stage_4(row):
                _, old = lv.coarse_rates(C_Y1, row)
                value, rate = lv.coarse_rates(C_NEW1, row)
                for s in range(2):
                    change = HALF_STEP * (rate[s] - old[s])
                    lv.put(cs, C_NEW + s, row, value[s] + change + lv.get(cp, N_J1 + s, row))

            for stage in (stage_1, stage_2, stage_3, stage_4):
                lv.each(stage)

        def corrections(starts):
            def body(row):
                for k, first in enumerate(starts):
                    for s in range(2):
                        d = lv.at(cs, first + s, row)
                        ring = [lv.at(cs, first + s, row, -1), lv.at(cs, first + s, row, 1), lv.left(d), lv.right(d)]
                        north, south, west, east = (lv.scaled(x - d, (DIFF_U, DIFF_V)[s]) for x in ring)
                        for p, (a, b) in enumerate(PHASES):
                            lv.set(lv.tl, k * 8 + s * 4 + p, row, (south if a else north) + (east if b else west))

            return body

        lv.clear_guards()
        lv.each(coefficients)
        lv.each(first_sweep)
        lv.each(second_sweep)
        lv.each(third_sweep)
        lv.each(first_slice)

        def one_slice(n, carry):
            even = lax.rem(n, 2) == 0
            pl.when(even)(lambda: chain(C_D2, C_D2 + 2))
            pl.when(jnp.logical_not(even))(lambda: chain(C_D2 + 2, C_D2))
            return carry

        lax.fori_loop(1, own + 1, one_slice, 0)

        first = own == 0
        even = lax.rem(own, 2) == 0
        now = jnp.where(even, C_D2, C_D2 + 2)
        before = jnp.where(first, C_D1, jnp.where(even, C_D2 + 2, C_D2))
        origin = jnp.where(first, 0, 2)
        lv.each(corrections((before, C_D1, now)))

        def own_nodes(row):
            for p in range(4):
                for t in range(0, lv.lanes, 128):
                    lane = pl.ds(t, 128)
                    high = pl.ds(GUARD + row, 8)
                    low = pl.ds(row, 8)
                    feed, both = lv.coef[p, low, lane], lv.coef[4 + p, low, lane]
                    rates, start = [], None
                    for k, (base, d) in enumerate(((origin, before), (1, C_D1), (2, now))):
                        pair = [lv.fine[base * 8 + s * 4 + p, high, lane] + cs[d + s, high, lane] for s in range(2)]
                        lin = [lv.lin[base * 8 + s * 4 + p, low, lane] + lv.tl[k * 8 + s * 4 + p, low, lane] for s in range(2)]
                        rates.append(lv.reacted(pair[0], pair[1], lin[0], lin[1], feed, both))
                        start = pair if k == 0 else start
                    for s in range(2):
                        f0, f1, f2 = (r[s] for r in rates)
                        second = start[s] + (W0[0] * f0 + W0[1] * f1 + W0[2] * f2)
                        lv.fine[24 + s * 4 + p, high, lane] = second
                        lv.rest[s * 4 + p, low, lane] = second + (W1[0] * f0 + (W1[1] - HALF_STEP) * f1 + W1[2] * f2)

        lv.each(own_nodes)

        def last_node(row):
            _, _, rates = lv.fine_rates(3, row)
            for s in range(2):
                ends = [lv.get(lv.rest, s * 4 + p, row) + HALF_STEP * rates[p][s] for p in range(4)]
                fix = lv.at(cs, C_NEW + s, row) - lv.block_mean(ends)
                for p in range(4):
                    lv.set(lv.rest, s * 4 + p, row, ends[p] + fix)

        lv.each(last_node)


def load_planes(level, sources, blocks, columns):
    matrix = split_matrix()
    for block in range(blocks):
        lane = pl.ds(128 * block, 128)
        for read, first in sources:
            values = [read(plane, block) for plane in range(4)]
            rows = values[0].shape[0]
            moved = permuted(jnp.concatenate(values, axis=0), matrix)
            columns[0], columns[1] = moved[:, :128], moved[:, 128:]
            half = rows // 2
            for plane in range(4):
                for a in range(2):
                    for b in range(2):
                        value = columns[b, pl.ds(plane * rows + a, half, stride=2), :]
                        p = 2 * a + b
                        if plane < 2:
                            level.fine[plane * 4 + p, pl.ds(GUARD + first, half), lane] = value
                        elif plane == 2:
                            level.coef[p, pl.ds(first, half), lane] = value
                        else:
                            level.coef[4 + p, pl.ds(first, half), lane] = value + level.coef[p, pl.ds(first, half), lane]


def merged(level, first, rows, block, matrix, columns):
    half = rows // 2
    groups = []
    lane = pl.ds(128 * block, 128)
    for s in range(2):
        for a in range(2):
            pair = [level.rest[s * 4 + 2 * a + b, pl.ds(first, half), lane] for b in range(2)]
            groups.append(jnp.concatenate(pair, axis=1))
    natural = permuted(jnp.concatenate(groups, axis=0), matrix)
    for s in range(2):
        for a in range(2):
            at = (2 * s + a) * half
            for b in range(2):
                columns[b, pl.ds(s * rows + a, half, stride=2), :] = natural[at : at + half, 128 * b : 128 * b + 128]
    return [[columns[b, pl.ds(s * rows, rows), :] for b in range(2)] for s in range(2)]


def own_first(rows):
    return pl.multiple_of(lax.axis_index("gx") * (rows // 2), rows // 2)


def source_list(refs, rows, parts):
    half = rows // 2
    if parts == 2:
        mine = own_first(rows)
        count = len(refs) // 2
        return [(refs[:count], mine), (refs[count:], pl.multiple_of(half - mine, half))]
    return [(tuple(ref.at[g] for ref in refs), g * half) for g in range(parts)]


def interior_kernel(parts, rows, columns_in, *refs):
    count = 6 if parts == 2 else 3
    ins, out, work = refs[:count], refs[count], refs[count + 1 :]
    level = Level(work[:-1], parts * rows // 2, columns_in // 2, None)

    def reader(three):
        state, feed, kill = three

        def read(plane, block):
            lane = pl.ds(256 * block, 256)
            return state[plane, :, lane] if plane < 2 else (feed, kill)[plane - 2][:, lane]

        return read

    sources = [(reader(three), first) for three, first in source_list(ins, rows, parts)]
    load_planes(level, sources, columns_in // 256, work[-1])
    level.run(lax.axis_index("ta"))
    matrix = merge_matrix()
    for block in range(columns_in // 256):
        natural = merged(level, own_first(rows), rows, block, matrix, work[-1])
        for s in range(2):
            for b in range(2):
                out[s, :, pl.ds(256 * block + 128 * b, 128)] = natural[s][b]


def border_kernel(parts, rows, halo, depth, width, *refs):
    count = 16 if parts == 2 else 8
    ins, done, out, work = refs[:count], refs[count], refs[count + 1], refs[count + 2 :]
    own_cols = width // 2 - halo
    lanes = width // 2
    index, size = lax.axis_index("gy"), lax.axis_size("gy")
    even = lax.rem(index, 2) == 0
    at = lax.broadcasted_iota(jnp.int32, (1, lanes), 1)
    outside = ((at < halo // 2) & (index == 0)) | ((at >= lanes - halo // 2) & (index == size - 1))
    level = Level(work[:-1], parts * rows // 2, lanes, jnp.where(outside, 0.0, 1.0))

    def reader(eight):
        state_l, feed_l, kill_l, state_r, feed_r, kill_r, from_a, from_b = eight

        def read(plane, block):
            pick = (lambda s, f, k: s[plane] if plane < 2 else (f, k)[plane - 2][...])
            low = jnp.where(even, from_b[:, halo * plane : halo * plane + halo], from_a[:, halo * plane : halo * plane + halo])
            high = jnp.where(even, from_a[:, halo * plane : halo * plane + halo], from_b[:, halo * plane : halo * plane + halo])
            left = pick(state_l, feed_l, kill_l)[:, :own_cols]
            right = pick(state_r, feed_r, kill_r)
            right = right[:, right.shape[1] - own_cols :]
            whole = jnp.concatenate([low, left, right, high], axis=1)
            return whole[:, 256 * block : 256 * block + 256]

        return read

    sources = [(reader(eight), first) for eight, first in source_list(ins, rows, parts)]
    load_planes(level, sources, width // 256, work[-1])
    level.run(lax.axis_index("ta"))
    matrix = merge_matrix()
    total = out.shape[-1]
    patch = 2 * depth
    out[0] = done[...]
    pieces = [merged(level, own_first(rows), rows, block, matrix, work[-1]) for block in range(width // 256)]
    tile = round_up(patch, 128)
    for s in range(2):
        whole = jnp.concatenate([part for piece in pieces for part in piece[s]], axis=1)
        low = whole[:, halo : halo + patch]
        high = whole[:, width - halo - patch : width - halo]
        old = out[0, s, :, pl.ds(0, tile)]
        out[0, s, :, pl.ds(0, tile)] = jnp.concatenate([low, old[:, patch:]], axis=1)
        old = out[0, s, :, pl.ds(total - tile, tile)]
        out[0, s, :, pl.ds(total - tile, tile)] = jnp.concatenate([old[:, : tile - patch], high], axis=1)


def pack_kernel(halo, state, feed, kill, to_a, to_b):
    planes = [state[0], state[1], feed[...], kill[...]]
    total = feed.shape[1]
    left = jnp.concatenate([x[:, :halo] for x in planes], axis=1)
    right = jnp.concatenate([x[:, total - halo :] for x in planes], axis=1)
    even = lax.rem(lax.axis_index("gy"), 2) == 0
    to_a[...] = jnp.where(even, right, left)
    to_b[...] = jnp.where(even, left, right)


def both_ways(pairs):
    return [pair for low, high in pairs for pair in ((low, high), (high, low))]


VMEM = pl.BlockSpec(memory_space=pltpu.VMEM)
PARAMS = pltpu.CompilerParams(vmem_limit_bytes=56 * 2**20)


def per_device(initial_state, feed_rate, kill_rate):
    slices, parts, blocks = (lax.axis_size(axis) for axis in ("ta", "gx", "gy"))
    _, rows, columns = initial_state.shape
    depth = 2 * (2 * slices + 2)
    halo = round_up(depth, 32)
    width = round_up(2 * halo + 4 * depth, 256)
    edge = round_up(width // 2 - halo, 128)

    def across(value):
        if parts == 2:
            return [value, lax.ppermute(value, "gx", [(0, 1), (1, 0)])]
        return [lax.all_gather(value, "gx")]

    def joined(groups):
        return [value for part in zip(*groups) for value in part]

    to_a, to_b = pl.pallas_call(
        functools.partial(pack_kernel, halo),
        out_shape=[jax.ShapeDtypeStruct((rows, 4 * halo), F32)] * 2,
        in_specs=[VMEM] * 3,
        out_specs=[VMEM] * 2,
        name="pack",
    )(initial_state, feed_rate, kill_rate)
    fields = [across(value) for value in (initial_state, feed_rate, kill_rate)]
    from_b = lax.ppermute(to_b, "gy", both_ways([(i, i + 1) for i in range(1, blocks - 1, 2)]))
    from_a = lax.ppermute(to_a, "gy", both_ways([(i, i + 1) for i in range(0, blocks - 1, 2)]))
    whole_rows = parts * rows // 2
    inner = pl.pallas_call(
        functools.partial(interior_kernel, parts, rows, columns),
        out_shape=jax.ShapeDtypeStruct((2, rows, columns), F32),
        in_specs=[VMEM] * (3 * len(fields[0])),
        out_specs=VMEM,
        scratch_shapes=scratch(whole_rows, columns // 2) + [pltpu.VMEM((2, 4 * rows, 128), F32)],
        compiler_params=PARAMS,
        name="interior",
    )(*joined(fields))
    strips = [across(value) for value in (from_a, from_b)]
    edges = [[value[..., :edge] for value in field] for field in fields]
    edges += [[value[..., columns - edge :] for value in field] for field in fields]
    return pl.pallas_call(
        functools.partial(border_kernel, parts, rows, halo, depth, width),
        out_shape=jax.ShapeDtypeStruct((1, 2, rows, columns), F32),
        in_specs=[VMEM] * (8 * len(fields[0]) + 1),
        out_specs=VMEM,
        scratch_shapes=scratch(whole_rows, width // 2) + [pltpu.VMEM((2, 4 * rows, 128), F32)],
        compiler_params=PARAMS,
        name="border",
    )(*joined(edges + strips), inner)


def solution(mesh):
    placed = (P(None, "gx", "gy"), P("gx", "gy"), P("gx", "gy"))
    return jax.shard_map(
        per_device, mesh=mesh, in_specs=placed, out_specs=P("ta", None, "gx", "gy"), check_vma=False
    )
```

time: 520 us -> 27.6 us (0.05)
  the two profiles are of different devices: /device:TPU:0 before, /device:TPU:29 now
where the time goes in v1:
time: 27.6 us; the launch traced here: 27.3 us
  Pallas kernels  15.2 us (55%)
  starting transfers between devices  6.54 us (24%)
  local copies, waits for them, and re-layouts  5.44 us (20%)
    pallas_call x1, Pallas kernels, per_device(): pl.pallas_call(functools.partial(interior_kernel, parts, rows, columns),...  9.25 us
    slice x5, local copies, waits for them, and re-layouts, per_device(): value[..., columns - edge:]  4.78 us
    pallas_call x1, Pallas kernels, per_device(): pl.pallas_call(functools.partial(border_kernel, parts, rows, halo, depth,...  4.25 us
    ppermute x5, starting transfers between devices, across(): return [value, lax.ppermute(value, 'gx', [(0, 1), (1, 0)])]  3.23 us
    ppermute x1, starting transfers between devices, per_device(): lax.ppermute(to_b, 'gy', both_ways([(i, i + 1) for i in range(1, blocks -...  2.09 us
    pallas_call x1, Pallas kernels, per_device(): pl.pallas_call(functools.partial(pack_kernel, halo), out_shape=[jax.Shape...  1.75 us
    ppermute x1, starting transfers between devices, per_device(): lax.ppermute(to_a, 'gy', both_ways([(i, i + 1) for i in range(0, blocks -...  1.21 us
    unnamed x14, local copies, waits for them, and re-layouts  0.66 us
  transfers between devices with their start and end apart: 7, of which 1 were waited for; matrix products, arithmetic and copies ran while one was open for 17% of the time, Pallas kernels for 40%

profile of v1, /device:TPU:29, one launch (start us, length us, event | category | flops | bytes accessed | tf_op | source)
XLA Modules:
  0.0 27.3 jit_solution(18005563293228229005)
XLA Ops:
  0.0 0.7 %collective-permute-start.2 = (f32[2,32,1024]{2,1,0:T(8,128)}, f32[2,32,1024]{2,1,0:T(8,128)S(1)}, u32[]{:S(2)}, u32[]{:S(2)}) collective-permute-start(f32[2,32,1024]{2,1,0:T(8,128)} %refs_0_.1), channel_id=1, source_target_pairs={{0,4},{4,0},{1,5},{5,1},{2,6},{6,2},{3,7},{7,3},{8,12},{12,8},{9,1... | collective-permute-start | bytes 786440 | tf_op jit(solution)/shard_map/ppermute | solution.py:502
  0.7 0.5 %collective-permute-start.4 = (f32[32,1024]{1,0:T(8,128)}, f32[32,1024]{1,0:T(8,128)S(1)}, u32[]{:S(2)}, u32[]{:S(2)}) collective-permute-start(f32[32,1024]{1,0:T(8,128)} %refs_2_.1), channel_id=1, source_target_pairs={{0,4},{4,0},{1,5},{5,1},{2,6},{6,2},{3,7},{7,3},{8,12},{12,8},{9,1... | collective-permute-start | bytes 393224 | tf_op jit(solution)/shard_map/ppermute | solution.py:502
  1.2 1.7 %pack.1 = (f32[32,128]{1,0:T(8,128)}, f32[32,128]{1,0:T(8,128)}) custom-call(f32[2,32,1024]{2,1,0:T(8,128)} %refs_0_.1, f32[32,1024]{1,0:T(8,128)} %refs_1_.1, f32[32,1024]{1,0:T(8,128)} %refs_2_.1), custom_call_target="tpu_custom_call" | custom-call | tf_op jit(solution)/shard_map/pack/pallas_call | solution.py:508
  2.9 1.2 %collective-permute-start = (f32[32,128]{1,0:T(8,128)}, f32[32,128]{1,0:T(8,128)S(1)}, u32[]{:S(2)}, u32[]{:S(2)}) collective-permute-start(f32[32,128]{1,0:T(8,128)} %get-tuple-element.7), channel_id=1, source_target_pairs={{0,1},{1,0},{2,3},{3,2},{4,5},{5,4},{6,7},{7,6},{8,9},{9,8},{10,11... | collective-permute-start | bytes 49160 | tf_op jit(solution)/shard_map/ppermute | solution.py:517
  4.1 2.1 %collective-permute-start.1 = (f32[32,128]{1,0:T(8,128)}, f32[32,128]{1,0:T(8,128)S(1)}, u32[]{:S(2)}, u32[]{:S(2)}) collective-permute-start(f32[32,128]{1,0:T(8,128)} %get-tuple-element.8), channel_id=1, source_target_pairs={{1,2},{2,1},{5,6},{6,5},{9,10},{10,9},{13,14},{14,13},{17,18},{18,... | collective-permute-start | bytes 49160 | tf_op jit(solution)/shard_map/ppermute | solution.py:516
  6.2 1.4 %fusion.4 = (f32[32,128]{1,0:T(8,128)}, f32[32,128]{1,0:T(8,128)}, f32[32,128]{1,0:T(8,128)}, f32[32,128]{1,0:T(8,128)}) fusion(f32[32,1024]{1,0:T(8,128)} %refs_2_.1, f32[32,1024]{1,0:T(8,128)} %refs_1_.1), kind=kLoop, calls=%fused_computation.4 | loop fusion | bytes 131072 | tf_op jit(solution)/shard_map/slice | solution.py:530
  7.7 1.4 %fusion.1 = (f32[2,32,128]{2,1,0:T(8,128)}, f32[2,32,128]{2,1,0:T(8,128)}) fusion(f32[2,32,1024]{2,1,0:T(8,128)} %refs_0_.1), kind=kLoop, calls=%fused_computation.1 | loop fusion | bytes 131072 | tf_op jit(solution)/shard_map/slice | solution.py:530
  9.1 0.0 collective-permute-done.refs_6_
  9.1 0.6 %collective-permute-start.5 = (f32[32,128]{1,0:T(8,128)S(1)}, f32[32,128]{1,0:T(8,128)S(1)}, u32[]{:S(2)}, u32[]{:S(2)}) collective-permute-start(f32[32,128]{1,0:T(8,128)S(1)} %collective-permute-done.refs_6_), channel_id=1, source_target_pairs={{0,4},{4,0},{1,5},{5,1},{2,6},{6,2},{3,7},{7,3},{8,12},{12,8},{9,1... | collective-permute-start | bytes 49160 | tf_op jit(solution)/shard_map/ppermute | solution.py:502
  9.7 0.1 collective-permute-done.1.refs_7_
  9.7 1.4 %collective-permute-start.6 = (f32[32,128]{1,0:T(8,128)S(1)}, f32[32,128]{1,0:T(8,128)S(1)}, u32[]{:S(2)}, u32[]{:S(2)}) collective-permute-start(f32[32,128]{1,0:T(8,128)S(1)} %collective-permute-done.1.refs_7_), channel_id=1, source_target_pairs={{0,4},{4,0},{1,5},{5,1},{2,6},{6,2},{3,7},{7,3},{8,12},{12,8},{9,1... | collective-permute-start | bytes 49160 | tf_op jit(solution)/shard_map/ppermute | solution.py:502
  11.2 0.0 collective-permute-done.4.refs_5_
  11.2 0.7 %fusion.2 = (f32[32,128]{1,0:T(8,128)}, f32[32,128]{1,0:T(8,128)}) fusion(f32[32,1024]{1,0:T(8,128)S(1)} %collective-permute-done.4.refs_5_), kind=kLoop, calls=%fused_computation.2 | loop fusion | bytes 65536 | tf_op jit(solution)/shard_map/slice | solution.py:530
  11.8 0.0 collective-permute-done.3.refs_4_
  11.8 0.7 %fusion.3 = (f32[32,128]{1,0:T(8,128)}, f32[32,128]{1,0:T(8,128)}) fusion(f32[32,1024]{1,0:T(8,128)S(1)} %collective-permute-done.3.refs_4_), kind=kLoop, calls=%fused_computation.3 | loop fusion | bytes 65536 | tf_op jit(solution)/shard_map/slice | solution.py:530
  12.5 0.0 collective-permute-done.2.refs_3_
  12.5 0.7 %fusion = (f32[2,32,128]{2,1,0:T(8,128)}, f32[2,32,128]{2,1,0:T(8,128)}) fusion(f32[2,32,1024]{2,1,0:T(8,128)S(1)} %collective-permute-done.2.refs_3_), kind=kLoop, calls=%fused_computation | loop fusion | bytes 131072 | tf_op jit(solution)/shard_map/slice | solution.py:530
  13.2 0.1 copy-done
  13.2 9.3 %interior.1.refs_16_ = f32[2,32,1024]{2,1,0:T(8,128)} custom-call(f32[2,32,1024]{2,1,0:T(8,128)} %refs_0_.1, f32[32,1024]{1,0:T(8,128)} %refs_1_.1, f32[32,1024]{1,0:T(8,128)} %refs_2_.1, f32[2,32,1024]{2,1,0:T(8,128)} %copy-done, f32[32,1024]{1,0:T(8,128)} %copy-done.1, f32[32,1024]{1,0:T(8,128)} %copy-done.2), custom_call_target="tpu_custom_call" | custom-call | tf_op jit(solution)/shard_map/interior/pallas_call | solution.py:519
  22.5 0.0 collective-permute-done.5.refs_14_
  22.5 0.0 collective-permute-done.6.refs_15_
  22.5 0.6 %copy-done.5 = f32[32,128]{1,0:T(8,128)} copy-done((f32[32,128]{1,0:T(8,128)}, f32[32,128]{1,0:T(8,128)S(1)}, u32[]{:S(2)}) %copy-start.5) | copy-done | bytes 16408
  23.1 0.0 copy-done.6
  23.1 4.2 %border.1 = f32[1,2,32,1024]{3,2,1,0:T(8,128)} custom-call(f32[2,32,128]{2,1,0:T(8,128)} %get-tuple-element.12.refs_0_, f32[32,128]{1,0:T(8,128)} %get-tuple-element.21.refs_1_, f32[32,128]{1,0:T(8,128)} %get-tuple-element.18.refs_2_, f32[2,32,128]{2,1,0:T(8,128)} %get-tuple-element.11.refs_3_, f32[32,128]{1,0:T(8,128)} %get-tuple-element.22.refs_4_, ...), custom_call_target="tpu_custom_call" | custom-call | tf_op jit(solution)/shard_map/border/pallas_call | solution.py:531
  (12 shorter events, 0.0 us)
Async XLA Ops:
  0.0 12.5 %collective-permute-start.2 = (f32[2,32,1024]{2,1,0:T(8,128)}, f32[2,32,1024]{2,1,0:T(8,128)S(1)}, u32[]{:S(2)}, u32[]{:S(2)}) collective-permute-start(f32[2,32,1024]{2,1,0:T(8,128)} %refs_0_.1), channel_id=1, source_target_pairs={{0,4},{4,0},{1,5},{5,1},{2,6},{6,2},{3,7},{7,3},{8,12},{12,8},{9,1... | collective-permute-start | bytes 786440 | tf_op jit(solution)/shard_map/ppermute | solution.py:502
  0.7 11.2 %collective-permute-start.3 = (f32[32,1024]{1,0:T(8,128)}, f32[32,1024]{1,0:T(8,128)S(1)}, u32[]{:S(2)}, u32[]{:S(2)}) collective-permute-start(f32[32,1024]{1,0:T(8,128)} %refs_1_.1), channel_id=1, source_target_pairs={{0,4},{4,0},{1,5},{5,1},{2,6},{6,2},{3,7},{7,3},{8,12},{12,8},{9,1... | collective-permute-start | bytes 393224 | tf_op jit(solution)/shard_map/ppermute | solution.py:502
  0.7 10.5 %collective-permute-start.4 = (f32[32,1024]{1,0:T(8,128)}, f32[32,1024]{1,0:T(8,128)S(1)}, u32[]{:S(2)}, u32[]{:S(2)}) collective-permute-start(f32[32,1024]{1,0:T(8,128)} %refs_2_.1), channel_id=1, source_target_pairs={{0,4},{4,0},{1,5},{5,1},{2,6},{6,2},{3,7},{7,3},{8,12},{12,8},{9,1... | collective-permute-start | bytes 393224 | tf_op jit(solution)/shard_map/ppermute | solution.py:502
  2.9 6.1 %collective-permute-start = (f32[32,128]{1,0:T(8,128)}, f32[32,128]{1,0:T(8,128)S(1)}, u32[]{:S(2)}, u32[]{:S(2)}) collective-permute-start(f32[32,128]{1,0:T(8,128)} %get-tuple-element.7), channel_id=1, source_target_pairs={{0,1},{1,0},{2,3},{3,2},{4,5},{5,4},{6,7},{7,6},{8,9},{9,8},{10,11... | collective-permute-start | bytes 49160 | tf_op jit(solution)/shard_map/ppermute | solution.py:517
  4.1 5.6 %collective-permute-start.1 = (f32[32,128]{1,0:T(8,128)}, f32[32,128]{1,0:T(8,128)S(1)}, u32[]{:S(2)}, u32[]{:S(2)}) collective-permute-start(f32[32,128]{1,0:T(8,128)} %get-tuple-element.8), channel_id=1, source_target_pairs={{1,2},{2,1},{5,6},{6,5},{9,10},{10,9},{13,14},{14,13},{17,18},{18,... | collective-permute-start | bytes 49160 | tf_op jit(solution)/shard_map/ppermute | solution.py:516
  9.1 2.8 %copy-start.3 = (f32[32,128]{1,0:T(8,128)}, f32[32,128]{1,0:T(8,128)S(1)}, u32[]{:S(2)}) copy-start(f32[32,128]{1,0:T(8,128)S(1)} %collective-permute-done.refs_6_) | copy-start | bytes 49156
  9.1 13.4 %collective-permute-start.5 = (f32[32,128]{1,0:T(8,128)S(1)}, f32[32,128]{1,0:T(8,128)S(1)}, u32[]{:S(2)}, u32[]{:S(2)}) collective-permute-start(f32[32,128]{1,0:T(8,128)S(1)} %collective-permute-done.refs_6_), channel_id=1, source_target_pairs={{0,4},{4,0},{1,5},{5,1},{2,6},{6,2},{3,7},{7,3},{8,12},{12,8},{9,1... | collective-permute-start | bytes 49160 | tf_op jit(solution)/shard_map/ppermute | solution.py:502
  9.7 2.1 %copy-start.4 = (f32[32,128]{1,0:T(8,128)}, f32[32,128]{1,0:T(8,128)S(1)}, u32[]{:S(2)}) copy-start(f32[32,128]{1,0:T(8,128)S(1)} %collective-permute-done.1.refs_7_) | copy-start | bytes 49156
  9.7 12.8 %collective-permute-start.6 = (f32[32,128]{1,0:T(8,128)S(1)}, f32[32,128]{1,0:T(8,128)S(1)}, u32[]{:S(2)}, u32[]{:S(2)}) collective-permute-start(f32[32,128]{1,0:T(8,128)S(1)} %collective-permute-done.1.refs_7_), channel_id=1, source_target_pairs={{0,4},{4,0},{1,5},{5,1},{2,6},{6,2},{3,7},{7,3},{8,12},{12,8},{9,1... | collective-permute-start | bytes 49160 | tf_op jit(solution)/shard_map/ppermute | solution.py:502
  11.2 2.0 %copy-start.2 = (f32[32,1024]{1,0:T(8,128)}, f32[32,1024]{1,0:T(8,128)S(1)}, u32[]{:S(2)}) copy-start(f32[32,1024]{1,0:T(8,128)S(1)} %collective-permute-done.4.refs_5_) | copy-start | bytes 393220
  11.8 1.3 %copy-start.1 = (f32[32,1024]{1,0:T(8,128)}, f32[32,1024]{1,0:T(8,128)S(1)}, u32[]{:S(2)}) copy-start(f32[32,1024]{1,0:T(8,128)S(1)} %collective-permute-done.3.refs_4_) | copy-start | bytes 393220
  12.5 0.7 %copy-start = (f32[2,32,1024]{2,1,0:T(8,128)}, f32[2,32,1024]{2,1,0:T(8,128)S(1)}, u32[]{:S(2)}) copy-start(f32[2,32,1024]{2,1,0:T(8,128)S(1)} %collective-permute-done.2.refs_3_) | copy-start | bytes 786436
  22.5 0.6 %copy-start.5 = (f32[32,128]{1,0:T(8,128)}, f32[32,128]{1,0:T(8,128)S(1)}, u32[]{:S(2)}) copy-start(f32[32,128]{1,0:T(8,128)S(1)} %collective-permute-done.5.refs_14_) | copy-start | bytes 49156
  22.5 0.6 %copy-start.6 = (f32[32,128]{1,0:T(8,128)}, f32[32,128]{1,0:T(8,128)S(1)}, u32[]{:S(2)}) copy-start(f32[32,128]{1,0:T(8,128)S(1)} %collective-permute-done.6.refs_15_) | copy-start | bytes 49156

commit v2 on v1

v2 whole, which is shorter than its diff:
```python
import functools
import math

import jax
import jax.numpy as jnp
from jax import lax
from jax.experimental import pallas as pl
from jax.experimental.pallas import tpu as pltpu
from jax.sharding import PartitionSpec as P

TURNS = 2

DIFF_U = 0.2
DIFF_V = 0.1
HALF_STEP = 0.5
W0 = (5.0 / 24.0, 1.0 / 3.0, -1.0 / 24.0)
W1 = (-1.0 / 24.0, 1.0 / 3.0, 5.0 / 24.0)
GUARD = 8
F32 = jnp.float32
BF16 = jnp.bfloat16
PHASES = ((0, 0), (0, 1), (1, 0), (1, 1))


def round_up(value, step):
    return -(-value // step) * step


def thirds(value):
    high = value.astype(BF16)
    rest = value - high.astype(F32)
    middle = rest.astype(BF16)
    low = (rest - middle.astype(F32)).astype(BF16)
    return high, middle, low


def permuted(value, matrix):
    rows = value.shape[0]
    parts = jnp.concatenate(thirds(value), axis=0)
    moved = jnp.dot(parts, matrix, preferred_element_type=F32)
    return (moved[2 * rows :] + moved[rows : 2 * rows]) + moved[:rows]


def group_matrix(tiles, inverse):
    group = 128 // tiles
    natural = lax.broadcasted_iota(jnp.int32, (256, 256), 1 if inverse else 0)
    grouped = lax.broadcasted_iota(jnp.int32, (256, 256), 0 if inverse else 1)
    wanted = 2 * tiles * (grouped % group) + 2 * ((grouped % 128) // group) + grouped // 128
    return jnp.where(natural == wanted, 1.0, 0.0).astype(BF16)


def exchanged(tiles, slot):
    count = len(tiles)
    if count == 1:
        return tiles
    group = 128 // count
    turned = [pltpu.roll(tile, k * group, 1) if k else tile for k, tile in enumerate(tiles)]
    results = []
    for q in range(count):
        value = turned[(count - q) % count]
        for at in range(1, count):
            value = jnp.where(slot == at, turned[(at - q) % count], value)
        results.append(pltpu.roll(value, (count - q) * group, 1) if q else value)
    return results


def slots(tiles):
    return lax.broadcasted_iota(jnp.int32, (1, 128), 1) // (128 // tiles)


C_X0, C_X1, C_X2, C_END, C_C1, C_NEW, C_E1, C_D1, C_D2 = (2 * i for i in range(9))
COARSE_STENCIL = 20
N_LAST, N_K0, N_K1, N_G0, N_RA, N_RB, N_RE, N_F1, N_RF2 = (2 * i for i in range(9))
COARSE_PLAIN = 18


def scratch(rows, lanes):
    guarded = rows + 2 * GUARD
    return [
        pltpu.VMEM((4 * 8, guarded, lanes), F32),
        pltpu.VMEM((3 * 8, rows, lanes), F32),
        pltpu.VMEM((8, rows, lanes), F32),
        pltpu.VMEM((8, rows, lanes), F32),
        pltpu.VMEM((COARSE_STENCIL, guarded, lanes), F32),
        pltpu.VMEM((COARSE_PLAIN, rows, lanes), F32),
        pltpu.VMEM((2, rows, lanes), F32),
        pltpu.VMEM((8, rows, lanes), F32),
        pltpu.VMEM((24, rows, lanes), F32),
    ]


class Level:
    def __init__(self, refs, rows, lanes, mask):
        (self.fine, self.lin, self.coef, self.rest, self.cs, self.cp, self.cc, self.mom, self.tl) = refs
        self.rows, self.lanes, self.mask = rows, lanes, mask
        self.chunks = rows // 8

    def each(self, body):
        if self.chunks <= 4:
            for i in range(self.chunks):
                body(8 * i)
        else:
            pl.loop(0, self.chunks)(lambda i: body(pl.multiple_of(8 * i, 8)))

    def left(self, value):
        if self.lanes == 128:
            return pltpu.roll(value, 1, 1)
        return jnp.concatenate([pltpu.roll(value[:, -128:], 1, 1), value[:, :-128]], axis=1)

    def right(self, value):
        if self.lanes == 128:
            return pltpu.roll(value, 127, 1)
        return jnp.concatenate([value[:, 128:], pltpu.roll(value[:, :128], 127, 1)], axis=1)

    def scaled(self, value, factor):
        if self.mask is None:
            return factor * value
        return (factor * self.mask) * value

    def at(self, ref, plane, row, shift=0):
        return ref[plane, pl.ds(GUARD + row + 8 * shift, 8), :]

    def put(self, ref, plane, row, value, lane=slice(None)):
        ref[plane, pl.ds(GUARD + row, 8), lane] = value
        sublane = lax.broadcasted_iota(jnp.int32, (8, 1), 0)
        last = self.rows - 8

        def top():
            ref[plane, pl.ds(0, 8), lane] = jnp.where(sublane == 0, 0.0, pltpu.roll(value, 1, 0))

        def bottom():
            ref[plane, pl.ds(GUARD + self.rows, 8), lane] = jnp.where(sublane == 7, 0.0, pltpu.roll(value, 7, 0))

        for edge, fill in ((last, top), (0, bottom)):
            if not isinstance(row, int):
                pl.when(row == edge)(fill)
            elif row == edge:
                fill()

    def get(self, ref, plane, row):
        return ref[plane, pl.ds(row, 8), :]

    def set(self, ref, plane, row, value):
        ref[plane, pl.ds(row, 8), :] = value

    def fine_rates(self, base, row):
        state = [[self.at(self.fine, base * 8 + s * 4 + p, row) for p in range(4)] for s in range(2)]
        linear, rates = [], []
        for p, (a, b) in enumerate(PHASES):
            laps = []
            for s in range(2):
                across = state[s][2 * a + 1 - b]
                along = state[s][2 * (1 - a) + b]
                moved = self.at(self.fine, base * 8 + s * 4 + 2 * (1 - a) + b, row, 1 if a else -1)
                side = self.right(across) if b else self.left(across)
                laps.append((along + moved) + (across + side) - 4.0 * state[s][p])
            u, v = state[0][p], state[1][p]
            feed = self.get(self.coef, p, row)
            both = self.get(self.coef, 4 + p, row)
            lin_u = self.scaled(laps[0], DIFF_U) + feed
            lin_v = self.scaled(laps[1], DIFF_V)
            linear.append((lin_u, lin_v))
            rates.append(self.reacted(u, v, lin_u, lin_v, feed, both))
        return state, linear, rates

    def reacted(self, u, v, lin_u, lin_v, feed, both):
        return lin_u - u * (feed + v * v), lin_v + v * (u * v - both)

    def neighbours(self, plane, row, value):
        rows = self.at(self.cs, plane, row, -1) + self.at(self.cs, plane, row, 1)
        return rows + (self.left(value) + self.right(value))

    def laplacians(self, first, row):
        pair = [self.at(self.cs, first + s, row) for s in range(2)]
        return pair, [self.neighbours(first + s, row, pair[s]) - 4.0 * pair[s] for s in range(2)]

    def coarse_rates(self, first, row):
        (u, v), laps = self.laplacians(first, row)
        scaled = [self.scaled(laps[s], 0.25 * (DIFF_U, DIFF_V)[s]) for s in range(2)]
        feed, both = self.get(self.cc, 0, row), self.get(self.cc, 1, row)
        return (u, v), scaled, self.reacted(u, v, scaled[0] + feed, scaled[1], feed, both)

    def moved_rates(self, shift, scaled, which, base, row):
        a, b = shift
        m_vv, m_uv, m_u, m_v = (self.get(self.mom, 4 * which + k, row) for k in range(4))
        react = a * (m_vv + b * (2.0 * m_v + b)) + b * (2.0 * m_uv + b * m_u)
        feed, both = self.get(self.cc, 0, row), self.get(self.cc, 1, row)
        rate_u = (self.get(self.cp, base, row) + 2.0 * scaled[0]) - (feed * a + react)
        rate_v = (self.get(self.cp, base + 1, row) + 2.0 * scaled[1]) + (react - both * b)
        return rate_u, rate_v

    def block_mean(self, values):
        return 0.25 * ((values[0] + values[1]) + (values[2] + values[3]))

    def run(self, own):
        lv = self
        cs, cp = self.cs, self.cp

        def first_sweep(row):
            for k in range(2):
                lv.set(lv.cc, k, row, lv.block_mean([lv.get(lv.coef, 4 * k + p, row) for p in range(4)]))
            state, linear, rates = lv.fine_rates(0, row)
            for s in range(2):
                for p in range(4):
                    lv.set(lv.lin, s * 4 + p, row, linear[p][s])
                    lv.put(lv.fine, 8 + s * 4 + p, row, state[s][p] + HALF_STEP * rates[p][s])
                mean = lv.block_mean([r[s] for r in rates])
                start = lv.block_mean(state[s])
                lv.set(cp, N_RA + s, row, mean)
                lv.put(cs, C_X0 + s, row, start)
                lv.put(cs, C_X1 + s, row, start + HALF_STEP * mean)
                lv.put(cs, C_END + s, row, start + mean)
                lv.put(cs, C_D1 + s, row, jnp.zeros_like(mean))

        def moments(which, state, row):
            u, v = state
            lv.set(lv.mom, 4 * which, row, lv.block_mean([v[p] * v[p] for p in range(4)]))
            lv.set(lv.mom, 4 * which + 1, row, lv.block_mean([u[p] * v[p] for p in range(4)]))
            lv.set(lv.mom, 4 * which + 2, row, lv.block_mean(u))
            lv.set(lv.mom, 4 * which + 3, row, lv.block_mean(v))

        def second_sweep(row):
            state, linear, rates = lv.fine_rates(1, row)
            _, _, g0 = lv.coarse_rates(C_X0, row)
            first, scaled, g1 = lv.coarse_rates(C_X1, row)
            for s in range(2):
                for p in range(4):
                    lv.set(lv.lin, 8 + s * 4 + p, row, linear[p][s])
                    lv.put(lv.fine, 16 + s * 4 + p, row, state[s][p] + HALF_STEP * rates[p][s])
                mean = lv.block_mean([r[s] for r in rates])
                lv.set(cp, N_F1 + s, row, mean)
                lv.set(cp, N_RB + s, row, mean - 2.0 * scaled[s])
                lv.put(cs, C_X2 + s, row, first[s] + HALF_STEP * mean)
                integral = HALF_STEP * lv.get(cp, N_RA + s, row)
                lv.set(cp, N_K0 + s, row, integral - HALF_STEP * g0[s])
                lv.set(cp, N_K1 + s, row, integral - HALF_STEP * g1[s])
            moments(0, state, row)

        def third_sweep(row):
            state, linear, rates = lv.fine_rates(2, row)
            for s in range(2):
                for p in range(4):
                    lv.set(lv.lin, 16 + s * 4 + p, row, linear[p][s])
            moments(1, state, row)
            second, laps = lv.laplacians(C_X2, row)
            for s in range(2):
                mean = lv.block_mean([r[s] for r in rates])
                lv.set(cp, N_RE + s, row, mean - lv.scaled(laps[s], 0.5 * (DIFF_U, DIFF_V)[s]))
            end, last = slice_end(C_D2, row)
            for s in range(2):
                j0, j1 = integrals(lv.get(cp, N_RA + s, row), lv.get(cp, N_F1 + s, row), last[s])
                lv.put(cs, C_NEW + s, row, lv.at(cs, C_X0 + s, row) + (j0 + j1))

        def integrals(f0, f1, f2):
            middle = W0[1] * f1
            return middle + (W0[0] * f0 + W0[2] * f2), middle + (W1[0] * f0 + W1[2] * f2)

        def slice_end(now, row):
            end, scaled, rate = lv.coarse_rates(C_END, row)
            shift = [end[s] - lv.at(cs, C_X2 + s, row) for s in range(2)]
            last = lv.moved_rates(shift, scaled, 1, N_RE, row)
            for s in range(2):
                half = HALF_STEP * rate[s]
                lv.set(cp, N_G0 + s, row, half)
                lv.put(cs, C_C1 + s, row, end[s] + half + lv.get(cp, N_K0 + s, row))
                lv.put(cs, now + s, row, shift[s])
                lv.set(cp, N_RF2 + s, row, last[s])
            return end, last

        def middle_nodes(row):
            mid, scaled, rate = lv.coarse_rates(C_C1, row)
            new, _, new_rate = lv.coarse_rates(C_NEW, row)
            shift = [mid[s] - lv.at(cs, C_X1 + s, row) for s in range(2)]
            f1 = lv.moved_rates(shift, scaled, 0, N_RB, row)
            for s in range(2):
                old = lv.at(cs, C_END + s, row)
                lv.set(cp, N_LAST + s, row, old)
                lv.set(cp, N_F1 + s, row, f1[s])
                lv.put(cs, C_D1 + s, row, shift[s])
                lv.put(cs, C_END + s, row, mid[s] + HALF_STEP * rate[s] + lv.get(cp, N_K1 + s, row))
                change = HALF_STEP * new_rate[s] - lv.get(cp, N_G0 + s, row)
                lv.put(cs, C_E1 + s, row, (new[s] - old) + change)

        def end_nodes(now):
            def body(row):
                before = [lv.get(cp, N_RF2 + s, row) for s in range(2)]
                _, last = slice_end(now, row)
                change, laps = lv.laplacians(C_E1, row)
                old, new, j1s = [], [], []
                for s in range(2):
                    j0, j1 = integrals(before[s], lv.get(cp, N_F1 + s, row), last[s])
                    old.append(lv.get(cp, N_LAST + s, row) + j0)
                    new.append(old[s] + change[s])
                    j1s.append(j1)
                feed, both = lv.get(lv.cc, 0, row), lv.get(lv.cc, 1, row)
                lin = [lv.scaled(laps[s], 0.25 * (DIFF_U, DIFF_V)[s]) for s in range(2)]
                rate_new = lv.reacted(new[0], new[1], lin[0], lin[1], feed, both)
                rate_old = lv.reacted(old[0], old[1], 0.0, 0.0, feed, both)
                for s in range(2):
                    total = new[s] + j1s[s] + HALF_STEP * (rate_new[s] - rate_old[s])
                    lv.put(cs, C_NEW + s, row, total)

            return body

        def corrections(starts):
            def body(row):
                for k, first in enumerate(starts):
                    for s in range(2):
                        d = lv.at(cs, first + s, row)
                        ring = [lv.at(cs, first + s, row, -1), lv.at(cs, first + s, row, 1), lv.left(d), lv.right(d)]
                        north, south, west, east = (lv.scaled(x - d, (DIFF_U, DIFF_V)[s]) for x in ring)
                        for p, (a, b) in enumerate(PHASES):
                            lv.set(lv.tl, k * 8 + s * 4 + p, row, (south if a else north) + (east if b else west))

            return body

        lv.each(first_sweep)
        lv.each(second_sweep)
        lv.each(third_sweep)

        def one_slice(n, carry):
            lv.each(middle_nodes)
            lv.each(end_nodes(C_D2 + 2 * lax.rem(n, 2)))
            return carry

        lax.fori_loop(1, own + 1, one_slice, 0)

        first = own == 0
        now = C_D2 + 2 * lax.rem(own, 2)
        before = jnp.where(first, C_D1, 2 * C_D2 + 2 - now)
        origin = jnp.where(first, 0, 2)
        lv.each(corrections((before, C_D1, now)))

        def own_nodes(row):
            for p in range(4):
                for t in range(0, lv.lanes, 128):
                    lane = pl.ds(t, 128)
                    high = pl.ds(GUARD + row, 8)
                    low = pl.ds(row, 8)
                    feed, both = lv.coef[p, low, lane], lv.coef[4 + p, low, lane]
                    rates, start = [], None
                    for k, (base, d) in enumerate(((origin, before), (1, C_D1), (2, now))):
                        pair = [lv.fine[base * 8 + s * 4 + p, high, lane] + cs[d + s, high, lane] for s in range(2)]
                        lin = [lv.lin[base * 8 + s * 4 + p, low, lane] + lv.tl[k * 8 + s * 4 + p, low, lane] for s in range(2)]
                        rates.append(lv.reacted(pair[0], pair[1], lin[0], lin[1], feed, both))
                        start = pair if k == 0 else start
                    for s in range(2):
                        f0, f1, f2 = (r[s] for r in rates)
                        second = start[s] + (W0[0] * f0 + W0[1] * f1 + W0[2] * f2)
                        lv.put(lv.fine, 24 + s * 4 + p, row, second, lane)
                        lv.rest[s * 4 + p, low, lane] = second + (W1[0] * f0 + (W1[1] - HALF_STEP) * f1 + W1[2] * f2)

        lv.each(own_nodes)

        def last_node(row):
            _, _, rates = lv.fine_rates(3, row)
            for s in range(2):
                ends = [lv.get(lv.rest, s * 4 + p, row) + HALF_STEP * rates[p][s] for p in range(4)]
                fix = lv.at(cs, C_NEW + s, row) - lv.block_mean(ends)
                for p in range(4):
                    lv.set(lv.rest, s * 4 + p, row, ends[p] + fix)

        lv.each(last_node)


def load_planes(level, sources, columns, natural):
    count = level.lanes // 128
    matrix = group_matrix(count, False)
    slot = slots(count)
    for read, first in sources:
        blocks = []
        for k in range(count):
            values = [read(plane, k) for plane in range(4)]
            blocks.append(permuted(jnp.concatenate(values, axis=0), matrix))
        rows = blocks[0].shape[0] // 4
        for b in range(2):
            tiles = exchanged([block[:, 128 * b : 128 * b + 128] for block in blocks], slot)
            for q, tile in enumerate(tiles):
                for plane in range(4):
                    natural[plane, 2 * q + b, pl.ds(first, rows), :] = tile[plane * rows : (plane + 1) * rows]
    chunks = level.chunks
    for q in range(count):
        for p, (a, b) in enumerate(PHASES):
            for t in range(chunks):
                picked = [natural[plane, 2 * q + b, pl.ds(2 * t + a, 8, stride=2 * chunks), :] for plane in range(4)]
                lane, row = pl.ds(128 * q, 128), 8 * t
                for s in range(2):
                    level.fine[s * 4 + p, pl.ds(GUARD + row, 8), lane] = picked[s]
                level.coef[p, pl.ds(row, 8), lane] = picked[2]
                level.coef[4 + p, pl.ds(row, 8), lane] = picked[2] + picked[3]
    for plane in range(8):
        for row in {0, level.rows - 8}:
            level.put(level.fine, plane, row, level.at(level.fine, plane, row))


def spread(level, natural):
    count, chunks = level.lanes // 128, level.chunks
    for s in range(2):
        for q in range(count):
            for p, (a, b) in enumerate(PHASES):
                for t in range(chunks):
                    value = level.rest[s * 4 + p, pl.ds(8 * t, 8), pl.ds(128 * q, 128)]
                    natural[s, 2 * q + b, pl.ds(2 * t + a, 8, stride=2 * chunks), :] = value


def merged(level, first, rows, natural):
    count = level.lanes // 128
    matrix = group_matrix(count, True)
    slot = slots(count)
    halves = []
    for b in range(2):
        tiles = []
        for q in range(count):
            tiles.append(jnp.concatenate([natural[s, 2 * q + b, pl.ds(first, rows), :] for s in range(2)], axis=0))
        halves.append(exchanged(tiles, slot))
    blocks = [permuted(jnp.concatenate([halves[0][k], halves[1][k]], axis=1), matrix) for k in range(count)]
    return [[block[s * rows : (s + 1) * rows] for block in blocks] for s in range(2)]


def own_first(rows):
    return pl.multiple_of(lax.axis_index("gx") * rows, rows)


def source_list(refs, rows, parts):
    if parts == 2:
        mine = own_first(rows)
        return [(refs[0::2], mine), (refs[1::2], pl.multiple_of(rows - mine, rows))]
    return [(tuple(ref.at[g] for ref in refs), g * rows) for g in range(parts)]


def interior_kernel(parts, rows, columns, halo, depth, width, *refs):
    count, outs = (6, 3) if parts == 2 else (3, 2)
    ins, window, keep, give = refs[:count], refs[count], refs[count + 1], refs[count + 2]
    work = refs[count + outs :]
    here = columns // 2 if parts == 2 else columns
    origin = pl.multiple_of(lax.axis_index("gx") * here, here) if parts == 2 else 0
    level = Level(work[:-1], parts * rows // 2, here // 2, None)
    seam = 4 * depth if parts == 2 else 0
    side = (width - seam) // 2 - halo

    def reader(state, feed, kill):
        def read(plane, block):
            lane = pl.ds(origin + 256 * block, 256)
            return state[plane, :, lane] if plane < 2 else (feed, kill)[plane - 2][:, lane]

        return read

    sources = []
    for (state, feed, kill), first in source_list(ins, rows, parts):
        sources.append((reader(state, feed, kill), first))
        for plane in range(4):
            value = state[plane] if plane < 2 else (feed, kill)[plane - 2][...]
            cuts = [value[:, :halo], value[:, :side], value[:, (columns - seam) // 2 : (columns + seam) // 2]]
            cuts += [value[:, columns - side :], value[:, columns - halo :]]
            window[plane, pl.ds(first, rows), :] = jnp.concatenate([cut for cut in cuts if cut.shape[1]], axis=1)
    load_planes(level, sources, here, work[-1])
    level.run(lax.axis_index("ta"))
    spread(level, work[-1])
    mine = own_first(rows)
    targets = [(keep, mine), (give, pl.multiple_of(rows - mine, rows))] if parts == 2 else [(keep, mine)]
    for target, first in targets:
        natural = merged(level, first, rows, work[-1])
        for s in range(2):
            for k, block in enumerate(natural[s]):
                target[s, :, pl.ds(256 * k, 256)] = block


def border_kernel(parts, rows, halo, depth, width, *refs):
    count, inners = (4, 2) if parts == 2 else (2, 1)
    strips, window, inner = refs[:count], refs[count], refs[count + 1 : count + 1 + inners]
    out, work = refs[count + 1 + inners], refs[count + 2 + inners :]
    lanes = width // 2
    seam = 4 * depth if parts == 2 else 0
    index, size = lax.axis_index("gy"), lax.axis_size("gy")
    even = lax.rem(index, 2) == 0
    tiles = lanes // 128
    at = lax.broadcasted_iota(jnp.int32, (1, lanes), 1)
    at = tiles * (at % 128) + at // 128
    outside = ((at < halo // 2) & (index == 0)) | ((at >= lanes - halo // 2) & (index == size - 1))
    level = Level(work[:-1], parts * rows // 2, lanes, jnp.where(outside, 0.0, 1.0))

    def reader(from_a, from_b, first):
        def read(plane, block):
            part = slice(halo * plane, halo * plane + halo)
            a, b = from_a[:, part], from_b[:, part]
            low, high = jnp.where(even, b, a), jnp.where(even, a, b)
            own = window[plane, pl.ds(first, rows), :]
            whole = jnp.concatenate([low, own[:, halo : width - halo], high], axis=1)
            return whole[:, 256 * block : 256 * block + 256]

        return read

    sources = [(reader(a, b, first), first) for (a, b), first in source_list(strips, rows, parts)]
    load_planes(level, sources, width, work[-1])
    total = out.shape[-1]
    share = total // inners
    for k, value in enumerate(inner):
        origin = lax.axis_index("gx") * share
        origin = 0 if inners == 1 else pl.multiple_of(origin if k == 0 else share - origin, share)
        out[0, :, :, pl.ds(origin, share)] = value[...]
    level.run(lax.axis_index("ta"))
    spread(level, work[-1])
    natural = merged(level, own_first(rows), rows, work[-1])
    pieces = [(0, halo, depth), (total - depth, width - halo - depth, depth)]
    if seam:
        pieces.append((total // 2 - depth, width // 2 - depth, depth))
        pieces.append((total // 2, width // 2, depth))
    for s in range(2):
        whole = jnp.concatenate(natural[s], axis=1) if len(natural[s]) > 1 else natural[s][0]
        for column, source, size in pieces:
            low = column // 128 * 128
            high = round_up(column + size, 128)
            old = out[0, s, :, pl.ds(low, high - low)]
            parts_of = [old[:, : column - low], whole[:, source : source + size], old[:, column + size - low :]]
            out[0, s, :, pl.ds(low, high - low)] = jnp.concatenate([x for x in parts_of if x.shape[1]], axis=1)


def pack_kernel(halo, state, feed, kill, to_a, to_b, left, right, sems):
    width, total = left.shape[-1], feed.shape[1]
    copies = []
    for side, (target, lane) in enumerate(((left, pl.ds(0, width)), (right, pl.ds(total - width, width)))):
        copies.append(pltpu.make_async_copy(state.at[:, :, lane], target.at[pl.ds(0, 2)], sems.at[side, 0]))
        copies.append(pltpu.make_async_copy(feed.at[:, lane], target.at[2], sems.at[side, 1]))
        copies.append(pltpu.make_async_copy(kill.at[:, lane], target.at[3], sems.at[side, 2]))
    for copy in copies:
        copy.start()
    for copy in copies:
        copy.wait()
    low = jnp.concatenate([left[plane, :, :halo] for plane in range(4)], axis=1)
    high = jnp.concatenate([right[plane, :, width - halo :] for plane in range(4)], axis=1)
    even = lax.rem(lax.axis_index("gy"), 2) == 0
    to_a[...] = jnp.where(even, high, low)
    to_b[...] = jnp.where(even, low, high)


def both_ways(pairs):
    return [pair for low, high in pairs for pair in ((low, high), (high, low))]


VMEM = pl.BlockSpec(memory_space=pltpu.VMEM)
ANY = pl.BlockSpec(memory_space=pl.ANY)


def work_of(rows, lanes):
    shapes = scratch(rows, lanes) + [pltpu.VMEM((4, 2 * lanes // 128, 2 * rows, 128), F32)]
    size = sum(4 * math.prod(shape.shape) for shape in shapes)
    return shapes, size


def per_device(initial_state, feed_rate, kill_rate):
    slices, parts, blocks = (lax.axis_size(axis) for axis in ("ta", "gx", "gy"))
    _, rows, columns = initial_state.shape
    depth = 2 * (2 * slices + 2)
    halo = round_up(depth, 32)
    seam = 4 * depth if parts == 2 else 0
    width = round_up(2 * halo + 4 * depth + seam, 256)
    strip = round_up(halo, 128)
    every = parts * rows
    here = columns // 2 if parts == 2 else columns

    def across(value):
        if parts == 2:
            return [value, lax.ppermute(value, "gx", [(0, 1), (1, 0)])]
        return [lax.all_gather(value, "gx")]

    to_a, to_b = pl.pallas_call(
        functools.partial(pack_kernel, halo),
        out_shape=[jax.ShapeDtypeStruct((rows, 4 * halo), F32)] * 2,
        in_specs=[ANY] * 3,
        out_specs=[VMEM] * 2,
        scratch_shapes=[pltpu.VMEM((4, rows, strip), F32)] * 2 + [pltpu.SemaphoreType.DMA((2, 3))],
        name="pack",
    )(initial_state, feed_rate, kill_rate)
    fields = [value for field in (initial_state, feed_rate, kill_rate) for value in across(field)]
    from_b = lax.ppermute(to_b, "gy", both_ways([(i, i + 1) for i in range(1, blocks - 1, 2)]))
    from_a = lax.ppermute(to_a, "gy", both_ways([(i, i + 1) for i in range(0, blocks - 1, 2)]))
    work, size = work_of(every // 2, here // 2)
    window, *inner = pl.pallas_call(
        functools.partial(interior_kernel, parts, rows, columns, halo, depth, width),
        out_shape=[jax.ShapeDtypeStruct((4, every, width), F32)]
        + [jax.ShapeDtypeStruct((2, rows, here), F32)] * (2 if parts == 2 else 1),
        in_specs=[VMEM] * len(fields),
        out_specs=[VMEM] * (3 if parts == 2 else 2),
        scratch_shapes=work,
        compiler_params=pltpu.CompilerParams(vmem_limit_bytes=size + 32 * every * (columns + width) + 2**22),
        cost_estimate=pl.CostEstimate(flops=40 * 2**20, bytes_accessed=20 * 2**20, transcendentals=0),
        name="interior",
    )(*fields)
    from_a, from_b, window, *inner = lax.optimization_barrier((from_a, from_b, window, *inner))
    if parts == 2:
        inner[1] = lax.ppermute(inner[1], "gx", [(0, 1), (1, 0)])
    strips = [value for strip in (from_a, from_b) for value in across(strip)]
    work, size = work_of(every // 2, width // 2)
    return pl.pallas_call(
        functools.partial(border_kernel, parts, rows, halo, depth, width),
        out_shape=jax.ShapeDtypeStruct((1, 2, rows, columns), F32),
        in_specs=[VMEM] * (len(strips) + 1 + len(inner)),
        out_specs=VMEM,
        scratch_shapes=work,
        compiler_params=pltpu.CompilerParams(vmem_limit_bytes=size + 32 * rows * columns + 2**23),
        name="border",
    )(*strips, window, *inner)


def solution(mesh):
    placed = (P(None, "gx", "gy"), P("gx", "gy"), P("gx", "gy"))
    return jax.shard_map(
        per_device, mesh=mesh, in_specs=placed, out_specs=P("ta", None, "gx", "gy"), check_vma=False
    )
```

time: 27.6 us -> 15.4 us (0.56)
  Pallas kernels: 15.2 us -> 7.25 us
  local copies, waits for them, and re-layouts: 5.44 us -> 0.01 us
  waiting for transfers between devices: 0.07 us -> 1.2 us
    pallas_call x1, Pallas kernels: 9.25 us -> 3.05 us  [per_device(): pl.pallas_call(functools.partial(interior_kernel, parts, rows, columns, h...]
    slice x5 -> x0, local copies, waits for them, and re-layouts: 4.78 us -> none  [per_device(): value[..., columns - edge:]]
    pallas_call x1, Pallas kernels: 4.25 us -> 2.65 us  [per_device(): pl.pallas_call(functools.partial(border_kernel, parts, rows, halo, depth,...]
    ppermute x0 -> x1, starting transfers between devices: none -> 1.49 us  [per_device(): inner[1] = lax.ppermute(inner[1], 'gx', [(0, 1), (1, 0)])]
    ppermute x5, starting transfers between devices: 3.23 us -> 1.76 us  [across(): return [value, lax.ppermute(value, 'gx', [(0, 1), (1, 0)])]]
    ppermute x5, waiting for transfers between devices: 0.01 us -> 0.85 us  [across(): return [value, lax.ppermute(value, 'gx', [(0, 1), (1, 0)])]]
    unnamed x14 -> x6, local copies, waits for them, and re-layouts: 0.66 us -> 0.01 us
    ppermute x1, waiting for transfers between devices: 0.05 us -> 0.35 us  [per_device(): lax.ppermute(to_b, 'gy', both_ways([(i, i + 1) for i in range(1, blocks -...]
  transfers between devices with their start and end apart: 7 -> 8, of which waited for: 1 -> 3; matrix products, arithmetic and copies ran while one was open for 17% -> 0% of each run, Pallas kernels for 40% -> 30%
where the time goes in v2:
time: 15.4 us; the launch traced here: 15.2 us
  Pallas kernels  7.25 us (47%)
  starting transfers between devices  6.64 us (43%)
  waiting for transfers between devices  1.2 us (8%)
    pallas_call x1, Pallas kernels, per_device(): pl.pallas_call(functools.partial(interior_kernel, parts, rows, columns, h...  3.05 us
    pallas_call x1, Pallas kernels, per_device(): pl.pallas_call(functools.partial(border_kernel, parts, rows, halo, depth,...  2.65 us
    ppermute x1, starting transfers between devices, per_device(): lax.ppermute(to_b, 'gy', both_ways([(i, i + 1) for i in range(1, blocks -...  2.09 us
    ppermute x5, starting transfers between devices, across(): return [value, lax.ppermute(value, 'gx', [(0, 1), (1, 0)])]  1.76 us
    pallas_call x1, Pallas kernels, per_device(): pl.pallas_call(functools.partial(pack_kernel, halo), out_shape=[jax.Shape...  1.56 us
    ppermute x1, starting transfers between devices, per_device(): inner[1] = lax.ppermute(inner[1], 'gx', [(0, 1), (1, 0)])  1.49 us
    ppermute x1, starting transfers between devices, per_device(): lax.ppermute(to_a, 'gy', both_ways([(i, i + 1) for i in range(0, blocks -...  1.29 us
    ppermute x5, waiting for transfers between devices, across(): return [value, lax.ppermute(value, 'gx', [(0, 1), (1, 0)])]  0.85 us
  transfers between devices with their start and end apart: 8, of which 3 were waited for; matrix products, arithmetic and copies ran while one was open for 0% of the time, Pallas kernels for 30%

profile of v2, /device:TPU:29, one launch (start us, length us, event | category | flops | bytes accessed | tf_op | source)
XLA Modules:
  0.0 15.2 jit_solution(3109286891852825881)
XLA Ops:
  0.0 0.0 copy-start
  0.0 0.0 copy-start.1
  0.0 0.7 %collective-permute-start.2 = (f32[2,32,1024]{2,1,0:T(8,128)}, f32[2,32,1024]{2,1,0:T(8,128)S(1)}, u32[]{:S(2)}, u32[]{:S(2)}) collective-permute-start(f32[2,32,1024]{2,1,0:T(8,128)} %refs_0_.1), channel_id=1, source_target_pairs={{0,4},{4,0},{1,5},{5,1},{2,6},{6,2},{3,7},{7,3},{8,12},{12,8},{9,1... | collective-permute-start | bytes 786440 | tf_op jit(solution)/shard_map/ppermute | solution.py:562
  0.8 0.1 collective-permute-start.3
  0.8 0.4 %collective-permute-start.4 = (f32[32,1024]{1,0:T(8,128)}, f32[32,1024]{1,0:T(8,128)S(1)}, u32[]{:S(2)}, u32[]{:S(2)}) collective-permute-start(f32[32,1024]{1,0:T(8,128)} %refs_4_.1), channel_id=1, source_target_pairs={{0,4},{4,0},{1,5},{5,1},{2,6},{6,2},{3,7},{7,3},{8,12},{12,8},{9,1... | collective-permute-start | bytes 393224 | tf_op jit(solution)/shard_map/ppermute | solution.py:562
  1.3 1.6 %pack.1 = (f32[32,128]{1,0:T(8,128)}, f32[32,128]{1,0:T(8,128)}) custom-call(f32[2,32,1024]{2,1,0:T(8,128)} %refs_0_.1, f32[32,1024]{1,0:T(8,128)} %refs_2_.1, f32[32,1024]{1,0:T(8,128)} %refs_4_.1), custom_call_target="tpu_custom_call" | custom-call | tf_op jit(solution)/shard_map/pack/pallas_call | solution.py:565
  2.8 1.3 %collective-permute-start = (f32[32,128]{1,0:T(8,128)}, f32[32,128]{1,0:T(8,128)S(1)}, u32[]{:S(2)}, u32[]{:S(2)}) collective-permute-start(f32[32,128]{1,0:T(8,128)} %get-tuple-element.15), channel_id=1, source_target_pairs={{0,1},{1,0},{2,3},{3,2},{4,5},{5,4},{6,7},{7,6},{8,9},{9,8},{10,11... | collective-permute-start | bytes 49160 | tf_op jit(solution)/shard_map/ppermute | solution.py:575
  4.1 2.1 %collective-permute-start.1 = (f32[32,128]{1,0:T(8,128)}, f32[32,128]{1,0:T(8,128)S(1)}, u32[]{:S(2)}, u32[]{:S(2)}) collective-permute-start(f32[32,128]{1,0:T(8,128)} %get-tuple-element.16), channel_id=1, source_target_pairs={{1,2},{2,1},{5,6},{6,5},{9,10},{10,9},{13,14},{14,13},{17,18},{18,... | collective-permute-start | bytes 49160 | tf_op jit(solution)/shard_map/ppermute | solution.py:574
  6.2 0.0 collective-permute-done.3.refs_3_
  6.2 0.0 collective-permute-done.4.refs_5_
  6.2 0.0 collective-permute-done.2.refs_1_
  6.3 0.0 copy-done
  6.3 0.0 copy-done.1
  6.3 0.0 copy-done.2
  6.3 3.0 %interior.1 = (f32[4,64,256]{2,1,0:T(8,128)S(1)}, f32[2,32,512]{2,1,0:T(8,128)S(1)}, f32[2,32,512]{2,1,0:T(8,128)S(1)}) custom-call(f32[2,32,1024]{2,1,0:T(8,128)S(1)} %copy-done, f32[2,32,1024]{2,1,0:T(8,128)S(1)} %collective-permute-done.2.refs_1_, f32[32,1024]{1,0:T(8,128)S(1)} %copy-done.1, f32[32,1024]{1,0:T(8,128)S(1)} %collective-permute-done.3.refs_3_, ...), custom_call_target="tpu_custom_call" | custom-call | flops 41943040 | bytes 20971520 | tf_op jit(solution)/shard_map/interior/pallas_call | solution.py:577
  9.3 0.0 collective-permute-done.refs_0_
  9.3 0.4 %collective-permute-done.1.refs_2_ = f32[32,128]{1,0:T(8,128)S(1)} collective-permute-done((f32[32,128]{1,0:T(8,128)}, f32[32,128]{1,0:T(8,128)S(1)}, u32[]{:S(2)}, u32[]{:S(2)}) %collective-permute-start.1) | collective-permute-done | bytes 16416 | tf_op jit(solution)/shard_map/ppermute | solution.py:574
  9.7 1.5 %collective-permute-start.7 = (f32[2,32,512]{2,1,0:T(8,128)S(1)}, f32[2,32,512]{2,1,0:T(8,128)S(1)}, u32[]{:S(2)}, u32[]{:S(2)}) collective-permute-start(f32[2,32,512]{2,1,0:T(8,128)S(1)} %get-tuple-element.24), channel_id=1, source_target_pairs={{0,4},{4,0},{1,5},{5,1},{2,6},{6,2},{3,7},{7,3},{8,12},{12,8},{9,1... | collective-permute-start | bytes 393224 | tf_op jit(solution)/shard_map/ppermute | solution.py:590
  11.2 0.0 collective-permute-start.5
  11.2 0.5 %collective-permute-start.6 = (f32[32,128]{1,0:T(8,128)S(1)}, f32[32,128]{1,0:T(8,128)S(1)}, u32[]{:S(2)}, u32[]{:S(2)}) collective-permute-start(f32[32,128]{1,0:T(8,128)S(1)} %collective-permute-done.1.refs_2_), channel_id=1, source_target_pairs={{0,4},{4,0},{1,5},{5,1},{2,6},{6,2},{3,7},{7,3},{8,12},{12,8},{9,1... | collective-permute-start | bytes 49160 | tf_op jit(solution)/shard_map/ppermute | solution.py:562
  11.7 0.7 %collective-permute-done.5.refs_1_ = f32[32,128]{1,0:T(8,128)S(1)} collective-permute-done((f32[32,128]{1,0:T(8,128)S(1)}, f32[32,128]{1,0:T(8,128)S(1)}, u32[]{:S(2)}, u32[]{:S(2)}) %collective-permute-start.5) | collective-permute-done | bytes 16416 | tf_op jit(solution)/shard_map/ppermute | solution.py:562
  12.4 0.2 %collective-permute-done.6.refs_3_ = f32[32,128]{1,0:T(8,128)S(1)} collective-permute-done((f32[32,128]{1,0:T(8,128)S(1)}, f32[32,128]{1,0:T(8,128)S(1)}, u32[]{:S(2)}, u32[]{:S(2)}) %collective-permute-start.6) | collective-permute-done | bytes 16416 | tf_op jit(solution)/shard_map/ppermute | solution.py:562
  12.5 0.0 collective-permute-done.7.refs_6_
  12.5 2.6 %border.1 = f32[1,2,32,1024]{3,2,1,0:T(8,128)} custom-call(f32[32,128]{1,0:T(8,128)S(1)} %collective-permute-done.refs_0_, f32[32,128]{1,0:T(8,128)S(1)} %collective-permute-done.5.refs_1_, f32[32,128]{1,0:T(8,128)S(1)} %collective-permute-done.1.refs_2_, f32[32,128]{1,0:T(8,128)S(1)} %collective-permute-done.6.refs_3_, ...), custom_call_target="tpu_custom_call" | custom-call | tf_op jit(solution)/shard_map/border/pallas_call | solution.py:593
  (1 shorter events, 0.0 us)
Async XLA Ops:
  0.0 6.3 %copy-start = (f32[2,32,1024]{2,1,0:T(8,128)S(1)}, f32[2,32,1024]{2,1,0:T(8,128)}, u32[]{:S(2)}) copy-start(f32[2,32,1024]{2,1,0:T(8,128)} %refs_0_.1) | copy-start | bytes 786436
  0.0 6.3 %copy-start.1 = (f32[32,1024]{1,0:T(8,128)S(1)}, f32[32,1024]{1,0:T(8,128)}, u32[]{:S(2)}) copy-start(f32[32,1024]{1,0:T(8,128)} %refs_2_.1) | copy-start | bytes 393220
  0.0 6.3 %copy-start.2 = (f32[32,1024]{1,0:T(8,128)S(1)}, f32[32,1024]{1,0:T(8,128)}, u32[]{:S(2)}) copy-start(f32[32,1024]{1,0:T(8,128)} %refs_4_.1) | copy-start | bytes 393220
  0.0 6.2 %collective-permute-start.2 = (f32[2,32,1024]{2,1,0:T(8,128)}, f32[2,32,1024]{2,1,0:T(8,128)S(1)}, u32[]{:S(2)}, u32[]{:S(2)}) collective-permute-start(f32[2,32,1024]{2,1,0:T(8,128)} %refs_0_.1), channel_id=1, source_target_pairs={{0,4},{4,0},{1,5},{5,1},{2,6},{6,2},{3,7},{7,3},{8,12},{12,8},{9,1... | collective-permute-start | bytes 786440 | tf_op jit(solution)/shard_map/ppermute | solution.py:562
  0.8 5.5 %collective-permute-start.3 = (f32[32,1024]{1,0:T(8,128)}, f32[32,1024]{1,0:T(8,128)S(1)}, u32[]{:S(2)}, u32[]{:S(2)}) collective-permute-start(f32[32,1024]{1,0:T(8,128)} %refs_2_.1), channel_id=1, source_target_pairs={{0,4},{4,0},{1,5},{5,1},{2,6},{6,2},{3,7},{7,3},{8,12},{12,8},{9,1... | collective-permute-start | bytes 393224 | tf_op jit(solution)/shard_map/ppermute | solution.py:562
  0.8 5.4 %collective-permute-start.4 = (f32[32,1024]{1,0:T(8,128)}, f32[32,1024]{1,0:T(8,128)S(1)}, u32[]{:S(2)}, u32[]{:S(2)}) collective-permute-start(f32[32,1024]{1,0:T(8,128)} %refs_4_.1), channel_id=1, source_target_pairs={{0,4},{4,0},{1,5},{5,1},{2,6},{6,2},{3,7},{7,3},{8,12},{12,8},{9,1... | collective-permute-start | bytes 393224 | tf_op jit(solution)/shard_map/ppermute | solution.py:562
  2.8 6.5 %collective-permute-start = (f32[32,128]{1,0:T(8,128)}, f32[32,128]{1,0:T(8,128)S(1)}, u32[]{:S(2)}, u32[]{:S(2)}) collective-permute-start(f32[32,128]{1,0:T(8,128)} %get-tuple-element.15), channel_id=1, source_target_pairs={{0,1},{1,0},{2,3},{3,2},{4,5},{5,4},{6,7},{7,6},{8,9},{9,8},{10,11... | collective-permute-start | bytes 49160 | tf_op jit(solution)/shard_map/ppermute | solution.py:575
  4.1 5.6 %collective-permute-start.1 = (f32[32,128]{1,0:T(8,128)}, f32[32,128]{1,0:T(8,128)S(1)}, u32[]{:S(2)}, u32[]{:S(2)}) collective-permute-start(f32[32,128]{1,0:T(8,128)} %get-tuple-element.16), channel_id=1, source_target_pairs={{1,2},{2,1},{5,6},{6,5},{9,10},{10,9},{13,14},{14,13},{17,18},{18,... | collective-permute-start | bytes 49160 | tf_op jit(solution)/shard_map/ppermute | solution.py:574
  9.7 2.8 %collective-permute-start.7 = (f32[2,32,512]{2,1,0:T(8,128)S(1)}, f32[2,32,512]{2,1,0:T(8,128)S(1)}, u32[]{:S(2)}, u32[]{:S(2)}) collective-permute-start(f32[2,32,512]{2,1,0:T(8,128)S(1)} %get-tuple-element.24), channel_id=1, source_target_pairs={{0,4},{4,0},{1,5},{5,1},{2,6},{6,2},{3,7},{7,3},{8,12},{12,8},{9,1... | collective-permute-start | bytes 393224 | tf_op jit(solution)/shard_map/ppermute | solution.py:590
  11.2 1.2 %collective-permute-start.5 = (f32[32,128]{1,0:T(8,128)S(1)}, f32[32,128]{1,0:T(8,128)S(1)}, u32[]{:S(2)}, u32[]{:S(2)}) collective-permute-start(f32[32,128]{1,0:T(8,128)S(1)} %collective-permute-done.refs_0_), channel_id=1, source_target_pairs={{0,4},{4,0},{1,5},{5,1},{2,6},{6,2},{3,7},{7,3},{8,12},{12,8},{9,1... | collective-permute-start | bytes 49160 | tf_op jit(solution)/shard_map/ppermute | solution.py:562
  11.2 1.3 %collective-permute-start.6 = (f32[32,128]{1,0:T(8,128)S(1)}, f32[32,128]{1,0:T(8,128)S(1)}, u32[]{:S(2)}, u32[]{:S(2)}) collective-permute-start(f32[32,128]{1,0:T(8,128)S(1)} %collective-permute-done.1.refs_2_), channel_id=1, source_target_pairs={{0,4},{4,0},{1,5},{5,1},{2,6},{6,2},{3,7},{7,3},{8,12},{12,8},{9,1... | collective-permute-start | bytes 49160 | tf_op jit(solution)/shard_map/ppermute | solution.py:562

commit v3 on v2

--- a/solution.py
+++ b/solution.py
@@ -483,6 +483,7 @@
             part = slice(halo * plane, halo * plane + halo)
             a, b = from_a[:, part], from_b[:, part]
             low, high = jnp.where(even, b, a), jnp.where(even, a, b)
+            low, high = jnp.where(index == 0, 0.0, low), jnp.where(index == size - 1, 0.0, high)
             own = window[plane, pl.ds(first, rows), :]
             whole = jnp.concatenate([low, own[:, halo : width - halo], high], axis=1)
             return whole[:, 256 * block : 256 * block + 256]
@@ -568,10 +569,11 @@
         in_specs=[ANY] * 3,
         out_specs=[VMEM] * 2,
         scratch_shapes=[pltpu.VMEM((4, rows, strip), F32)] * 2 + [pltpu.SemaphoreType.DMA((2, 3))],
+        compiler_params=pltpu.CompilerParams(vmem_limit_bytes=54 * 2**20 - 2**17),
         name="pack",
     )(initial_state, feed_rate, kill_rate)
     fields = [value for field in (initial_state, feed_rate, kill_rate) for value in across(field)]
-    from_b = lax.ppermute(to_b, "gy", both_ways([(i, i + 1) for i in range(1, blocks - 1, 2)]))
+    from_b = lax.ppermute(to_b, "gy", both_ways([(i, (i + 1) % blocks) for i in range(1, blocks - blocks % 2, 2)]))
     from_a = lax.ppermute(to_a, "gy", both_ways([(i, i + 1) for i in range(0, blocks - 1, 2)]))
     work, size = work_of(every // 2, here // 2)
     window, *inner = pl.pallas_call(

time: 15.4 us -> 13.2 us (0.86)
  the two profiles are of different devices: /device:TPU:29 before, /device:TPU:0 now
where the time goes in v3:
time: 13.2 us; the launch traced here: 13 us
  starting transfers between devices  5.66 us (43%)
  Pallas kernels  5.16 us (39%)
  waiting for transfers between devices  2.08 us (16%)
    ppermute x1, starting transfers between devices, per_device(): lax.ppermute(to_a, 'gy', both_ways([(i, i + 1) for i in range(0, blocks -...  2.63 us
    pallas_call x1, Pallas kernels, per_device(): pl.pallas_call(functools.partial(interior_kernel, parts, rows, columns, h...  2.2 us
    pallas_call x1, Pallas kernels, per_device(): pl.pallas_call(functools.partial(border_kernel, parts, rows, halo, depth,...  2.01 us
    ppermute x5, starting transfers between devices, across(): return [value, lax.ppermute(value, 'gx', [(0, 1), (1, 0)])]  1.54 us
    ppermute x1, starting transfers between devices, per_device(): lax.ppermute(to_b, 'gy', both_ways([(i, (i + 1) % blocks) for i in range(...  1.49 us
    ppermute x5, waiting for transfers between devices, across(): return [value, lax.ppermute(value, 'gx', [(0, 1), (1, 0)])]  1.19 us
    pallas_call x1, Pallas kernels, per_device(): pl.pallas_call(functools.partial(pack_kernel, halo), out_shape=[jax.Shape...  0.95 us
    ppermute x1, waiting for transfers between devices, per_device(): lax.ppermute(to_b, 'gy', both_ways([(i, (i + 1) % blocks) for i in range(...  0.88 us
  transfers between devices with their start and end apart: 8, of which 3 were waited for; matrix products, arithmetic and copies ran while one was open for 0% of the time, Pallas kernels for 24%

profile of v3, /device:TPU:0, one launch (start us, length us, event | category | flops | bytes accessed | tf_op | source)
XLA Modules:
  0.0 13.0 jit_solution(1472620043219178819)
XLA Ops:
  0.0 0.0 copy-start
  0.0 0.0 copy-start.1
  0.0 0.5 %collective-permute-start.2 = (f32[2,32,1024]{2,1,0:T(8,128)}, f32[2,32,1024]{2,1,0:T(8,128)S(1)}, u32[]{:S(2)}, u32[]{:S(2)}) collective-permute-start(f32[2,32,1024]{2,1,0:T(8,128)} %refs_0_.1), channel_id=1, source_target_pairs={{0,4},{4,0},{1,5},{5,1},{2,6},{6,2},{3,7},{7,3},{8,12},{12,8},{9,1... | collective-permute-start | bytes 786440 | tf_op jit(solution)/shard_map/ppermute | solution.py:563
  0.5 0.1 collective-permute-start.3
  0.6 0.4 %collective-permute-start.4 = (f32[32,1024]{1,0:T(8,128)}, f32[32,1024]{1,0:T(8,128)S(1)}, u32[]{:S(2)}, u32[]{:S(2)}) collective-permute-start(f32[32,1024]{1,0:T(8,128)} %refs_4_.1), channel_id=1, source_target_pairs={{0,4},{4,0},{1,5},{5,1},{2,6},{6,2},{3,7},{7,3},{8,12},{12,8},{9,1... | collective-permute-start | bytes 393224 | tf_op jit(solution)/shard_map/ppermute | solution.py:563
  1.0 1.0 %pack.1 = (f32[32,128]{1,0:T(8,128)S(1)}, f32[32,128]{1,0:T(8,128)S(1)}) custom-call(f32[2,32,1024]{2,1,0:T(8,128)} %refs_0_.1, f32[32,1024]{1,0:T(8,128)} %refs_2_.1, f32[32,1024]{1,0:T(8,128)} %refs_4_.1), custom_call_target="tpu_custom_call" | custom-call | tf_op jit(solution)/shard_map/pack/pallas_call | solution.py:566
  2.0 2.6 %collective-permute-start = (f32[32,128]{1,0:T(8,128)S(1)}, f32[32,128]{1,0:T(8,128)S(1)}, u32[]{:S(2)}, u32[]{:S(2)}) collective-permute-start(f32[32,128]{1,0:T(8,128)S(1)} %get-tuple-element.15), channel_id=1, source_target_pairs={{0,1},{1,0},{2,3},{3,2},{4,5},{5,4},{6,7},{7,6},{8,9},{9,8},{10,11... | collective-permute-start | bytes 49160 | tf_op jit(solution)/shard_map/ppermute | solution.py:577
  4.6 1.5 %collective-permute-start.1 = (f32[32,128]{1,0:T(8,128)S(1)}, f32[32,128]{1,0:T(8,128)S(1)}, u32[]{:S(2)}, u32[]{:S(2)}) collective-permute-start(f32[32,128]{1,0:T(8,128)S(1)} %get-tuple-element.16), channel_id=1, source_target_pairs={{1,2},{2,1},{3,0},{0,3},{5,6},{6,5},{7,4},{4,7},{9,10},{10,9},{11,... | collective-permute-start | bytes 49160 | tf_op jit(solution)/shard_map/ppermute | solution.py:576
  6.1 0.0 collective-permute-done.3.refs_3_
  6.1 0.0 collective-permute-done.4.refs_5_
  6.1 0.0 collective-permute-done.2.refs_1_
  6.1 0.0 copy-done
  6.1 0.0 copy-done.1
  6.2 0.0 copy-done.2
  6.2 2.2 %interior.1 = (f32[4,64,256]{2,1,0:T(8,128)S(1)}, f32[2,32,512]{2,1,0:T(8,128)S(1)}, f32[2,32,512]{2,1,0:T(8,128)S(1)}) custom-call(f32[2,32,1024]{2,1,0:T(8,128)S(1)} %copy-done, f32[2,32,1024]{2,1,0:T(8,128)S(1)} %collective-permute-done.2.refs_1_, f32[32,1024]{1,0:T(8,128)S(1)} %copy-done.1, f32[32,1024]{1,0:T(8,128)S(1)} %collective-permute-done.3.refs_3_, ...), custom_call_target="tpu_custom_call" | custom-call | flops 41943040 | bytes 20971520 | tf_op jit(solution)/shard_map/interior/pallas_call | solution.py:579
  8.4 0.0 collective-permute-done.refs_0_
  8.4 0.9 %collective-permute-done.1.refs_2_ = f32[32,128]{1,0:T(8,128)S(1)} collective-permute-done((f32[32,128]{1,0:T(8,128)S(1)}, f32[32,128]{1,0:T(8,128)S(1)}, u32[]{:S(2)}, u32[]{:S(2)}) %collective-permute-start.1) | collective-permute-done | bytes 16416 | tf_op jit(solution)/shard_map/ppermute | solution.py:576
  9.3 0.0 collective-permute-start.7
  9.3 0.5 %collective-permute-start.5 = (f32[32,128]{1,0:T(8,128)S(1)}, f32[32,128]{1,0:T(8,128)S(1)}, u32[]{:S(2)}, u32[]{:S(2)}) collective-permute-start(f32[32,128]{1,0:T(8,128)S(1)} %collective-permute-done.refs_0_), channel_id=1, source_target_pairs={{0,4},{4,0},{1,5},{5,1},{2,6},{6,2},{3,7},{7,3},{8,12},{12,8},{9,1... | collective-permute-start | bytes 49160 | tf_op jit(solution)/shard_map/ppermute | solution.py:563
  9.8 0.0 collective-permute-start.6
  9.8 0.9 %collective-permute-done.5.refs_1_ = f32[32,128]{1,0:T(8,128)S(1)} collective-permute-done((f32[32,128]{1,0:T(8,128)S(1)}, f32[32,128]{1,0:T(8,128)S(1)}, u32[]{:S(2)}, u32[]{:S(2)}) %collective-permute-start.5) | collective-permute-done | bytes 16416 | tf_op jit(solution)/shard_map/ppermute | solution.py:563
  10.6 0.3 %collective-permute-done.6.refs_3_ = f32[32,128]{1,0:T(8,128)S(1)} collective-permute-done((f32[32,128]{1,0:T(8,128)S(1)}, f32[32,128]{1,0:T(8,128)S(1)}, u32[]{:S(2)}, u32[]{:S(2)}) %collective-permute-start.6) | collective-permute-done | bytes 16416 | tf_op jit(solution)/shard_map/ppermute | solution.py:563
  11.0 0.0 collective-permute-done.7.refs_6_
  11.0 2.0 %border.1 = f32[1,2,32,1024]{3,2,1,0:T(8,128)} custom-call(f32[32,128]{1,0:T(8,128)S(1)} %collective-permute-done.refs_0_, f32[32,128]{1,0:T(8,128)S(1)} %collective-permute-done.5.refs_1_, f32[32,128]{1,0:T(8,128)S(1)} %collective-permute-done.1.refs_2_, f32[32,128]{1,0:T(8,128)S(1)} %collective-permute-done.6.refs_3_, ...), custom_call_target="tpu_custom_call" | custom-call | tf_op jit(solution)/shard_map/border/pallas_call | solution.py:595
  (1 shorter events, 0.0 us)
Async XLA Ops:
  0.0 6.1 %copy-start = (f32[2,32,1024]{2,1,0:T(8,128)S(1)}, f32[2,32,1024]{2,1,0:T(8,128)}, u32[]{:S(2)}) copy-start(f32[2,32,1024]{2,1,0:T(8,128)} %refs_0_.1) | copy-start | bytes 786436
  0.0 6.1 %copy-start.1 = (f32[32,1024]{1,0:T(8,128)S(1)}, f32[32,1024]{1,0:T(8,128)}, u32[]{:S(2)}) copy-start(f32[32,1024]{1,0:T(8,128)} %refs_2_.1) | copy-start | bytes 393220
  0.0 6.2 %copy-start.2 = (f32[32,1024]{1,0:T(8,128)S(1)}, f32[32,1024]{1,0:T(8,128)}, u32[]{:S(2)}) copy-start(f32[32,1024]{1,0:T(8,128)} %refs_4_.1) | copy-start | bytes 393220
  0.0 6.1 %collective-permute-start.2 = (f32[2,32,1024]{2,1,0:T(8,128)}, f32[2,32,1024]{2,1,0:T(8,128)S(1)}, u32[]{:S(2)}, u32[]{:S(2)}) collective-permute-start(f32[2,32,1024]{2,1,0:T(8,128)} %refs_0_.1), channel_id=1, source_target_pairs={{0,4},{4,0},{1,5},{5,1},{2,6},{6,2},{3,7},{7,3},{8,12},{12,8},{9,1... | collective-permute-start | bytes 786440 | tf_op jit(solution)/shard_map/ppermute | solution.py:563
  0.5 5.6 %collective-permute-start.3 = (f32[32,1024]{1,0:T(8,128)}, f32[32,1024]{1,0:T(8,128)S(1)}, u32[]{:S(2)}, u32[]{:S(2)}) collective-permute-start(f32[32,1024]{1,0:T(8,128)} %refs_2_.1), channel_id=1, source_target_pairs={{0,4},{4,0},{1,5},{5,1},{2,6},{6,2},{3,7},{7,3},{8,12},{12,8},{9,1... | collective-permute-start | bytes 393224 | tf_op jit(solution)/shard_map/ppermute | solution.py:563
  0.6 5.5 %collective-permute-start.4 = (f32[32,1024]{1,0:T(8,128)}, f32[32,1024]{1,0:T(8,128)S(1)}, u32[]{:S(2)}, u32[]{:S(2)}) collective-permute-start(f32[32,1024]{1,0:T(8,128)} %refs_4_.1), channel_id=1, source_target_pairs={{0,4},{4,0},{1,5},{5,1},{2,6},{6,2},{3,7},{7,3},{8,12},{12,8},{9,1... | collective-permute-start | bytes 393224 | tf_op jit(solution)/shard_map/ppermute | solution.py:563
  2.0 6.4 %collective-permute-start = (f32[32,128]{1,0:T(8,128)S(1)}, f32[32,128]{1,0:T(8,128)S(1)}, u32[]{:S(2)}, u32[]{:S(2)}) collective-permute-start(f32[32,128]{1,0:T(8,128)S(1)} %get-tuple-element.15), channel_id=1, source_target_pairs={{0,1},{1,0},{2,3},{3,2},{4,5},{5,4},{6,7},{7,6},{8,9},{9,8},{10,11... | collective-permute-start | bytes 49160 | tf_op jit(solution)/shard_map/ppermute | solution.py:577
  4.6 4.6 %collective-permute-start.1 = (f32[32,128]{1,0:T(8,128)S(1)}, f32[32,128]{1,0:T(8,128)S(1)}, u32[]{:S(2)}, u32[]{:S(2)}) collective-permute-start(f32[32,128]{1,0:T(8,128)S(1)} %get-tuple-element.16), channel_id=1, source_target_pairs={{1,2},{2,1},{3,0},{0,3},{5,6},{6,5},{7,4},{4,7},{9,10},{10,9},{11,... | collective-permute-start | bytes 49160 | tf_op jit(solution)/shard_map/ppermute | solution.py:576
  9.3 1.7 %collective-permute-start.7 = (f32[2,32,512]{2,1,0:T(8,128)S(1)}, f32[2,32,512]{2,1,0:T(8,128)S(1)}, u32[]{:S(2)}, u32[]{:S(2)}) collective-permute-start(f32[2,32,512]{2,1,0:T(8,128)S(1)} %get-tuple-element.24), channel_id=1, source_target_pairs={{0,4},{4,0},{1,5},{5,1},{2,6},{6,2},{3,7},{7,3},{8,12},{12,8},{9,1... | collective-permute-start | bytes 393224 | tf_op jit(solution)/shard_map/ppermute | solution.py:592
  9.3 1.4 %collective-permute-start.5 = (f32[32,128]{1,0:T(8,128)S(1)}, f32[32,128]{1,0:T(8,128)S(1)}, u32[]{:S(2)}, u32[]{:S(2)}) collective-permute-start(f32[32,128]{1,0:T(8,128)S(1)} %collective-permute-done.refs_0_), channel_id=1, source_target_pairs={{0,4},{4,0},{1,5},{5,1},{2,6},{6,2},{3,7},{7,3},{8,12},{12,8},{9,1... | collective-permute-start | bytes 49160 | tf_op jit(solution)/shard_map/ppermute | solution.py:563
  9.8 1.2 %collective-permute-start.6 = (f32[32,128]{1,0:T(8,128)S(1)}, f32[32,128]{1,0:T(8,128)S(1)}, u32[]{:S(2)}, u32[]{:S(2)}) collective-permute-start(f32[32,128]{1,0:T(8,128)S(1)} %collective-permute-done.1.refs_2_), channel_id=1, source_target_pairs={{0,4},{4,0},{1,5},{5,1},{2,6},{6,2},{3,7},{7,3},{8,12},{12,8},{9,1... | collective-permute-start | bytes 49160 | tf_op jit(solution)/shard_map/ppermute | solution.py:563

commit v4 on v3

--- a/solution.py
+++ b/solution.py
@@ -423,12 +423,15 @@
 def source_list(refs, rows, parts):
     if parts == 2:
         mine = own_first(rows)
-        return [(refs[0::2], mine), (refs[1::2], pl.multiple_of(rows - mine, rows))]
-    return [(tuple(ref.at[g] for ref in refs), g * rows) for g in range(parts)]
+        state, feed, kill = refs[4:]
+        other = [state.at[0], state.at[1], feed, kill]
+        return [(refs[:4], mine), (other, pl.multiple_of(rows - mine, rows))]
+    state, feed, kill = refs
+    return [([state.at[g, 0], state.at[g, 1], feed.at[g], kill.at[g]], g * rows) for g in range(parts)]
 
 
 def interior_kernel(parts, rows, columns, halo, depth, width, *refs):
-    count, outs = (6, 3) if parts == 2 else (3, 2)
+    count, outs = (7, 3) if parts == 2 else (3, 2)
     ins, window, keep, give = refs[:count], refs[count], refs[count + 1], refs[count + 2]
     work = refs[count + outs :]
     here = columns // 2 if parts == 2 else columns
@@ -437,18 +440,14 @@
     seam = 4 * depth if parts == 2 else 0
     side = (width - seam) // 2 - halo
 
-    def reader(state, feed, kill):
-        def read(plane, block):
-            lane = pl.ds(origin + 256 * block, 256)
-            return state[plane, :, lane] if plane < 2 else (feed, kill)[plane - 2][:, lane]
-
-        return read
+    def reader(planes):
+        return lambda plane, block: planes[plane][:, pl.ds(origin + 256 * block, 256)]
 
     sources = []
-    for (state, feed, kill), first in source_list(ins, rows, parts):
-        sources.append((reader(state, feed, kill), first))
+    for planes, first in source_list(ins, rows, parts):
+        sources.append((reader(planes), first))
         for plane in range(4):
-            value = state[plane] if plane < 2 else (feed, kill)[plane - 2][...]
+            value = planes[plane][...]
             cuts = [value[:, :halo], value[:, :side], value[:, (columns - seam) // 2 : (columns + seam) // 2]]
             cuts += [value[:, columns - side :], value[:, columns - halo :]]
             window[plane, pl.ds(first, rows), :] = jnp.concatenate([cut for cut in cuts if cut.shape[1]], axis=1)
@@ -464,12 +463,8 @@
                 target[s, :, pl.ds(256 * k, 256)] = block
 
 
-def border_kernel(parts, rows, halo, depth, width, *refs):
-    count, inners = (4, 2) if parts == 2 else (2, 1)
-    strips, window, inner = refs[:count], refs[count], refs[count + 1 : count + 1 + inners]
-    out, work = refs[count + 1 + inners], refs[count + 2 + inners :]
+def border_kernel(parts, rows, halo, depth, width, window, from_a, from_b, out, *work):
     lanes = width // 2
-    seam = 4 * depth if parts == 2 else 0
     index, size = lax.axis_index("gy"), lax.axis_size("gy")
     even = lax.rem(index, 2) == 0
     tiles = lanes // 128
@@ -478,10 +473,10 @@
     outside = ((at < halo // 2) & (index == 0)) | ((at >= lanes - halo // 2) & (index == size - 1))
     level = Level(work[:-1], parts * rows // 2, lanes, jnp.where(outside, 0.0, 1.0))
 
-    def reader(from_a, from_b, first):
+    def reader(first):
         def read(plane, block):
             part = slice(halo * plane, halo * plane + halo)
-            a, b = from_a[:, part], from_b[:, part]
+            a, b = from_a[pl.ds(first, rows), :][:, part], from_b[pl.ds(first, rows), :][:, part]
             low, high = jnp.where(even, b, a), jnp.where(even, a, b)
             low, high = jnp.where(index == 0, 0.0, low), jnp.where(index == size - 1, 0.0, high)
             own = window[plane, pl.ds(first, rows), :]
@@ -490,23 +485,29 @@
 
         return read
 
-    sources = [(reader(a, b, first), first) for (a, b), first in source_list(strips, rows, parts)]
-    load_planes(level, sources, width, work[-1])
-    total = out.shape[-1]
-    share = total // inners
-    for k, value in enumerate(inner):
-        origin = lax.axis_index("gx") * share
-        origin = 0 if inners == 1 else pl.multiple_of(origin if k == 0 else share - origin, share)
-        out[0, :, :, pl.ds(origin, share)] = value[...]
+    load_planes(level, [(reader(g * rows), g * rows) for g in range(parts)], width, work[-1])
     level.run(lax.axis_index("ta"))
     spread(level, work[-1])
     natural = merged(level, own_first(rows), rows, work[-1])
+    for s in range(2):
+        for k, block in enumerate(natural[s]):
+            out[s, :, pl.ds(256 * k, 256)] = block
+
+
+def final_kernel(halo, depth, width, *refs):
+    inner, border, out = refs[:-2], refs[-2], refs[-1]
+    total = out.shape[-1]
+    share = total // len(inner)
+    for k, value in enumerate(inner):
+        origin = lax.axis_index("gx") * share
+        origin = 0 if len(inner) == 1 else pl.multiple_of(origin if k == 0 else share - origin, share)
+        out[0, :, :, pl.ds(origin, share)] = value[...]
     pieces = [(0, halo, depth), (total - depth, width - halo - depth, depth)]
-    if seam:
+    if len(inner) > 1:
         pieces.append((total // 2 - depth, width // 2 - depth, depth))
         pieces.append((total // 2, width // 2, depth))
     for s in range(2):
-        whole = jnp.concatenate(natural[s], axis=1) if len(natural[s]) > 1 else natural[s][0]
+        whole = border[s]
         for column, source, size in pieces:
             low = column // 128 * 128
             high = round_up(column + size, 128)
@@ -515,22 +516,26 @@
             out[0, s, :, pl.ds(low, high - low)] = jnp.concatenate([x for x in parts_of if x.shape[1]], axis=1)
 
 
-def pack_kernel(halo, state, feed, kill, to_a, to_b, left, right, sems):
-    width, total = left.shape[-1], feed.shape[1]
-    copies = []
-    for side, (target, lane) in enumerate(((left, pl.ds(0, width)), (right, pl.ds(total - width, width)))):
-        copies.append(pltpu.make_async_copy(state.at[:, :, lane], target.at[pl.ds(0, 2)], sems.at[side, 0]))
-        copies.append(pltpu.make_async_copy(feed.at[:, lane], target.at[2], sems.at[side, 1]))
-        copies.append(pltpu.make_async_copy(kill.at[:, lane], target.at[3], sems.at[side, 2]))
+def pack_kernel(parts, rows, halo, *refs):
+    ins, to_a, to_b = refs[:-2], refs[-2], refs[-1]
+    even = lax.rem(lax.axis_index("gy"), 2) == 0
+    for planes, first in source_list(ins, rows, parts):
+        total = planes[0].shape[-1]
+        tile = round_up(halo, 128)
+        low = jnp.concatenate([ref[:, pl.ds(0, tile)][:, :halo] for ref in planes], axis=1)
+        high = jnp.concatenate([ref[:, pl.ds(total - tile, tile)][:, tile - halo :] for ref in planes], axis=1)
+        to_a[pl.ds(first, rows), :] = jnp.where(even, high, low)
+        to_b[pl.ds(first, rows), :] = jnp.where(even, low, high)
+
+
+def fetch_kernel(state, feed, kill, *refs):
+    planes, sems = refs[:4], refs[4]
+    sources = (state.at[0], state.at[1], feed, kill)
+    copies = [pltpu.make_async_copy(sources[i], planes[i], sems.at[i]) for i in range(4)]
     for copy in copies:
         copy.start()
     for copy in copies:
         copy.wait()
-    low = jnp.concatenate([left[plane, :, :halo] for plane in range(4)], axis=1)
-    high = jnp.concatenate([right[plane, :, width - halo :] for plane in range(4)], axis=1)
-    even = lax.rem(lax.axis_index("gy"), 2) == 0
-    to_a[...] = jnp.where(even, high, low)
-    to_b[...] = jnp.where(even, low, high)
 
 
 def both_ways(pairs):
@@ -563,16 +568,27 @@
             return [value, lax.ppermute(value, "gx", [(0, 1), (1, 0)])]
         return [lax.all_gather(value, "gx")]
 
+    given = (initial_state, feed_rate, kill_rate)
+    fields = [value for field in given for value in across(field)]
+    if parts == 2:
+        own = pl.pallas_call(
+            fetch_kernel,
+            out_shape=[jax.ShapeDtypeStruct((rows, columns), F32)] * 4,
+            in_specs=[ANY] * 3,
+            out_specs=[VMEM] * 4,
+            scratch_shapes=[pltpu.SemaphoreType.DMA((4,))],
+            compiler_params=pltpu.CompilerParams(vmem_limit_bytes=1709 * 2**15),
+            name="fetch",
+        )(*given)
+        fields = [*own, *fields[1::2]]
     to_a, to_b = pl.pallas_call(
-        functools.partial(pack_kernel, halo),
-        out_shape=[jax.ShapeDtypeStruct((rows, 4 * halo), F32)] * 2,
-        in_specs=[ANY] * 3,
+        functools.partial(pack_kernel, parts, rows, halo),
+        out_shape=[jax.ShapeDtypeStruct((every, 4 * halo), F32)] * 2,
+        in_specs=[VMEM] * len(fields),
         out_specs=[VMEM] * 2,
-        scratch_shapes=[pltpu.VMEM((4, rows, strip), F32)] * 2 + [pltpu.SemaphoreType.DMA((2, 3))],
-        compiler_params=pltpu.CompilerParams(vmem_limit_bytes=54 * 2**20 - 2**17),
+        compiler_params=pltpu.CompilerParams(vmem_limit_bytes=32 * every * columns + 2**22),
         name="pack",
-    )(initial_state, feed_rate, kill_rate)
-    fields = [value for field in (initial_state, feed_rate, kill_rate) for value in across(field)]
+    )(*fields)
     from_b = lax.ppermute(to_b, "gy", both_ways([(i, (i + 1) % blocks) for i in range(1, blocks - blocks % 2, 2)]))
     from_a = lax.ppermute(to_a, "gy", both_ways([(i, i + 1) for i in range(0, blocks - 1, 2)]))
     work, size = work_of(every // 2, here // 2)
@@ -590,17 +606,25 @@
     from_a, from_b, window, *inner = lax.optimization_barrier((from_a, from_b, window, *inner))
     if parts == 2:
         inner[1] = lax.ppermute(inner[1], "gx", [(0, 1), (1, 0)])
-    strips = [value for strip in (from_a, from_b) for value in across(strip)]
     work, size = work_of(every // 2, width // 2)
-    return pl.pallas_call(
+    border = pl.pallas_call(
         functools.partial(border_kernel, parts, rows, halo, depth, width),
-        out_shape=jax.ShapeDtypeStruct((1, 2, rows, columns), F32),
-        in_specs=[VMEM] * (len(strips) + 1 + len(inner)),
+        out_shape=jax.ShapeDtypeStruct((2, rows, width), F32),
+        in_specs=[VMEM] * 3,
         out_specs=VMEM,
         scratch_shapes=work,
-        compiler_params=pltpu.CompilerParams(vmem_limit_bytes=size + 32 * rows * columns + 2**23),
+        compiler_params=pltpu.CompilerParams(vmem_limit_bytes=size + 32 * every * width + 2**23),
+        cost_estimate=pl.CostEstimate(flops=10 * 2**20, bytes_accessed=10 * 2**20, transcendentals=0),
         name="border",
-    )(*strips, window, *inner)
+    )(window, from_a, from_b)
+    return pl.pallas_call(
+        functools.partial(final_kernel, halo, depth, width),
+        out_shape=jax.ShapeDtypeStruct((1, 2, rows, columns), F32),
+        in_specs=[VMEM] * (len(inner) + 1),
+        out_specs=VMEM,
+        compiler_params=pltpu.CompilerParams(vmem_limit_bytes=64 * rows * columns + 2**22),
+        name="final",
+    )(*inner, border)
 
 
 def solution(mesh):

time: 13.2 us -> 12.3 us (0.932); the launches traced: 13 us -> 12.2 us
  waiting for transfers between devices: 2.08 us -> 1.35 us
  starting transfers between devices: 5.66 us -> 5.38 us
  Pallas kernels: 5.16 us -> 5.43 us
    ppermute x5 -> x3, waiting for transfers between devices: 1.19 us -> 0.1 us  [across(): return [value, lax.ppermute(value, 'gx', [(0, 1), (1, 0)])]]
    pallas_call x1 -> x3, Pallas kernels: 0.95 us -> 2.03 us  [the longest x1 1.13 us: per_device(): pl.pallas_call(fetch_kernel, out_shape=[jax.ShapeDtypeStruct((rows, colum...]
    pallas_call x1, Pallas kernels: 2.01 us -> 1.19 us  [per_device(): pl.pallas_call(functools.partial(border_kernel, parts, rows, halo, depth,...]
    ppermute x5 -> x3, starting transfers between devices: 1.54 us -> 0.96 us  [across(): return [value, lax.ppermute(value, 'gx', [(0, 1), (1, 0)])]]
    ppermute x1, starting transfers between devices: 2.63 us -> 2.92 us  [per_device(): lax.ppermute(to_a, 'gy', both_ways([(i, i + 1) for i in range(0, blocks -...]
    ppermute x1, waiting for transfers between devices: 0.88 us -> 1.09 us  [per_device(): lax.ppermute(to_b, 'gy', both_ways([(i, (i + 1) % blocks) for i in range(...]
    ppermute x1, waiting for transfers between devices: 0.01 us -> 0.15 us  [per_device(): inner[1] = lax.ppermute(inner[1], 'gx', [(0, 1), (1, 0)])]
  transfers between devices with their start and end apart: 8 -> 6, of which waited for: 3 -> 3; matrix products, arithmetic and copies ran while one was open for 0% -> 0% of each run, Pallas kernels for 24% -> 37%
where the time goes in v4:
time: 12.3 us; the launch traced here: 12.2 us
  Pallas kernels  5.43 us (44%)
  starting transfers between devices  5.38 us (44%)
  waiting for transfers between devices  1.35 us (11%)
    ppermute x1, starting transfers between devices, per_device(): lax.ppermute(to_a, 'gy', both_ways([(i, i + 1) for i in range(0, blocks -...  2.92 us
    pallas_call x1, Pallas kernels, per_device(): pl.pallas_call(functools.partial(interior_kernel, parts, rows, columns, h...  2.21 us
    ppermute x1, starting transfers between devices, per_device(): lax.ppermute(to_b, 'gy', both_ways([(i, (i + 1) % blocks) for i in range(...  1.49 us
    pallas_call x1, Pallas kernels, per_device(): pl.pallas_call(functools.partial(border_kernel, parts, rows, halo, depth,...  1.19 us
    pallas_call x1, Pallas kernels, per_device(): pl.pallas_call(fetch_kernel, out_shape=[jax.ShapeDtypeStruct((rows, colum...  1.13 us
    ppermute x1, waiting for transfers between devices, per_device(): lax.ppermute(to_b, 'gy', both_ways([(i, (i + 1) % blocks) for i in range(...  1.09 us
    ppermute x3, starting transfers between devices, across(): return [value, lax.ppermute(value, 'gx', [(0, 1), (1, 0)])]  0.96 us
    pallas_call x1, Pallas kernels, per_device(): pl.pallas_call(functools.partial(final_kernel, halo, depth, width), out_s...  0.79 us
  transfers between devices with their start and end apart: 6, of which 3 were waited for; matrix products, arithmetic and copies ran while one was open for 0% of the time, Pallas kernels for 37%

profile of v4, /device:TPU:0, one launch (start us, length us, event | category | flops | bytes accessed | tf_op | source)
XLA Modules:
  0.0 12.2 jit_solution(3911972041022085755)
XLA Ops:
  0.0 0.5 %collective-permute-start = (f32[2,32,1024]{2,1,0:T(8,128)}, f32[2,32,1024]{2,1,0:T(8,128)S(1)}, u32[]{:S(2)}, u32[]{:S(2)}) collective-permute-start(f32[2,32,1024]{2,1,0:T(8,128)} %state.1), channel_id=1, source_target_pairs={{0,4},{4,0},{1,5},{5,1},{2,6},{6,2},{3,7},{7,3},{8,12},{12,8},{9,1... | collective-permute-start | bytes 786440 | tf_op jit(solution)/shard_map/ppermute | solution.py:568
  0.5 0.1 collective-permute-start.1
  0.5 0.5 %collective-permute-start.2 = (f32[32,1024]{1,0:T(8,128)}, f32[32,1024]{1,0:T(8,128)S(1)}, u32[]{:S(2)}, u32[]{:S(2)}) collective-permute-start(f32[32,1024]{1,0:T(8,128)} %kill.1), channel_id=1, source_target_pairs={{0,4},{4,0},{1,5},{5,1},{2,6},{6,2},{3,7},{7,3},{8,12},{12,8},{9,1... | collective-permute-start | bytes 393224 | tf_op jit(solution)/shard_map/ppermute | solution.py:568
  1.0 1.1 %fetch.1 = (f32[32,1024]{1,0:T(8,128)S(1)}, f32[32,1024]{1,0:T(8,128)S(1)}, f32[32,1024]{1,0:T(8,128)S(1)}, f32[32,1024]{1,0:T(8,128)S(1)}) custom-call(f32[2,32,1024]{2,1,0:T(8,128)} %state.1, f32[32,1024]{1,0:T(8,128)} %feed.1, f32[32,1024]{1,0:T(8,128)} %kill.1), custom_call_target="tpu_custom_call" | custom-call | tf_op jit(solution)/shard_map/fetch/pallas_call | solution.py:574
  2.1 0.0 collective-permute-done.1.refs_5_
  2.1 0.1 collective-permute-done.2.refs_6_
  2.2 0.0 collective-permute-done.refs_4_
  2.2 0.1 pack.1
  2.3 2.9 %collective-permute-start.3 = (f32[64,128]{1,0:T(8,128)S(1)}, f32[64,128]{1,0:T(8,128)S(1)}, u32[]{:S(2)}, u32[]{:S(2)}) collective-permute-start(f32[64,128]{1,0:T(8,128)S(1)} %get-tuple-element.23), channel_id=1, source_target_pairs={{0,1},{1,0},{2,3},{3,2},{4,5},{5,4},{6,7},{7,6},{8,9},{9,8},{10,11... | collective-permute-start | bytes 98312 | tf_op jit(solution)/shard_map/ppermute | solution.py:593
  5.3 1.5 %collective-permute-start.4 = (f32[64,128]{1,0:T(8,128)S(1)}, f32[64,128]{1,0:T(8,128)S(1)}, u32[]{:S(2)}, u32[]{:S(2)}) collective-permute-start(f32[64,128]{1,0:T(8,128)S(1)} %get-tuple-element.24), channel_id=1, source_target_pairs={{1,2},{2,1},{3,0},{0,3},{5,6},{6,5},{7,4},{4,7},{9,10},{10,9},{11,... | collective-permute-start | bytes 98312 | tf_op jit(solution)/shard_map/ppermute | solution.py:592
  6.7 2.2 %interior.1 = (f32[4,64,256]{2,1,0:T(8,128)S(1)}, f32[2,32,512]{2,1,0:T(8,128)S(1)}, f32[2,32,512]{2,1,0:T(8,128)S(1)}) custom-call(f32[32,1024]{1,0:T(8,128)S(1)} %get-tuple-element.19.refs_0_, f32[32,1024]{1,0:T(8,128)S(1)} %get-tuple-element.20.refs_1_, f32[32,1024]{1,0:T(8,128)S(1)} %get-tuple-element.21.refs_2_, ...), custom_call_target="tpu_custom_call" | custom-call | flops 41943040 | bytes 20971520 | tf_op jit(solution)/shard_map/interior/pallas_call | solution.py:595
  9.0 0.0 collective-permute-done.3.from_a
  9.0 1.1 %collective-permute-done.4.from_b = f32[64,128]{1,0:T(8,128)S(1)} collective-permute-done((f32[64,128]{1,0:T(8,128)S(1)}, f32[64,128]{1,0:T(8,128)S(1)}, u32[]{:S(2)}, u32[]{:S(2)}) %collective-permute-start.4) | collective-permute-done | bytes 32800 | tf_op jit(solution)/shard_map/ppermute | solution.py:592
  10.1 0.0 collective-permute-start.5
  10.1 1.2 %border.1.refs_2_ = f32[2,32,256]{2,1,0:T(8,128)S(1)} custom-call(f32[4,64,256]{2,1,0:T(8,128)S(1)} %get-tuple-element.30.window, f32[64,128]{1,0:T(8,128)S(1)} %collective-permute-done.3.from_a, f32[64,128]{1,0:T(8,128)S(1)} %collective-permute-done.4.from_b), custom_call_target="tpu_custom_call" | custom-call | flops 10485760 | bytes 10485760 | tf_op jit(solution)/shard_map/border/pallas_call | solution.py:610
  11.3 0.2 %collective-permute-done.5.refs_1_ = f32[2,32,512]{2,1,0:T(8,128)S(1)} collective-permute-done((f32[2,32,512]{2,1,0:T(8,128)S(1)}, f32[2,32,512]{2,1,0:T(8,128)S(1)}, u32[]{:S(2)}, u32[]{:S(2)}) %collective-permute-start.5) | collective-permute-done | bytes 131104 | tf_op jit(solution)/shard_map/ppermute | solution.py:608
  11.4 0.8 %final.1 = f32[1,2,32,1024]{3,2,1,0:T(8,128)} custom-call(f32[2,32,512]{2,1,0:T(8,128)S(1)} %get-tuple-element.28.refs_0_, f32[2,32,512]{2,1,0:T(8,128)S(1)} %collective-permute-done.5.refs_1_, f32[2,32,256]{2,1,0:T(8,128)S(1)} %border.1.refs_2_), custom_call_target="tpu_custom_call" | custom-call | tf_op jit(solution)/shard_map/final/pallas_call | solution.py:620
Async XLA Ops:
  0.0 2.2 %collective-permute-start = (f32[2,32,1024]{2,1,0:T(8,128)}, f32[2,32,1024]{2,1,0:T(8,128)S(1)}, u32[]{:S(2)}, u32[]{:S(2)}) collective-permute-start(f32[2,32,1024]{2,1,0:T(8,128)} %state.1), channel_id=1, source_target_pairs={{0,4},{4,0},{1,5},{5,1},{2,6},{6,2},{3,7},{7,3},{8,12},{12,8},{9,1... | collective-permute-start | bytes 786440 | tf_op jit(solution)/shard_map/ppermute | solution.py:568
  0.5 1.6 %collective-permute-start.1 = (f32[32,1024]{1,0:T(8,128)}, f32[32,1024]{1,0:T(8,128)S(1)}, u32[]{:S(2)}, u32[]{:S(2)}) collective-permute-start(f32[32,1024]{1,0:T(8,128)} %feed.1), channel_id=1, source_target_pairs={{0,4},{4,0},{1,5},{5,1},{2,6},{6,2},{3,7},{7,3},{8,12},{12,8},{9,1... | collective-permute-start | bytes 393224 | tf_op jit(solution)/shard_map/ppermute | solution.py:568
  0.5 1.7 %collective-permute-start.2 = (f32[32,1024]{1,0:T(8,128)}, f32[32,1024]{1,0:T(8,128)S(1)}, u32[]{:S(2)}, u32[]{:S(2)}) collective-permute-start(f32[32,1024]{1,0:T(8,128)} %kill.1), channel_id=1, source_target_pairs={{0,4},{4,0},{1,5},{5,1},{2,6},{6,2},{3,7},{7,3},{8,12},{12,8},{9,1... | collective-permute-start | bytes 393224 | tf_op jit(solution)/shard_map/ppermute | solution.py:568
  2.3 6.6 %collective-permute-start.3 = (f32[64,128]{1,0:T(8,128)S(1)}, f32[64,128]{1,0:T(8,128)S(1)}, u32[]{:S(2)}, u32[]{:S(2)}) collective-permute-start(f32[64,128]{1,0:T(8,128)S(1)} %get-tuple-element.23), channel_id=1, source_target_pairs={{0,1},{1,0},{2,3},{3,2},{4,5},{5,4},{6,7},{7,6},{8,9},{9,8},{10,11... | collective-permute-start | bytes 98312 | tf_op jit(solution)/shard_map/ppermute | solution.py:593
  5.3 4.8 %collective-permute-start.4 = (f32[64,128]{1,0:T(8,128)S(1)}, f32[64,128]{1,0:T(8,128)S(1)}, u32[]{:S(2)}, u32[]{:S(2)}) collective-permute-start(f32[64,128]{1,0:T(8,128)S(1)} %get-tuple-element.24), channel_id=1, source_target_pairs={{1,2},{2,1},{3,0},{0,3},{5,6},{6,5},{7,4},{4,7},{9,10},{10,9},{11,... | collective-permute-start | bytes 98312 | tf_op jit(solution)/shard_map/ppermute | solution.py:592
  10.1 1.3 %collective-permute-start.5 = (f32[2,32,512]{2,1,0:T(8,128)S(1)}, f32[2,32,512]{2,1,0:T(8,128)S(1)}, u32[]{:S(2)}, u32[]{:S(2)}) collective-permute-start(f32[2,32,512]{2,1,0:T(8,128)S(1)} %get-tuple-element.29), channel_id=1, source_target_pairs={{0,4},{4,0},{1,5},{5,1},{2,6},{6,2},{3,7},{7,3},{8,12},{12,8},{9,1... | collective-permute-start | bytes 393224 | tf_op jit(solution)/shard_map/ppermute | solution.py:608

commit v5 on v4

--- a/solution.py
+++ b/solution.py
@@ -73,24 +73,35 @@
 COARSE_PLAIN = 18
 
 
-def scratch(rows, lanes):
+def state_shapes(rows, lanes):
     guarded = rows + 2 * GUARD
     return [
-        pltpu.VMEM((4 * 8, guarded, lanes), F32),
-        pltpu.VMEM((3 * 8, rows, lanes), F32),
-        pltpu.VMEM((8, rows, lanes), F32),
-        pltpu.VMEM((8, rows, lanes), F32),
-        pltpu.VMEM((COARSE_STENCIL, guarded, lanes), F32),
-        pltpu.VMEM((COARSE_PLAIN, rows, lanes), F32),
-        pltpu.VMEM((2, rows, lanes), F32),
-        pltpu.VMEM((8, rows, lanes), F32),
-        pltpu.VMEM((24, rows, lanes), F32),
+        (24, guarded, lanes),
+        (24, rows, lanes),
+        (8, rows, lanes),
+        (COARSE_STENCIL, guarded, lanes),
+        (COARSE_PLAIN, rows, lanes),
+        (2, rows, lanes),
+        (8, rows, lanes),
     ]
+
+
+def late_shapes(rows, lanes):
+    return [
+        (8, rows + 2 * GUARD, lanes),
+        (8, rows, lanes),
+        (24, rows, lanes),
+    ]
+
+
+def natural_shape(rows, lanes):
+    return (4, 2 * lanes // 128, 2 * rows, 128)
 
 
 class Level:
     def __init__(self, refs, rows, lanes, mask):
-        (self.fine, self.lin, self.coef, self.rest, self.cs, self.cp, self.cc, self.mom, self.tl) = refs
+        self.fine, self.lin, self.coef, self.cs, self.cp, self.cc, self.mom, *late = refs
+        self.fresh, self.rest, self.tl = late or (None, None, None)
         self.rows, self.lanes, self.mask = rows, lanes, mask
         self.chunks = rows // 8
 
@@ -143,14 +154,15 @@
         ref[plane, pl.ds(row, 8), :] = value
 
     def fine_rates(self, base, row):
-        state = [[self.at(self.fine, base * 8 + s * 4 + p, row) for p in range(4)] for s in range(2)]
+        ref, base = (self.fresh, 0) if base == 3 else (self.fine, base)
+        state = [[self.at(ref, base * 8 + s * 4 + p, row) for p in range(4)] for s in range(2)]
         linear, rates = [], []
         for p, (a, b) in enumerate(PHASES):
             laps = []
             for s in range(2):
                 across = state[s][2 * a + 1 - b]
                 along = state[s][2 * (1 - a) + b]
-                moved = self.at(self.fine, base * 8 + s * 4 + 2 * (1 - a) + b, row, 1 if a else -1)
+                moved = self.at(ref, base * 8 + s * 4 + 2 * (1 - a) + b, row, 1 if a else -1)
                 side = self.right(across) if b else self.left(across)
                 laps.append((along + moved) + (across + side) - 4.0 * state[s][p])
             u, v = state[0][p], state[1][p]
@@ -191,7 +203,7 @@
     def block_mean(self, values):
         return 0.25 * ((values[0] + values[1]) + (values[2] + values[3]))
 
-    def run(self, own):
+    def run(self, own, start=True, finish=True):
         lv = self
         cs, cp = self.cs, self.cp
 
@@ -313,16 +325,20 @@
 
             return body
 
-        lv.each(first_sweep)
-        lv.each(second_sweep)
-        lv.each(third_sweep)
+        if start:
+            lv.each(first_sweep)
+            lv.each(second_sweep)
+            lv.each(third_sweep)
 
         def one_slice(n, carry):
             lv.each(middle_nodes)
             lv.each(end_nodes(C_D2 + 2 * lax.rem(n, 2)))
             return carry
 
-        lax.fori_loop(1, own + 1, one_slice, 0)
+        if start:
+            lax.fori_loop(1, own + 1, one_slice, 0)
+        if not finish:
+            return
 
         first = own == 0
         now = C_D2 + 2 * lax.rem(own, 2)
@@ -346,7 +362,7 @@
                     for s in range(2):
                         f0, f1, f2 = (r[s] for r in rates)
                         second = start[s] + (W0[0] * f0 + W0[1] * f1 + W0[2] * f2)
-                        lv.put(lv.fine, 24 + s * 4 + p, row, second, lane)
+                        lv.put(lv.fresh, s * 4 + p, row, second, lane)
                         lv.rest[s * 4 + p, low, lane] = second + (W1[0] * f0 + (W1[1] - HALF_STEP) * f1 + W1[2] * f2)
 
         lv.each(own_nodes)
@@ -430,43 +446,53 @@
     return [([state.at[g, 0], state.at[g, 1], feed.at[g], kill.at[g]], g * rows) for g in range(parts)]
 
 
-def interior_kernel(parts, rows, columns, halo, depth, width, *refs):
-    count, outs = (7, 3) if parts == 2 else (3, 2)
-    ins, window, keep, give = refs[:count], refs[count], refs[count + 1], refs[count + 2]
-    work = refs[count + outs :]
+def interior_kernel(parts, rows, columns, halo, depth, width, start, finish, *refs):
+    refs = list(refs)
+    take = lambda count: [refs.pop(0) for _ in range(count)]
     here = columns // 2 if parts == 2 else columns
     origin = pl.multiple_of(lax.axis_index("gx") * here, here) if parts == 2 else 0
-    level = Level(work[:-1], parts * rows // 2, here // 2, None)
     seam = 4 * depth if parts == 2 else 0
     side = (width - seam) // 2 - halo
+    ins = take(7 if parts == 2 else 3) if start else []
+    given = [] if start else take(7)
+    window = take(1)[0] if start else None
+    outs = take(2 if parts == 2 else 1) if finish else []
+    state = take(7) if start else given
+    late = take(3) if finish else []
+    (natural,) = take(1)
+    level = Level(state + late, parts * rows // 2, here // 2, None)
 
     def reader(planes):
         return lambda plane, block: planes[plane][:, pl.ds(origin + 256 * block, 256)]
 
-    sources = []
-    for planes, first in source_list(ins, rows, parts):
-        sources.append((reader(planes), first))
-        for plane in range(4):
-            value = planes[plane][...]
-            cuts = [value[:, :halo], value[:, :side], value[:, (columns - seam) // 2 : (columns + seam) // 2]]
-            cuts += [value[:, columns - side :], value[:, columns - halo :]]
-            window[plane, pl.ds(first, rows), :] = jnp.concatenate([cut for cut in cuts if cut.shape[1]], axis=1)
-    load_planes(level, sources, here, work[-1])
-    level.run(lax.axis_index("ta"))
-    spread(level, work[-1])
-    mine = own_first(rows)
-    targets = [(keep, mine), (give, pl.multiple_of(rows - mine, rows))] if parts == 2 else [(keep, mine)]
-    for target, first in targets:
-        natural = merged(level, first, rows, work[-1])
-        for s in range(2):
-            for k, block in enumerate(natural[s]):
-                target[s, :, pl.ds(256 * k, 256)] = block
-
-
-def border_kernel(parts, rows, halo, depth, width, window, from_a, from_b, out, *work):
+    if start:
+        sources = []
+        for planes, first in source_list(ins, rows, parts):
+            sources.append((reader(planes), first))
+            for plane in range(4):
+                value = planes[plane][...]
+                cuts = [value[:, :halo], value[:, :side], value[:, (columns - seam) // 2 : (columns + seam) // 2]]
+                cuts += [value[:, columns - side :], value[:, columns - halo :]]
+                window[plane, pl.ds(first, rows), :] = jnp.concatenate([cut for cut in cuts if cut.shape[1]], axis=1)
+        load_planes(level, sources, here, natural)
+    level.run(lax.axis_index("ta"), start, finish)
+    if finish:
+        spread(level, natural)
+        mine = own_first(rows)
+        firsts = [mine, pl.multiple_of(rows - mine, rows)] if parts == 2 else [mine]
+        for target, first in zip(outs, firsts):
+            blocks = merged(level, first, rows, natural)
+            for s in range(2):
+                for k, block in enumerate(blocks[s]):
+                    target[s, :, pl.ds(256 * k, 256)] = block
+
+
+def border_kernel(parts, rows, halo, depth, width, window, near, far, out, *work):
     lanes = width // 2
     index, size = lax.axis_index("gy"), lax.axis_size("gy")
-    even = lax.rem(index, 2) == 0
+    swap = lax.rem(index, 2) == 0
+    if parts == 2:
+        swap = swap == (lax.axis_index("gx") == 0)
     tiles = lanes // 128
     at = lax.broadcasted_iota(jnp.int32, (1, lanes), 1)
     at = tiles * (at % 128) + at // 128
@@ -476,8 +502,8 @@
     def reader(first):
         def read(plane, block):
             part = slice(halo * plane, halo * plane + halo)
-            a, b = from_a[pl.ds(first, rows), :][:, part], from_b[pl.ds(first, rows), :][:, part]
-            low, high = jnp.where(even, b, a), jnp.where(even, a, b)
+            a, b = near[pl.ds(first, rows), :][:, part], far[pl.ds(first, rows), :][:, part]
+            low, high = jnp.where(swap, b, a), jnp.where(swap, a, b)
             low, high = jnp.where(index == 0, 0.0, low), jnp.where(index == size - 1, 0.0, high)
             own = window[plane, pl.ds(first, rows), :]
             whole = jnp.concatenate([low, own[:, halo : width - halo], high], axis=1)
@@ -517,15 +543,18 @@
 
 
 def pack_kernel(parts, rows, halo, *refs):
-    ins, to_a, to_b = refs[:-2], refs[-2], refs[-1]
+    count = 7 if parts == 2 else 3
+    ins, outs = refs[:count], refs[count:]
     even = lax.rem(lax.axis_index("gy"), 2) == 0
+    if parts == 2:
+        even = even == (lax.axis_index("gx") == 0)
     for planes, first in source_list(ins, rows, parts):
         total = planes[0].shape[-1]
         tile = round_up(halo, 128)
         low = jnp.concatenate([ref[:, pl.ds(0, tile)][:, :halo] for ref in planes], axis=1)
         high = jnp.concatenate([ref[:, pl.ds(total - tile, tile)][:, tile - halo :] for ref in planes], axis=1)
-        to_a[pl.ds(first, rows), :] = jnp.where(even, high, low)
-        to_b[pl.ds(first, rows), :] = jnp.where(even, low, high)
+        for k, out in enumerate(outs):
+            out[pl.ds(first, rows), :] = jnp.where(even, low, high) if k else jnp.where(even, high, low)
 
 
 def fetch_kernel(state, feed, kill, *refs):
@@ -546,10 +575,29 @@
 ANY = pl.BlockSpec(memory_space=pl.ANY)
 
 
-def work_of(rows, lanes):
-    shapes = scratch(rows, lanes) + [pltpu.VMEM((4, 2 * lanes // 128, 2 * rows, 128), F32)]
-    size = sum(4 * math.prod(shape.shape) for shape in shapes)
-    return shapes, size
+def arrays(shapes):
+    return [jax.ShapeDtypeStruct(shape, F32) for shape in shapes]
+
+
+def buffers(shapes):
+    return [pltpu.VMEM(shape, F32) for shape in shapes]
+
+
+def size_of(shapes):
+    return sum(4 * math.prod(shape) for shape in shapes)
+
+
+def called(name, kernel, outs, scratch, limit, inputs, specs=VMEM, flops=0):
+    return pl.pallas_call(
+        kernel,
+        out_shape=outs,
+        in_specs=[specs] * len(inputs),
+        out_specs=[VMEM] * len(outs),
+        scratch_shapes=scratch,
+        compiler_params=pltpu.CompilerParams(vmem_limit_bytes=limit),
+        cost_estimate=pl.CostEstimate(flops=flops, bytes_accessed=flops // 2, transcendentals=0),
+        name=name,
+    )(*inputs)
 
 
 def per_device(initial_state, feed_rate, kill_rate):
@@ -559,72 +607,60 @@
     halo = round_up(depth, 32)
     seam = 4 * depth if parts == 2 else 0
     width = round_up(2 * halo + 4 * depth + seam, 256)
-    strip = round_up(halo, 128)
     every = parts * rows
     here = columns // 2 if parts == 2 else columns
-
-    def across(value):
-        if parts == 2:
-            return [value, lax.ppermute(value, "gx", [(0, 1), (1, 0)])]
-        return [lax.all_gather(value, "gx")]
-
     given = (initial_state, feed_rate, kill_rate)
-    fields = [value for field in given for value in across(field)]
+    plane_bytes = 4 * every * columns
+
+    low_pairs = both_ways([(i, i + 1) for i in range(0, blocks - 1, 2)])
+    high_pairs = both_ways([(i, (i + 1) % blocks) for i in range(1, blocks - blocks % 2, 2)])
+
+    def crossed(value):
+        return lax.ppermute(value, "gx", [(0, 1), (1, 0)])
+
     if parts == 2:
-        own = pl.pallas_call(
-            fetch_kernel,
-            out_shape=[jax.ShapeDtypeStruct((rows, columns), F32)] * 4,
-            in_specs=[ANY] * 3,
-            out_specs=[VMEM] * 4,
-            scratch_shapes=[pltpu.SemaphoreType.DMA((4,))],
-            compiler_params=pltpu.CompilerParams(vmem_limit_bytes=1709 * 2**15),
-            name="fetch",
-        )(*given)
-        fields = [*own, *fields[1::2]]
-    to_a, to_b = pl.pallas_call(
-        functools.partial(pack_kernel, parts, rows, halo),
-        out_shape=[jax.ShapeDtypeStruct((every, 4 * halo), F32)] * 2,
-        in_specs=[VMEM] * len(fields),
-        out_specs=[VMEM] * 2,
-        compiler_params=pltpu.CompilerParams(vmem_limit_bytes=32 * every * columns + 2**22),
-        name="pack",
-    )(*fields)
-    from_b = lax.ppermute(to_b, "gy", both_ways([(i, (i + 1) % blocks) for i in range(1, blocks - blocks % 2, 2)]))
-    from_a = lax.ppermute(to_a, "gy", both_ways([(i, i + 1) for i in range(0, blocks - 1, 2)]))
-    work, size = work_of(every // 2, here // 2)
-    window, *inner = pl.pallas_call(
-        functools.partial(interior_kernel, parts, rows, columns, halo, depth, width),
-        out_shape=[jax.ShapeDtypeStruct((4, every, width), F32)]
-        + [jax.ShapeDtypeStruct((2, rows, here), F32)] * (2 if parts == 2 else 1),
-        in_specs=[VMEM] * len(fields),
-        out_specs=[VMEM] * (3 if parts == 2 else 2),
-        scratch_shapes=work,
-        compiler_params=pltpu.CompilerParams(vmem_limit_bytes=size + 32 * every * (columns + width) + 2**22),
-        cost_estimate=pl.CostEstimate(flops=40 * 2**20, bytes_accessed=20 * 2**20, transcendentals=0),
-        name="interior",
-    )(*fields)
-    from_a, from_b, window, *inner = lax.optimization_barrier((from_a, from_b, window, *inner))
+        others = [crossed(value) for value in given]
+        limit = 1709 * 2**15
+        own = called("fetch", fetch_kernel, arrays([(rows, columns)] * 4), [pltpu.SemaphoreType.DMA((4,))], limit, given, ANY)
+        fields = [*own, *others]
+    else:
+        fields = [lax.all_gather(value, "gx") for value in given]
+    pack = functools.partial(pack_kernel, parts, rows, halo)
+    sent = called("pack", pack, arrays([(every, 4 * halo)] * (1 if parts == 2 else 2)), [], 8 * plane_bytes + 2**22, fields)
     if parts == 2:
-        inner[1] = lax.ppermute(inner[1], "gx", [(0, 1), (1, 0)])
-    work, size = work_of(every // 2, width // 2)
-    border = pl.pallas_call(
-        functools.partial(border_kernel, parts, rows, halo, depth, width),
-        out_shape=jax.ShapeDtypeStruct((2, rows, width), F32),
-        in_specs=[VMEM] * 3,
-        out_specs=VMEM,
-        scratch_shapes=work,
-        compiler_params=pltpu.CompilerParams(vmem_limit_bytes=size + 32 * every * width + 2**23),
-        cost_estimate=pl.CostEstimate(flops=10 * 2**20, bytes_accessed=10 * 2**20, transcendentals=0),
-        name="border",
-    )(window, from_a, from_b)
-    return pl.pallas_call(
-        functools.partial(final_kernel, halo, depth, width),
-        out_shape=jax.ShapeDtypeStruct((1, 2, rows, columns), F32),
-        in_specs=[VMEM] * (len(inner) + 1),
-        out_specs=VMEM,
-        compiler_params=pltpu.CompilerParams(vmem_limit_bytes=64 * rows * columns + 2**22),
-        name="final",
-    )(*inner, border)
+        pairs = low_pairs + [(blocks + source, blocks + target) for source, target in high_pairs]
+        near = lax.ppermute(sent[0], ("gx", "gy"), pairs)
+    else:
+        near = lax.ppermute(sent[0], "gy", low_pairs)
+        far = lax.ppermute(sent[1], "gy", high_pairs)
+
+    state, late = state_shapes(every // 2, here // 2), late_shapes(every // 2, here // 2)
+    natural = natural_shape(every // 2, here // 2)
+    limit = size_of(state + late + [natural]) + 32 * every * (columns + width) + 2**22
+    interior = functools.partial(interior_kernel, parts, rows, columns, halo, depth, width)
+    window_shape = (4, every, width)
+    result_shape = (2, rows, here)
+    if parts == 2:
+        first = functools.partial(interior, True, False)
+        made = called("interior", first, arrays([window_shape] + state), buffers([natural]), limit, fields, flops=2**24)
+        near, window, *made = lax.optimization_barrier((near, *made))
+        far = crossed(near)
+        last = functools.partial(interior, False, True)
+        keep, give = called("own", last, arrays([result_shape] * 2), buffers(late + [natural]), limit, made, flops=2**23)
+        far, give = lax.optimization_barrier((far, give))
+        inner = [keep, crossed(give)]
+    else:
+        whole = functools.partial(interior, True, True)
+        scratch = buffers(state + late + [natural])
+        window, *inner = called("interior", whole, arrays([window_shape, result_shape]), scratch, limit, fields, flops=2**24)
+    work = state_shapes(every // 2, width // 2) + late_shapes(every // 2, width // 2)
+    work.append(natural_shape(every // 2, width // 2))
+    limit = size_of(work) + 32 * every * width + 2**23
+    border = functools.partial(border_kernel, parts, rows, halo, depth, width)
+    (edges,) = called("border", border, arrays([(2, rows, width)]), buffers(work), limit, (window, near, far), flops=2**23)
+    final = functools.partial(final_kernel, halo, depth, width)
+    (out,) = called("final", final, arrays([(1, 2, rows, columns)]), [], 16 * plane_bytes + 2**22, (*inner, edges))
+    return out
 
 
 def solution(mesh):

time: 12.3 us -> 11.3 us (0.919)
  the two profiles are of different devices: /device:TPU:0 before, /device:TPU:25 now
where the time goes in v5:
time: 11.3 us; the launch traced here: 11.1 us
  Pallas kernels  6.87 us (61%)
  starting transfers between devices  3.92 us (35%)
  waiting for transfers between devices  0.25 us (2%)
    pallas_call x6, Pallas kernels, called(): pl.pallas_call(kernel, out_shape=outs, in_specs=[specs] * len(inputs), ou...  6.87 us
    ppermute x1, starting transfers between devices, per_device(): near = lax.ppermute(sent[0], ('gx', 'gy'), pairs)  2.23 us
    ppermute x5, starting transfers between devices, crossed(): return lax.ppermute(value, 'gx', [(0, 1), (1, 0)])  1.68 us
    ppermute x5, waiting for transfers between devices, crossed(): return lax.ppermute(value, 'gx', [(0, 1), (1, 0)])  0.25 us
  transfers between devices with their start and end apart: 6, of which 2 were waited for; matrix products, arithmetic and copies ran while one was open for 0% of the time, Pallas kernels for 54%

profile of v5, /device:TPU:25, one launch (start us, length us, event | category | flops | bytes accessed | tf_op | source)
XLA Modules:
  0.0 11.1 jit_solution(480683277592848426)
XLA Ops:
  0.0 0.7 %collective-permute-start = (f32[2,32,1024]{2,1,0:T(8,128)}, f32[2,32,1024]{2,1,0:T(8,128)S(1)}, u32[]{:S(2)}, u32[]{:S(2)}) collective-permute-start(f32[2,32,1024]{2,1,0:T(8,128)} %state.1), channel_id=1, source_target_pairs={{0,4},{4,0},{1,5},{5,1},{2,6},{6,2},{3,7},{7,3},{8,12},{12,8},{9,1... | collective-permute-start | bytes 786440 | tf_op jit(solution)/shard_map/ppermute | solution.py:619
  0.7 0.0 collective-permute-start.1
  0.7 0.5 %collective-permute-start.2 = (f32[32,1024]{1,0:T(8,128)}, f32[32,1024]{1,0:T(8,128)S(1)}, u32[]{:S(2)}, u32[]{:S(2)}) collective-permute-start(f32[32,1024]{1,0:T(8,128)} %kill.1), channel_id=1, source_target_pairs={{0,4},{4,0},{1,5},{5,1},{2,6},{6,2},{3,7},{7,3},{8,12},{12,8},{9,1... | collective-permute-start | bytes 393224 | tf_op jit(solution)/shard_map/ppermute | solution.py:619
  1.2 1.1 %fetch.1 = (f32[32,1024]{1,0:T(8,128)S(1)}, f32[32,1024]{1,0:T(8,128)S(1)}, f32[32,1024]{1,0:T(8,128)S(1)}, f32[32,1024]{1,0:T(8,128)S(1)}) custom-call(f32[2,32,1024]{2,1,0:T(8,128)} %state.1, f32[32,1024]{1,0:T(8,128)} %feed.1, f32[32,1024]{1,0:T(8,128)} %kill.1), custom_call_target="tpu_custom_call" | custom-call | tf_op jit(solution)/shard_map/fetch/pallas_call | solution.py:591
  2.3 0.0 collective-permute-done.1.refs_5_
  2.3 0.1 collective-permute-done.2.refs_6_
  2.4 0.0 collective-permute-done.refs_4_
  2.4 0.1 %pack.1 = f32[64,128]{1,0:T(8,128)S(1)} custom-call(f32[32,1024]{1,0:T(8,128)S(1)} %get-tuple-element.30.refs_0_, f32[32,1024]{1,0:T(8,128)S(1)} %get-tuple-element.31.refs_1_, f32[32,1024]{1,0:T(8,128)S(1)} %get-tuple-element.32.refs_2_, f32[32,1024]{1,0:T(8,128)S(1)} %get-tuple-element.33.refs_3_, f32[2,32,1024]{2,1,0:T(8,128)S(1)} %collective-permute-done.refs_4_, ...), custom_call_target="tpu_custom_call" | custom-call | tf_op jit(solution)/shard_map/pack/pallas_call | solution.py:591
  2.6 2.2 %collective-permute-start.3 = (f32[64,128]{1,0:T(8,128)S(1)}, f32[64,128]{1,0:T(8,128)S(1)}, u32[]{:S(2)}, u32[]{:S(2)}) collective-permute-start(f32[64,128]{1,0:T(8,128)S(1)} %pack.1), channel_id=1, source_target_pairs={{0,1},{1,0},{2,3},{3,2},{5,6},{6,5},{7,4},{4,7},{8,9},{9,8},{10,11... | collective-permute-start | bytes 98312 | tf_op jit(solution)/shard_map/ppermute | solution.py:632
  4.8 2.1 %interior.1 = (f32[4,64,256]{2,1,0:T(8,128)S(1)}, f32[24,48,256]{2,1,0:T(8,128)S(1)}, f32[24,32,256]{2,1,0:T(8,128)S(1)}, f32[8,32,256]{2,1,0:T(8,128)S(1)}, f32...) custom-call(f32[32,1024]{1,0:T(8,128)S(1)} %get-tuple-element.30.ref, ...), custom_call_target="tpu_custom_call" | custom-call | flops 16777216 | bytes 8388608 | tf_op jit(solution)/shard_map/interior/pallas_call | solution.py:591
  6.9 0.0 collective-permute-done.3.near
  6.9 0.2 %collective-permute-start.4 = (f32[64,128]{1,0:T(8,128)S(1)}, f32[64,128]{1,0:T(8,128)S(1)}, u32[]{:S(2)}, u32[]{:S(2)}) collective-permute-start(f32[64,128]{1,0:T(8,128)S(1)} %collective-permute-done.3.near), channel_id=1, source_target_pairs={{0,4},{4,0},{1,5},{5,1},{2,6},{6,2},{3,7},{7,3},{8,12},{12,8},{9,1... | collective-permute-start | bytes 98312 | tf_op jit(solution)/shard_map/ppermute | solution.py:619
  7.1 0.9 %own.1 = (f32[2,32,512]{2,1,0:T(8,128)S(1)}, f32[2,32,512]{2,1,0:T(8,128)S(1)}) custom-call(f32[24,48,256]{2,1,0:T(8,128)S(1)} %get-tuple-element.42.refs_0_, f32[24,32,256]{2,1,0:T(8,128)S(1)} %get-tuple-element.43.refs_1_, f32[8,32,256]{2,1,0:T(8,128)S(1)} %get-tuple-element.44.refs_2_, f32[20,48,256]{2,1,0:T(8,128)S(1)} %get-tuple-element.45.refs_3_, ...), custom_call_target="tpu_custom_call" | custom-call | flops 8388608 | bytes 4194304 | tf_op jit(solution)/shard_map/own/pallas_call | solution.py:591
  8.0 0.2 %collective-permute-done.4.far = f32[64,128]{1,0:T(8,128)S(1)} collective-permute-done((f32[64,128]{1,0:T(8,128)S(1)}, f32[64,128]{1,0:T(8,128)S(1)}, u32[]{:S(2)}, u32[]{:S(2)}) %collective-permute-start.4) | collective-permute-done | bytes 32800 | tf_op jit(solution)/shard_map/ppermute | solution.py:619
  8.2 0.3 %collective-permute-start.5 = (f32[2,32,512]{2,1,0:T(8,128)S(1)}, f32[2,32,512]{2,1,0:T(8,128)S(1)}, u32[]{:S(2)}, u32[]{:S(2)}) collective-permute-start(f32[2,32,512]{2,1,0:T(8,128)S(1)} %get-tuple-element.52), channel_id=1, source_target_pairs={{0,4},{4,0},{1,5},{5,1},{2,6},{6,2},{3,7},{7,3},{8,12},{12,8},{9,1... | collective-permute-start | bytes 393224 | tf_op jit(solution)/shard_map/ppermute | solution.py:619
  8.5 1.8 %border.1.refs_2_ = f32[2,32,256]{2,1,0:T(8,128)S(1)} custom-call(f32[4,64,256]{2,1,0:T(8,128)S(1)} %get-tuple-element.53.window, f32[64,128]{1,0:T(8,128)S(1)} %collective-permute-done.3.near, f32[64,128]{1,0:T(8,128)S(1)} %collective-permute-done.4.far), custom_call_target="tpu_custom_call" | custom-call | flops 8388608 | bytes 4194304 | tf_op jit(solution)/shard_map/border/pallas_call | solution.py:591
  10.3 0.0 collective-permute-done.5.refs_1_
  10.3 0.8 %final.1 = f32[1,2,32,1024]{3,2,1,0:T(8,128)} custom-call(f32[2,32,512]{2,1,0:T(8,128)S(1)} %get-tuple-element.49.refs_0_, f32[2,32,512]{2,1,0:T(8,128)S(1)} %collective-permute-done.5.refs_1_, f32[2,32,256]{2,1,0:T(8,128)S(1)} %border.1.refs_2_), custom_call_target="tpu_custom_call" | custom-call | tf_op jit(solution)/shard_map/final/pallas_call | solution.py:591
Async XLA Ops:
  0.0 2.4 %collective-permute-start = (f32[2,32,1024]{2,1,0:T(8,128)}, f32[2,32,1024]{2,1,0:T(8,128)S(1)}, u32[]{:S(2)}, u32[]{:S(2)}) collective-permute-start(f32[2,32,1024]{2,1,0:T(8,128)} %state.1), channel_id=1, source_target_pairs={{0,4},{4,0},{1,5},{5,1},{2,6},{6,2},{3,7},{7,3},{8,12},{12,8},{9,1... | collective-permute-start | bytes 786440 | tf_op jit(solution)/shard_map/ppermute | solution.py:619
  0.7 1.6 %collective-permute-start.1 = (f32[32,1024]{1,0:T(8,128)}, f32[32,1024]{1,0:T(8,128)S(1)}, u32[]{:S(2)}, u32[]{:S(2)}) collective-permute-start(f32[32,1024]{1,0:T(8,128)} %feed.1), channel_id=1, source_target_pairs={{0,4},{4,0},{1,5},{5,1},{2,6},{6,2},{3,7},{7,3},{8,12},{12,8},{9,1... | collective-permute-start | bytes 393224 | tf_op jit(solution)/shard_map/ppermute | solution.py:619
  0.7 1.7 %collective-permute-start.2 = (f32[32,1024]{1,0:T(8,128)}, f32[32,1024]{1,0:T(8,128)S(1)}, u32[]{:S(2)}, u32[]{:S(2)}) collective-permute-start(f32[32,1024]{1,0:T(8,128)} %kill.1), channel_id=1, source_target_pairs={{0,4},{4,0},{1,5},{5,1},{2,6},{6,2},{3,7},{7,3},{8,12},{12,8},{9,1... | collective-permute-start | bytes 393224 | tf_op jit(solution)/shard_map/ppermute | solution.py:619
  2.6 4.4 %collective-permute-start.3 = (f32[64,128]{1,0:T(8,128)S(1)}, f32[64,128]{1,0:T(8,128)S(1)}, u32[]{:S(2)}, u32[]{:S(2)}) collective-permute-start(f32[64,128]{1,0:T(8,128)S(1)} %pack.1), channel_id=1, source_target_pairs={{0,1},{1,0},{2,3},{3,2},{5,6},{6,5},{7,4},{4,7},{8,9},{9,8},{10,11... | collective-permute-start | bytes 98312 | tf_op jit(solution)/shard_map/ppermute | solution.py:632
  6.9 1.3 %collective-permute-start.4 = (f32[64,128]{1,0:T(8,128)S(1)}, f32[64,128]{1,0:T(8,128)S(1)}, u32[]{:S(2)}, u32[]{:S(2)}) collective-permute-start(f32[64,128]{1,0:T(8,128)S(1)} %collective-permute-done.3.near), channel_id=1, source_target_pairs={{0,4},{4,0},{1,5},{5,1},{2,6},{6,2},{3,7},{7,3},{8,12},{12,8},{9,1... | collective-permute-start | bytes 98312 | tf_op jit(solution)/shard_map/ppermute | solution.py:619
  8.2 2.1 %collective-permute-start.5 = (f32[2,32,512]{2,1,0:T(8,128)S(1)}, f32[2,32,512]{2,1,0:T(8,128)S(1)}, u32[]{:S(2)}, u32[]{:S(2)}) collective-permute-start(f32[2,32,512]{2,1,0:T(8,128)S(1)} %get-tuple-element.52), channel_id=1, source_target_pairs={{0,4},{4,0},{1,5},{5,1},{2,6},{6,2},{3,7},{7,3},{8,12},{12,8},{9,1... | collective-permute-start | bytes 393224 | tf_op jit(solution)/shard_map/ppermute | solution.py:619

commit v6 on v5

--- a/solution.py
+++ b/solution.py
@@ -15,7 +15,6 @@
 HALF_STEP = 0.5
 W0 = (5.0 / 24.0, 1.0 / 3.0, -1.0 / 24.0)
 W1 = (-1.0 / 24.0, 1.0 / 3.0, 5.0 / 24.0)
-GUARD = 8
 F32 = jnp.float32
 BF16 = jnp.bfloat16
 PHASES = ((0, 0), (0, 1), (1, 0), (1, 1))
@@ -41,11 +40,14 @@
 
 
 def group_matrix(tiles, inverse):
-    group = 128 // tiles
-    natural = lax.broadcasted_iota(jnp.int32, (256, 256), 1 if inverse else 0)
-    grouped = lax.broadcasted_iota(jnp.int32, (256, 256), 0 if inverse else 1)
-    wanted = 2 * tiles * (grouped % group) + 2 * ((grouped % 128) // group) + grouped // 128
-    return jnp.where(natural == wanted, 1.0, 0.0).astype(BF16)
+    group, bits = 128 // tiles, (tiles - 1).bit_length()
+    source = lax.broadcasted_iota(jnp.int32, (256, 256), 0)
+    target = lax.broadcasted_iota(jnp.int32, (1, 256), 1)
+    if inverse:
+        wanted = ((target & 1) << 7) + (((target >> 1) & (tiles - 1)) << (7 - bits)) + (target >> (1 + bits))
+    else:
+        wanted = ((target & (group - 1)) << (1 + bits)) + (((target & 127) >> (7 - bits)) << 1) + (target >> 7)
+    return jnp.where(source == wanted, 1.0, 0.0).astype(BF16)
 
 
 def exchanged(tiles, slot):
@@ -64,22 +66,21 @@
 
 
 def slots(tiles):
-    return lax.broadcasted_iota(jnp.int32, (1, 128), 1) // (128 // tiles)
-
-
-C_X0, C_X1, C_X2, C_END, C_C1, C_NEW, C_E1, C_D1, C_D2 = (2 * i for i in range(9))
+    return lax.broadcasted_iota(jnp.int32, (1, 128), 1) >> (7 - (tiles - 1).bit_length())
+
+
+C_X0, C_X1, C_X2, C_END, C_C1, C_NEW, C_E1, C_D1, C_D2, C_D2_BEFORE = (2 * i for i in range(10))
 COARSE_STENCIL = 20
 N_LAST, N_K0, N_K1, N_G0, N_RA, N_RB, N_RE, N_F1, N_RF2 = (2 * i for i in range(9))
 COARSE_PLAIN = 18
 
 
 def state_shapes(rows, lanes):
-    guarded = rows + 2 * GUARD
     return [
-        (24, guarded, lanes),
+        (24, rows, lanes),
         (24, rows, lanes),
         (8, rows, lanes),
-        (COARSE_STENCIL, guarded, lanes),
+        (COARSE_STENCIL, rows, lanes),
         (COARSE_PLAIN, rows, lanes),
         (2, rows, lanes),
         (8, rows, lanes),
@@ -88,7 +89,7 @@
 
 def late_shapes(rows, lanes):
     return [
-        (8, rows + 2 * GUARD, lanes),
+        (8, rows, lanes),
         (8, rows, lanes),
         (24, rows, lanes),
     ]
@@ -128,24 +129,22 @@
         return (factor * self.mask) * value
 
     def at(self, ref, plane, row, shift=0):
-        return ref[plane, pl.ds(GUARD + row + 8 * shift, 8), :]
+        target = row + 8 * shift
+        if isinstance(row, int) and 0 <= target < self.rows:
+            return ref[plane, pl.ds(target, 8), :]
+        sublane = lax.broadcasted_iota(jnp.int32, (8, 1), 0)
+        if isinstance(row, int):
+            value = ref[plane, pl.ds(target % self.rows, 8), :]
+            return jnp.where(sublane == (0 if shift < 0 else 7), 0.0, pltpu.roll(value, 1 if shift < 0 else 7, 0))
+        if shift == 0:
+            return ref[plane, pl.ds(row, 8), :]
+        inside = (target >= 0) & (target < self.rows)
+        value = ref[plane, pl.ds(pl.multiple_of(lax.rem(target + self.rows, self.rows), 8), 8), :]
+        wrapped = jnp.where(sublane == (0 if shift < 0 else 7), 0.0, pltpu.roll(value, 1 if shift < 0 else 7, 0))
+        return jnp.where(inside, value, wrapped)
 
     def put(self, ref, plane, row, value, lane=slice(None)):
-        ref[plane, pl.ds(GUARD + row, 8), lane] = value
-        sublane = lax.broadcasted_iota(jnp.int32, (8, 1), 0)
-        last = self.rows - 8
-
-        def top():
-            ref[plane, pl.ds(0, 8), lane] = jnp.where(sublane == 0, 0.0, pltpu.roll(value, 1, 0))
-
-        def bottom():
-            ref[plane, pl.ds(GUARD + self.rows, 8), lane] = jnp.where(sublane == 7, 0.0, pltpu.roll(value, 7, 0))
-
-        for edge, fill in ((last, top), (0, bottom)):
-            if not isinstance(row, int):
-                pl.when(row == edge)(fill)
-            elif row == edge:
-                fill()
+        ref[plane, pl.ds(row, 8), lane] = value
 
     def get(self, ref, plane, row):
         return ref[plane, pl.ds(row, 8), :]
@@ -222,6 +221,7 @@
                 lv.put(cs, C_X1 + s, row, start + HALF_STEP * mean)
                 lv.put(cs, C_END + s, row, start + mean)
                 lv.put(cs, C_D1 + s, row, jnp.zeros_like(mean))
+                lv.put(cs, C_D2 + s, row, jnp.zeros_like(mean))
 
         def moments(which, state, row):
             u, v = state
@@ -257,7 +257,7 @@
             for s in range(2):
                 mean = lv.block_mean([r[s] for r in rates])
                 lv.set(cp, N_RE + s, row, mean - lv.scaled(laps[s], 0.5 * (DIFF_U, DIFF_V)[s]))
-            end, last = slice_end(C_D2, row)
+            end, last = slice_end(row)
             for s in range(2):
                 j0, j1 = integrals(lv.get(cp, N_RA + s, row), lv.get(cp, N_F1 + s, row), last[s])
                 lv.put(cs, C_NEW + s, row, lv.at(cs, C_X0 + s, row) + (j0 + j1))
@@ -266,7 +266,7 @@
             middle = W0[1] * f1
             return middle + (W0[0] * f0 + W0[2] * f2), middle + (W1[0] * f0 + W1[2] * f2)
 
-        def slice_end(now, row):
+        def slice_end(row):
             end, scaled, rate = lv.coarse_rates(C_END, row)
             shift = [end[s] - lv.at(cs, C_X2 + s, row) for s in range(2)]
             last = lv.moved_rates(shift, scaled, 1, N_RE, row)
@@ -274,7 +274,8 @@
                 half = HALF_STEP * rate[s]
                 lv.set(cp, N_G0 + s, row, half)
                 lv.put(cs, C_C1 + s, row, end[s] + half + lv.get(cp, N_K0 + s, row))
-                lv.put(cs, now + s, row, shift[s])
+                lv.put(cs, C_D2_BEFORE + s, row, lv.at(cs, C_D2 + s, row))
+                lv.put(cs, C_D2 + s, row, shift[s])
                 lv.set(cp, N_RF2 + s, row, last[s])
             return end, last
 
@@ -292,26 +293,23 @@
                 change = HALF_STEP * new_rate[s] - lv.get(cp, N_G0 + s, row)
                 lv.put(cs, C_E1 + s, row, (new[s] - old) + change)
 
-        def end_nodes(now):
-            def body(row):
-                before = [lv.get(cp, N_RF2 + s, row) for s in range(2)]
-                _, last = slice_end(now, row)
-                change, laps = lv.laplacians(C_E1, row)
-                old, new, j1s = [], [], []
-                for s in range(2):
-                    j0, j1 = integrals(before[s], lv.get(cp, N_F1 + s, row), last[s])
-                    old.append(lv.get(cp, N_LAST + s, row) + j0)
-                    new.append(old[s] + change[s])
-                    j1s.append(j1)
-                feed, both = lv.get(lv.cc, 0, row), lv.get(lv.cc, 1, row)
-                lin = [lv.scaled(laps[s], 0.25 * (DIFF_U, DIFF_V)[s]) for s in range(2)]
-                rate_new = lv.reacted(new[0], new[1], lin[0], lin[1], feed, both)
-                rate_old = lv.reacted(old[0], old[1], 0.0, 0.0, feed, both)
-                for s in range(2):
-                    total = new[s] + j1s[s] + HALF_STEP * (rate_new[s] - rate_old[s])
-                    lv.put(cs, C_NEW + s, row, total)
-
-            return body
+        def end_nodes(row):
+            before = [lv.get(cp, N_RF2 + s, row) for s in range(2)]
+            _, last = slice_end(row)
+            change, laps = lv.laplacians(C_E1, row)
+            old, new, j1s = [], [], []
+            for s in range(2):
+                j0, j1 = integrals(before[s], lv.get(cp, N_F1 + s, row), last[s])
+                old.append(lv.get(cp, N_LAST + s, row) + j0)
+                new.append(old[s] + change[s])
+                j1s.append(j1)
+            feed, both = lv.get(lv.cc, 0, row), lv.get(lv.cc, 1, row)
+            lin = [lv.scaled(laps[s], 0.25 * (DIFF_U, DIFF_V)[s]) for s in range(2)]
+            rate_new = lv.reacted(new[0], new[1], lin[0], lin[1], feed, both)
+            rate_old = lv.reacted(old[0], old[1], 0.0, 0.0, feed, both)
+            for s in range(2):
+                total = new[s] + j1s[s] + HALF_STEP * (rate_new[s] - rate_old[s])
+                lv.put(cs, C_NEW + s, row, total)
 
         def corrections(starts):
             def body(row):
@@ -332,7 +330,7 @@
 
         def one_slice(n, carry):
             lv.each(middle_nodes)
-            lv.each(end_nodes(C_D2 + 2 * lax.rem(n, 2)))
+            lv.each(end_nodes)
             return carry
 
         if start:
@@ -340,30 +338,27 @@
         if not finish:
             return
 
-        first = own == 0
-        now = C_D2 + 2 * lax.rem(own, 2)
-        before = jnp.where(first, C_D1, 2 * C_D2 + 2 - now)
-        origin = jnp.where(first, 0, 2)
-        lv.each(corrections((before, C_D1, now)))
+        origin = jnp.where(own == 0, 0, 2)
+        starts = (C_D2_BEFORE, C_D1, C_D2)
+        lv.each(corrections(starts))
 
         def own_nodes(row):
             for p in range(4):
                 for t in range(0, lv.lanes, 128):
                     lane = pl.ds(t, 128)
-                    high = pl.ds(GUARD + row, 8)
-                    low = pl.ds(row, 8)
-                    feed, both = lv.coef[p, low, lane], lv.coef[4 + p, low, lane]
+                    tile = pl.ds(row, 8)
+                    feed, both = lv.coef[p, tile, lane], lv.coef[4 + p, tile, lane]
                     rates, start = [], None
-                    for k, (base, d) in enumerate(((origin, before), (1, C_D1), (2, now))):
-                        pair = [lv.fine[base * 8 + s * 4 + p, high, lane] + cs[d + s, high, lane] for s in range(2)]
-                        lin = [lv.lin[base * 8 + s * 4 + p, low, lane] + lv.tl[k * 8 + s * 4 + p, low, lane] for s in range(2)]
+                    for k, (base, d) in enumerate(zip((origin, 1, 2), starts)):
+                        pair = [lv.fine[base * 8 + s * 4 + p, tile, lane] + cs[d + s, tile, lane] for s in range(2)]
+                        lin = [lv.lin[base * 8 + s * 4 + p, tile, lane] + lv.tl[k * 8 + s * 4 + p, tile, lane] for s in range(2)]
                         rates.append(lv.reacted(pair[0], pair[1], lin[0], lin[1], feed, both))
                         start = pair if k == 0 else start
                     for s in range(2):
                         f0, f1, f2 = (r[s] for r in rates)
                         second = start[s] + (W0[0] * f0 + W0[1] * f1 + W0[2] * f2)
                         lv.put(lv.fresh, s * 4 + p, row, second, lane)
-                        lv.rest[s * 4 + p, low, lane] = second + (W1[0] * f0 + (W1[1] - HALF_STEP) * f1 + W1[2] * f2)
+                        lv.rest[s * 4 + p, tile, lane] = second + (W1[0] * f0 + (W1[1] - HALF_STEP) * f1 + W1[2] * f2)
 
         lv.each(own_nodes)
 
@@ -400,12 +395,9 @@
                 picked = [natural[plane, 2 * q + b, pl.ds(2 * t + a, 8, stride=2 * chunks), :] for plane in range(4)]
                 lane, row = pl.ds(128 * q, 128), 8 * t
                 for s in range(2):
-                    level.fine[s * 4 + p, pl.ds(GUARD + row, 8), lane] = picked[s]
+                    level.fine[s * 4 + p, pl.ds(row, 8), lane] = picked[s]
                 level.coef[p, pl.ds(row, 8), lane] = picked[2]
                 level.coef[4 + p, pl.ds(row, 8), lane] = picked[2] + picked[3]
-    for plane in range(8):
-        for row in {0, level.rows - 8}:
-            level.put(level.fine, plane, row, level.at(level.fine, plane, row))
 
 
 def spread(level, natural):
@@ -418,9 +410,8 @@
                     natural[s, 2 * q + b, pl.ds(2 * t + a, 8, stride=2 * chunks), :] = value
 
 
-def merged(level, first, rows, natural):
+def merged(level, first, rows, natural, matrix):
     count = level.lanes // 128
-    matrix = group_matrix(count, True)
     slot = slots(count)
     halves = []
     for b in range(2):
@@ -430,6 +421,22 @@
         halves.append(exchanged(tiles, slot))
     blocks = [permuted(jnp.concatenate([halves[0][k], halves[1][k]], axis=1), matrix) for k in range(count)]
     return [[block[s * rows : (s + 1) * rows] for block in blocks] for s in range(2)]
+
+
+def woven(natural, first, rows):
+    lane = lax.broadcasted_iota(jnp.int32, (8, 128), 1)
+    results = []
+    for s in range(2):
+        blocks = []
+        for at in range(0, rows, 8):
+            pair = [natural[s, b, pl.ds(pl.multiple_of(first + at, 8), 8), :] for b in range(2)]
+            halves = []
+            for k in range(2):
+                even, odd = (jnp.take_along_axis(x, (lane >> 1) + 64 * k, axis=1) for x in pair)
+                halves.append(jnp.where((lane & 1) == 0, even, odd))
+            blocks.append(jnp.concatenate(halves, axis=1))
+        results.append([jnp.concatenate(blocks, axis=0)])
+    return results
 
 
 def own_first(rows):
@@ -471,17 +478,19 @@
             sources.append((reader(planes), first))
             for plane in range(4):
                 value = planes[plane][...]
-                cuts = [value[:, :halo], value[:, :side], value[:, (columns - seam) // 2 : (columns + seam) // 2]]
-                cuts += [value[:, columns - side :], value[:, columns - halo :]]
+                blank = jnp.zeros((rows, halo), F32)
+                cuts = [blank, value[:, :side], value[:, (columns - seam) // 2 : (columns + seam) // 2]]
+                cuts += [value[:, columns - side :], blank]
                 window[plane, pl.ds(first, rows), :] = jnp.concatenate([cut for cut in cuts if cut.shape[1]], axis=1)
         load_planes(level, sources, here, natural)
     level.run(lax.axis_index("ta"), start, finish)
     if finish:
         spread(level, natural)
+        matrix = group_matrix(level.lanes // 128, True)
         mine = own_first(rows)
         firsts = [mine, pl.multiple_of(rows - mine, rows)] if parts == 2 else [mine]
         for target, first in zip(outs, firsts):
-            blocks = merged(level, first, rows, natural)
+            blocks = merged(level, first, rows, natural, matrix)
             for s in range(2):
                 for k, block in enumerate(blocks[s]):
                     target[s, :, pl.ds(256 * k, 256)] = block
@@ -499,14 +508,17 @@
     outside = ((at < halo // 2) & (index == 0)) | ((at >= lanes - halo // 2) & (index == size - 1))
     level = Level(work[:-1], parts * rows // 2, lanes, jnp.where(outside, 0.0, 1.0))
 
+    strips = []
+    for edge, (a, b) in ((0, (far, near)), (size - 1, (near, far))):
+        strip = jnp.where(index == edge, 0.0, jnp.where(swap, a[...], b[...]))
+        strips.append(unfolded(strip, parts * rows, 4 * depth))
+
     def reader(first):
         def read(plane, block):
-            part = slice(halo * plane, halo * plane + halo)
-            a, b = near[pl.ds(first, rows), :][:, part], far[pl.ds(first, rows), :][:, part]
-            low, high = jnp.where(swap, b, a), jnp.where(swap, a, b)
-            low, high = jnp.where(index == 0, 0.0, low), jnp.where(index == size - 1, 0.0, high)
+            low, high = (strip[first : first + rows, depth * plane : depth * plane + depth] for strip in strips)
             own = window[plane, pl.ds(first, rows), :]
-            whole = jnp.concatenate([low, own[:, halo : width - halo], high], axis=1)
+            cuts = [own[:, : halo - depth], low, own[:, halo : width - halo], high, own[:, width - halo + depth :]]
+            whole = jnp.concatenate([cut for cut in cuts if cut.shape[1]], axis=1)
             return whole[:, 256 * block : 256 * block + 256]
 
         return read
@@ -514,47 +526,104 @@
     load_planes(level, [(reader(g * rows), g * rows) for g in range(parts)], width, work[-1])
     level.run(lax.axis_index("ta"))
     spread(level, work[-1])
-    natural = merged(level, own_first(rows), rows, work[-1])
+    natural = woven(work[-1], own_first(rows), rows) if tiles == 1 else None
+    natural = natural or merged(level, own_first(rows), rows, work[-1], group_matrix(tiles, True))
     for s in range(2):
         for k, block in enumerate(natural[s]):
             out[s, :, pl.ds(256 * k, 256)] = block
 
 
-def final_kernel(halo, depth, width, *refs):
-    inner, border, out = refs[:-2], refs[-2], refs[-1]
+def final_kernel(halo, depth, width, inner, border, out):
     total = out.shape[-1]
-    share = total // len(inner)
-    for k, value in enumerate(inner):
-        origin = lax.axis_index("gx") * share
-        origin = 0 if len(inner) == 1 else pl.multiple_of(origin if k == 0 else share - origin, share)
-        out[0, :, :, pl.ds(origin, share)] = value[...]
-    pieces = [(0, halo, depth), (total - depth, width - halo - depth, depth)]
-    if len(inner) > 1:
-        pieces.append((total // 2 - depth, width // 2 - depth, depth))
-        pieces.append((total // 2, width // 2, depth))
+    out[0] = inner[...]
     for s in range(2):
-        whole = border[s]
-        for column, source, size in pieces:
+        for column, source in ((0, halo), (total - depth, width - halo - depth)):
             low = column // 128 * 128
-            high = round_up(column + size, 128)
-            old = out[0, s, :, pl.ds(low, high - low)]
-            parts_of = [old[:, : column - low], whole[:, source : source + size], old[:, column + size - low :]]
+            high = round_up(column + depth, 128)
+            old, new = out[0, s, :, pl.ds(low, high - low)], border[s][:, source : source + depth]
+            parts_of = [old[:, : column - low], new, old[:, column + depth - low :]]
             out[0, s, :, pl.ds(low, high - low)] = jnp.concatenate([x for x in parts_of if x.shape[1]], axis=1)
 
 
-def pack_kernel(parts, rows, halo, *refs):
+def joined_kernel(halo, depth, width, keep, got, border, out, ends, middle, sems):
+    total = out.shape[-1]
+    half = total // 2
+    tile = round_up(depth, 128)
+    core = lax.axis_index("gx")
+    copies = []
+    for k, value in enumerate((keep, got)):
+        origin = pl.multiple_of((core if k == 0 else 1 - core) * half + tile, 128)
+        inside = pl.ds(tile, half - 2 * tile)
+        target = out.at[0, :, :, pl.ds(origin, half - 2 * tile)]
+        copies.append(pltpu.make_async_copy(value.at[:, :, inside], target, sems.at[k]))
+        copies[-1].start()
+    first = core == 0
+    low, high = pl.ds(0, tile), pl.ds(half - tile, tile)
+    for s in range(2):
+        old = [jnp.where(first, a[s, :, at], b[s, :, at]) for a, b in ((keep, got), (got, keep)) for at in (low, high)]
+        new = border[s]
+        starts = (halo, width // 2 - depth, width // 2, width - halo - depth)
+        new = [new[:, at : at + depth] for at in starts]
+        ends[0, s] = jnp.concatenate([new[0], old[0][:, depth:]], axis=1)
+        ends[1, s] = jnp.concatenate([old[3][:, : tile - depth], new[3]], axis=1)
+        middle[s] = jnp.concatenate([old[1][:, : tile - depth], new[1], new[2], old[2][:, depth:]], axis=1)
+    copies.append(pltpu.make_async_copy(ends.at[0], out.at[0, :, :, pl.ds(0, tile)], sems.at[2]))
+    copies.append(pltpu.make_async_copy(ends.at[1], out.at[0, :, :, pl.ds(total - tile, tile)], sems.at[3]))
+    copies.append(pltpu.make_async_copy(middle, out.at[0, :, :, pl.ds(half - tile, 2 * tile)], sems.at[4]))
+    for copy in copies[2:]:
+        copy.start()
+    for copy in copies:
+        copy.wait()
+
+
+def folds(rows, lanes):
+    return 8 * -(-(rows // 8 * lanes) // 128) if lanes < 128 else rows
+
+
+def folded(strip):
+    rows, lanes = strip.shape
+    kept, spare = folds(rows, lanes), 128 - lanes
+    if lanes >= 128:
+        return strip
+    stream = [strip[at : at + 8] for at in range(kept, rows, 8)]
+    missing = kept // 8 * spare - (rows - kept) // 8 * lanes
+    stream = jnp.concatenate(stream + [jnp.zeros((8, missing), F32)] * (missing > 0), axis=1)
+    groups = []
+    for k in range(kept // 8):
+        groups.append(jnp.concatenate([strip[8 * k : 8 * k + 8], stream[:, k * spare : (k + 1) * spare]], axis=1))
+    return jnp.concatenate(groups, axis=0)
+
+
+def unfolded(value, rows, lanes):
+    kept = folds(rows, lanes)
+    if lanes >= 128:
+        return value
+    stream = jnp.concatenate([value[at : at + 8, lanes:] for at in range(0, kept, 8)], axis=1)
+    tail = [stream[:, k * lanes : (k + 1) * lanes] for k in range((rows - kept) // 8)]
+    return jnp.concatenate([value[:, :lanes], *tail], axis=0)
+
+
+def pack_kernel(parts, rows, depth, *refs):
     count = 7 if parts == 2 else 3
     ins, outs = refs[:count], refs[count:]
     even = lax.rem(lax.axis_index("gy"), 2) == 0
     if parts == 2:
         even = even == (lax.axis_index("gx") == 0)
-    for planes, first in source_list(ins, rows, parts):
+    strips = []
+    for planes, _ in source_list(ins, rows, parts):
         total = planes[0].shape[-1]
-        tile = round_up(halo, 128)
-        low = jnp.concatenate([ref[:, pl.ds(0, tile)][:, :halo] for ref in planes], axis=1)
-        high = jnp.concatenate([ref[:, pl.ds(total - tile, tile)][:, tile - halo :] for ref in planes], axis=1)
-        for k, out in enumerate(outs):
-            out[pl.ds(first, rows), :] = jnp.where(even, low, high) if k else jnp.where(even, high, low)
+        tile = round_up(depth, 128)
+        low = jnp.concatenate([ref[:, pl.ds(0, tile)][:, :depth] for ref in planes], axis=1)
+        high = jnp.concatenate([ref[:, pl.ds(total - tile, tile)][:, tile - depth :] for ref in planes], axis=1)
+        strips.append((jnp.where(even, high, low), jnp.where(even, low, high)))
+    if parts == 2:
+        (own, _), (other, _) = strips
+        first = lax.axis_index("gx") == 0
+        whole = [jnp.concatenate([jnp.where(first, own, other), jnp.where(first, other, own)], axis=0)]
+    else:
+        whole = [jnp.concatenate(each, axis=0) for each in zip(*strips)]
+    for out, strip in zip(outs, whole):
+        out[...] = folded(strip)
 
 
 def fetch_kernel(state, feed, kill, *refs):
@@ -587,12 +656,12 @@
     return sum(4 * math.prod(shape) for shape in shapes)
 
 
-def called(name, kernel, outs, scratch, limit, inputs, specs=VMEM, flops=0):
+def called(name, kernel, outs, scratch, limit, inputs, specs=VMEM, out_specs=VMEM, flops=0):
     return pl.pallas_call(
         kernel,
         out_shape=outs,
         in_specs=[specs] * len(inputs),
-        out_specs=[VMEM] * len(outs),
+        out_specs=[out_specs] * len(outs),
         scratch_shapes=scratch,
         compiler_params=pltpu.CompilerParams(vmem_limit_bytes=limit),
         cost_estimate=pl.CostEstimate(flops=flops, bytes_accessed=flops // 2, transcendentals=0),
@@ -625,11 +694,20 @@
         fields = [*own, *others]
     else:
         fields = [lax.all_gather(value, "gx") for value in given]
-    pack = functools.partial(pack_kernel, parts, rows, halo)
-    sent = called("pack", pack, arrays([(every, 4 * halo)] * (1 if parts == 2 else 2)), [], 8 * plane_bytes + 2**22, fields)
+    pack = functools.partial(pack_kernel, parts, rows, depth)
+    strips = arrays([(folds(every, 4 * depth), max(4 * depth, 128))] * (1 if parts == 2 else 2))
+    sent = called("pack", pack, strips, [], 8 * plane_bytes + 2**22, fields)
     if parts == 2:
-        pairs = low_pairs + [(blocks + source, blocks + target) for source, target in high_pairs]
-        near = lax.ppermute(sent[0], ("gx", "gy"), pairs)
+        pairs = []
+        for n in range(slices):
+            base = n * 2 * blocks
+            inner_pairs = both_ways([(i, i + 1) for i in range(1, blocks - 1, 2)])
+            pairs += [(base + source, base + target) for source, target in low_pairs]
+            pairs += [(base + blocks + source, base + blocks + target) for source, target in inner_pairs]
+            if n ^ 1 < slices:
+                met = {0, blocks - 1} - {source for source, _ in inner_pairs}
+                pairs += [(base + blocks + i, (n ^ 1) * 2 * blocks + blocks + i) for i in sorted(met)]
+        near = lax.ppermute(sent[0], ("ta", "gx", "gy"), pairs)
     else:
         near = lax.ppermute(sent[0], "gy", low_pairs)
         far = lax.ppermute(sent[1], "gy", high_pairs)
@@ -658,8 +736,15 @@
     limit = size_of(work) + 32 * every * width + 2**23
     border = functools.partial(border_kernel, parts, rows, halo, depth, width)
     (edges,) = called("border", border, arrays([(2, rows, width)]), buffers(work), limit, (window, near, far), flops=2**23)
-    final = functools.partial(final_kernel, halo, depth, width)
-    (out,) = called("final", final, arrays([(1, 2, rows, columns)]), [], 16 * plane_bytes + 2**22, (*inner, edges))
+    result = arrays([(1, 2, rows, columns)])
+    if parts == 2:
+        tile = round_up(depth, 128)
+        scratch = buffers([(2, 2, rows, tile), (2, rows, 2 * tile)]) + [pltpu.SemaphoreType.DMA((5,))]
+        final = functools.partial(joined_kernel, halo, depth, width)
+        (out,) = called("final", final, result, scratch, 2**23, (*inner, edges), out_specs=ANY)
+    else:
+        final = functools.partial(final_kernel, halo, depth, width)
+        (out,) = called("final", final, result, [], 16 * plane_bytes + 2**22, (*inner, edges))
     return out
 
 

time: 11.3 us -> 11 us (0.973)
  starting transfers between devices: 3.92 us -> 3.23 us
  waiting for transfers between devices: 0.25 us -> 0.54 us
  Pallas kernels: 6.87 us -> 7.01 us
    ppermute x1, starting transfers between devices: 2.23 us -> 0.19 us  [per_device(): near = lax.ppermute(sent[0], ('ta', 'gx', 'gy'), pairs)]
    ppermute x5, starting transfers between devices: 1.68 us -> 3.04 us  [crossed(): return lax.ppermute(value, 'gx', [(0, 1), (1, 0)])]
    ppermute x1, waiting for transfers between devices: 0.01 us -> 0.44 us  [per_device(): near = lax.ppermute(sent[0], ('ta', 'gx', 'gy'), pairs)]
    ppermute x5, waiting for transfers between devices: 0.25 us -> 0.1 us  [crossed(): return lax.ppermute(value, 'gx', [(0, 1), (1, 0)])]
    pallas_call x6, Pallas kernels: 6.87 us -> 7.01 us  [called(): pl.pallas_call(kernel, out_shape=outs, in_specs=[specs] * len(inputs), ou...]
  transfers between devices with their start and end apart: 6 -> 6, of which waited for: 2 -> 2; matrix products, arithmetic and copies ran while one was open for 0% -> 0% of each run, Pallas kernels for 54% -> 56%
where the time goes in v6:
time: 11 us; the launch traced here: 10.8 us
  Pallas kernels  7.01 us (64%)
  starting transfers between devices  3.23 us (29%)
  waiting for transfers between devices  0.54 us (5%)
    pallas_call x6, Pallas kernels, called(): pl.pallas_call(kernel, out_shape=outs, in_specs=[specs] * len(inputs), ou...  7.01 us
    ppermute x5, starting transfers between devices, crossed(): return lax.ppermute(value, 'gx', [(0, 1), (1, 0)])  3.04 us
    ppermute x1, waiting for transfers between devices, per_device(): near = lax.ppermute(sent[0], ('ta', 'gx', 'gy'), pairs)  0.44 us
  transfers between devices with their start and end apart: 6, of which 2 were waited for; matrix products, arithmetic and copies ran while one was open for 0% of the time, Pallas kernels for 56%

profile of v6, /device:TPU:25, one launch (start us, length us, event | category | flops | bytes accessed | tf_op | source)
XLA Modules:
  0.0 10.8 jit_solution(364949536250983849)
XLA Ops:
  0.0 0.7 %collective-permute-start = (f32[2,32,1024]{2,1,0:T(8,128)}, f32[2,32,1024]{2,1,0:T(8,128)S(1)}, u32[]{:S(2)}, u32[]{:S(2)}) collective-permute-start(f32[2,32,1024]{2,1,0:T(8,128)} %state.1), channel_id=1, source_target_pairs={{0,4},{4,0},{1,5},{5,1},{2,6},{6,2},{3,7},{7,3},{8,12},{12,8},{9,1... | collective-permute-start | bytes 786440 | tf_op jit(solution)/shard_map/ppermute | solution.py:688
  0.7 0.0 collective-permute-start.1
  0.7 0.5 %collective-permute-start.2 = (f32[32,1024]{1,0:T(8,128)}, f32[32,1024]{1,0:T(8,128)S(1)}, u32[]{:S(2)}, u32[]{:S(2)}) collective-permute-start(f32[32,1024]{1,0:T(8,128)} %kill.1), channel_id=1, source_target_pairs={{0,4},{4,0},{1,5},{5,1},{2,6},{6,2},{3,7},{7,3},{8,12},{12,8},{9,1... | collective-permute-start | bytes 393224 | tf_op jit(solution)/shard_map/ppermute | solution.py:688
  1.2 1.1 %fetch.1 = (f32[32,1024]{1,0:T(8,128)S(1)}, f32[32,1024]{1,0:T(8,128)S(1)}, f32[32,1024]{1,0:T(8,128)S(1)}, f32[32,1024]{1,0:T(8,128)S(1)}) custom-call(f32[2,32,1024]{2,1,0:T(8,128)} %state.1, f32[32,1024]{1,0:T(8,128)} %feed.1, f32[32,1024]{1,0:T(8,128)} %kill.1), custom_call_target="tpu_custom_call" | custom-call | tf_op jit(solution)/shard_map/fetch/pallas_call | solution.py:660
  2.3 0.0 collective-permute-done.1.refs_5_
  2.3 0.1 collective-permute-done.2.refs_6_
  2.4 0.0 collective-permute-done.refs_4_
  2.4 0.2 %pack.1 = f32[40,128]{1,0:T(8,128)S(1)} custom-call(f32[32,1024]{1,0:T(8,128)S(1)} %get-tuple-element.30.refs_0_, f32[32,1024]{1,0:T(8,128)S(1)} %get-tuple-element.31.refs_1_, f32[32,1024]{1,0:T(8,128)S(1)} %get-tuple-element.32.refs_2_, f32[32,1024]{1,0:T(8,128)S(1)} %get-tuple-element.33.refs_3_, f32[2,32,1024]{2,1,0:T(8,128)S(1)} %collective-permute-done.refs_4_, ...), custom_call_target="tpu_custom_call" | custom-call | tf_op jit(solution)/shard_map/pack/pallas_call | solution.py:660
  2.7 0.2 %collective-permute-start.3 = (f32[40,128]{1,0:T(8,128)S(1)}, f32[40,128]{1,0:T(8,128)S(1)}, u32[]{:S(2)}, u32[]{:S(2)}) collective-permute-start(f32[40,128]{1,0:T(8,128)S(1)} %pack.1), channel_id=1, source_target_pairs={{0,1},{1,0},{2,3},{3,2},{5,6},{6,5},{4,12},{7,15},{8,9},{9,8},{10,... | collective-permute-start | bytes 61448 | tf_op jit(solution)/shard_map/ppermute | solution.py:710
  2.9 2.0 %interior.1 = (f32[4,64,256]{2,1,0:T(8,128)S(1)}, f32[24,32,256]{2,1,0:T(8,128)S(1)}, f32[24,32,256]{2,1,0:T(8,128)S(1)}, f32[8,32,256]{2,1,0:T(8,128)S(1)}, f32...) custom-call(f32[32,1024]{1,0:T(8,128)S(1)} %get-tuple-element.30.ref, ...), custom_call_target="tpu_custom_call" | custom-call | flops 16777216 | bytes 8388608 | tf_op jit(solution)/shard_map/interior/pallas_call | solution.py:660
  4.9 0.4 %collective-permute-done.3.near = f32[40,128]{1,0:T(8,128)S(1)} collective-permute-done((f32[40,128]{1,0:T(8,128)S(1)}, f32[40,128]{1,0:T(8,128)S(1)}, u32[]{:S(2)}, u32[]{:S(2)}) %collective-permute-start.3) | collective-permute-done | bytes 20512 | tf_op jit(solution)/shard_map/ppermute | solution.py:710
  5.3 1.6 %collective-permute-start.4 = (f32[40,128]{1,0:T(8,128)S(1)}, f32[40,128]{1,0:T(8,128)S(1)}, u32[]{:S(2)}, u32[]{:S(2)}) collective-permute-start(f32[40,128]{1,0:T(8,128)S(1)} %collective-permute-done.3.near), channel_id=1, source_target_pairs={{0,4},{4,0},{1,5},{5,1},{2,6},{6,2},{3,7},{7,3},{8,12},{12,8},{9,1... | collective-permute-start | bytes 61448 | tf_op jit(solution)/shard_map/ppermute | solution.py:688
  6.9 0.9 %own.1 = (f32[2,32,512]{2,1,0:T(8,128)S(1)}, f32[2,32,512]{2,1,0:T(8,128)S(1)}) custom-call(f32[24,32,256]{2,1,0:T(8,128)S(1)} %get-tuple-element.42.refs_0_, f32[24,32,256]{2,1,0:T(8,128)S(1)} %get-tuple-element.43.refs_1_, f32[8,32,256]{2,1,0:T(8,128)S(1)} %get-tuple-element.44.refs_2_, f32[20,32,256]{2,1,0:T(8,128)S(1)} %get-tuple-element.45.refs_3_, ...), custom_call_target="tpu_custom_call" | custom-call | flops 8388608 | bytes 4194304 | tf_op jit(solution)/shard_map/own/pallas_call | solution.py:660
  7.9 0.0 collective-permute-done.4.far
  7.9 0.2 %collective-permute-start.5 = (f32[2,32,512]{2,1,0:T(8,128)S(1)}, f32[2,32,512]{2,1,0:T(8,128)S(1)}, u32[]{:S(2)}, u32[]{:S(2)}) collective-permute-start(f32[2,32,512]{2,1,0:T(8,128)S(1)} %get-tuple-element.52), channel_id=1, source_target_pairs={{0,4},{4,0},{1,5},{5,1},{2,6},{6,2},{3,7},{7,3},{8,12},{12,8},{9,1... | collective-permute-start | bytes 393224 | tf_op jit(solution)/shard_map/ppermute | solution.py:688
  8.1 1.9 %border.1 = f32[2,32,256]{2,1,0:T(8,128)S(1)} custom-call(f32[4,64,256]{2,1,0:T(8,128)S(1)} %get-tuple-element.53.window, f32[40,128]{1,0:T(8,128)S(1)} %collective-permute-done.3.near, f32[40,128]{1,0:T(8,128)S(1)} %collective-permute-done.4.far), custom_call_target="tpu_custom_call" | custom-call | flops 8388608 | bytes 4194304 | tf_op jit(solution)/shard_map/border/pallas_call | solution.py:660
  10.0 0.0 collective-permute-done.5.got
  10.1 0.8 %final.1 = f32[1,2,32,1024]{3,2,1,0:T(8,128)} custom-call(f32[2,32,512]{2,1,0:T(8,128)S(1)} %get-tuple-element.49.keep, f32[2,32,512]{2,1,0:T(8,128)S(1)} %collective-permute-done.5.got, f32[2,32,256]{2,1,0:T(8,128)S(1)} %border.1), custom_call_target="tpu_custom_call" | custom-call | tf_op jit(solution)/shard_map/final/pallas_call | solution.py:660
Async XLA Ops:
  0.0 2.4 %collective-permute-start = (f32[2,32,1024]{2,1,0:T(8,128)}, f32[2,32,1024]{2,1,0:T(8,128)S(1)}, u32[]{:S(2)}, u32[]{:S(2)}) collective-permute-start(f32[2,32,1024]{2,1,0:T(8,128)} %state.1), channel_id=1, source_target_pairs={{0,4},{4,0},{1,5},{5,1},{2,6},{6,2},{3,7},{7,3},{8,12},{12,8},{9,1... | collective-permute-start | bytes 786440 | tf_op jit(solution)/shard_map/ppermute | solution.py:688
  0.7 1.6 %collective-permute-start.1 = (f32[32,1024]{1,0:T(8,128)}, f32[32,1024]{1,0:T(8,128)S(1)}, u32[]{:S(2)}, u32[]{:S(2)}) collective-permute-start(f32[32,1024]{1,0:T(8,128)} %feed.1), channel_id=1, source_target_pairs={{0,4},{4,0},{1,5},{5,1},{2,6},{6,2},{3,7},{7,3},{8,12},{12,8},{9,1... | collective-permute-start | bytes 393224 | tf_op jit(solution)/shard_map/ppermute | solution.py:688
  0.7 1.7 %collective-permute-start.2 = (f32[32,1024]{1,0:T(8,128)}, f32[32,1024]{1,0:T(8,128)S(1)}, u32[]{:S(2)}, u32[]{:S(2)}) collective-permute-start(f32[32,1024]{1,0:T(8,128)} %kill.1), channel_id=1, source_target_pairs={{0,4},{4,0},{1,5},{5,1},{2,6},{6,2},{3,7},{7,3},{8,12},{12,8},{9,1... | collective-permute-start | bytes 393224 | tf_op jit(solution)/shard_map/ppermute | solution.py:688
  2.7 2.7 %collective-permute-start.3 = (f32[40,128]{1,0:T(8,128)S(1)}, f32[40,128]{1,0:T(8,128)S(1)}, u32[]{:S(2)}, u32[]{:S(2)}) collective-permute-start(f32[40,128]{1,0:T(8,128)S(1)} %pack.1), channel_id=1, source_target_pairs={{0,1},{1,0},{2,3},{3,2},{5,6},{6,5},{4,12},{7,15},{8,9},{9,8},{10,... | collective-permute-start | bytes 61448 | tf_op jit(solution)/shard_map/ppermute | solution.py:710
  5.3 2.6 %collective-permute-start.4 = (f32[40,128]{1,0:T(8,128)S(1)}, f32[40,128]{1,0:T(8,128)S(1)}, u32[]{:S(2)}, u32[]{:S(2)}) collective-permute-start(f32[40,128]{1,0:T(8,128)S(1)} %collective-permute-done.3.near), channel_id=1, source_target_pairs={{0,4},{4,0},{1,5},{5,1},{2,6},{6,2},{3,7},{7,3},{8,12},{12,8},{9,1... | collective-permute-start | bytes 61448 | tf_op jit(solution)/shard_map/ppermute | solution.py:688
  7.9 2.2 %collective-permute-start.5 = (f32[2,32,512]{2,1,0:T(8,128)S(1)}, f32[2,32,512]{2,1,0:T(8,128)S(1)}, u32[]{:S(2)}, u32[]{:S(2)}) collective-permute-start(f32[2,32,512]{2,1,0:T(8,128)S(1)} %get-tuple-element.52), channel_id=1, source_target_pairs={{0,4},{4,0},{1,5},{5,1},{2,6},{6,2},{3,7},{7,3},{8,12},{12,8},{9,1... | collective-permute-start | bytes 393224 | tf_op jit(solution)/shard_map/ppermute | solution.py:688

commit v7 on v6

--- a/solution.py
+++ b/solution.py
@@ -75,24 +75,24 @@
 COARSE_PLAIN = 18
 
 
-def state_shapes(rows, lanes):
-    return [
-        (24, rows, lanes),
-        (24, rows, lanes),
-        (8, rows, lanes),
-        (COARSE_STENCIL, rows, lanes),
-        (COARSE_PLAIN, rows, lanes),
-        (2, rows, lanes),
-        (8, rows, lanes),
-    ]
-
-
-def late_shapes(rows, lanes):
-    return [
-        (8, rows, lanes),
-        (8, rows, lanes),
-        (24, rows, lanes),
-    ]
+PLANES = {
+    "fine": 24,
+    "lin": 24,
+    "coef": 8,
+    "cs": COARSE_STENCIL,
+    "cp": COARSE_PLAIN,
+    "cc": 2,
+    "mom": 8,
+    "fresh": 8,
+    "rest": 8,
+    "tl": 24,
+    "ends": 8,
+}
+HANDED = ("fresh", "rest", "coef", "cs")
+
+
+def shapes_of(names, rows, lanes):
+    return [(PLANES[name], rows, lanes) for name in names]
 
 
 def natural_shape(rows, lanes):
@@ -101,8 +101,8 @@
 
 class Level:
     def __init__(self, refs, rows, lanes, mask):
-        self.fine, self.lin, self.coef, self.cs, self.cp, self.cc, self.mom, *late = refs
-        self.fresh, self.rest, self.tl = late or (None, None, None)
+        for name, ref in refs.items():
+            setattr(self, name, ref)
         self.rows, self.lanes, self.mask = rows, lanes, mask
         self.chunks = rows // 8
 
@@ -204,7 +204,7 @@
 
     def run(self, own, start=True, finish=True):
         lv = self
-        cs, cp = self.cs, self.cp
+        cs, cp = self.cs, getattr(self, "cp", None)
 
         def first_sweep(row):
             for k in range(2):
@@ -323,25 +323,13 @@
 
             return body
 
-        if start:
-            lv.each(first_sweep)
-            lv.each(second_sweep)
-            lv.each(third_sweep)
-
         def one_slice(n, carry):
             lv.each(middle_nodes)
             lv.each(end_nodes)
             return carry
 
-        if start:
-            lax.fori_loop(1, own + 1, one_slice, 0)
-        if not finish:
-            return
-
         origin = jnp.where(own == 0, 0, 2)
         starts = (C_D2_BEFORE, C_D1, C_D2)
-        lv.each(corrections(starts))
-
         def own_nodes(row):
             for p in range(4):
                 for t in range(0, lv.lanes, 128):
@@ -360,17 +348,23 @@
                         lv.put(lv.fresh, s * 4 + p, row, second, lane)
                         lv.rest[s * 4 + p, tile, lane] = second + (W1[0] * f0 + (W1[1] - HALF_STEP) * f1 + W1[2] * f2)
 
-        lv.each(own_nodes)
-
         def last_node(row):
             _, _, rates = lv.fine_rates(3, row)
             for s in range(2):
                 ends = [lv.get(lv.rest, s * 4 + p, row) + HALF_STEP * rates[p][s] for p in range(4)]
                 fix = lv.at(cs, C_NEW + s, row) - lv.block_mean(ends)
                 for p in range(4):
-                    lv.set(lv.rest, s * 4 + p, row, ends[p] + fix)
-
-        lv.each(last_node)
+                    lv.set(lv.ends, s * 4 + p, row, ends[p] + fix)
+
+        if start:
+            lv.each(first_sweep)
+            lv.each(second_sweep)
+            lv.each(third_sweep)
+            lax.fori_loop(1, own + 1, one_slice, 0)
+            lv.each(corrections(starts))
+            lv.each(own_nodes)
+        if finish:
+            lv.each(last_node)
 
 
 def load_planes(level, sources, columns, natural):
@@ -406,7 +400,7 @@
         for q in range(count):
             for p, (a, b) in enumerate(PHASES):
                 for t in range(chunks):
-                    value = level.rest[s * 4 + p, pl.ds(8 * t, 8), pl.ds(128 * q, 128)]
+                    value = level.ends[s * 4 + p, pl.ds(8 * t, 8), pl.ds(128 * q, 128)]
                     natural[s, 2 * q + b, pl.ds(2 * t + a, 8, stride=2 * chunks), :] = value
 
 
@@ -461,13 +455,15 @@
     seam = 4 * depth if parts == 2 else 0
     side = (width - seam) // 2 - halo
     ins = take(7 if parts == 2 else 3) if start else []
-    given = [] if start else take(7)
+    names = [] if finish and start else list(HANDED)
+    handed = take(len(names)) if not start else []
     window = take(1)[0] if start else None
     outs = take(2 if parts == 2 else 1) if finish else []
-    state = take(7) if start else given
-    late = take(3) if finish else []
+    handed = handed or take(len(names))
+    names += [name for name in PLANES if name not in names] if start else ["ends"]
+    handed += take(len(names) - len(handed))
     (natural,) = take(1)
-    level = Level(state + late, parts * rows // 2, here // 2, None)
+    level = Level(dict(zip(names, handed)), parts * rows // 2, here // 2, None)
 
     def reader(planes):
         return lambda plane, block: planes[plane][:, pl.ds(origin + 256 * block, 256)]
@@ -506,16 +502,16 @@
     at = lax.broadcasted_iota(jnp.int32, (1, lanes), 1)
     at = tiles * (at % 128) + at // 128
     outside = ((at < halo // 2) & (index == 0)) | ((at >= lanes - halo // 2) & (index == size - 1))
-    level = Level(work[:-1], parts * rows // 2, lanes, jnp.where(outside, 0.0, 1.0))
+    level = Level(dict(zip(PLANES, work)), parts * rows // 2, lanes, jnp.where(outside, 0.0, 1.0))
 
     strips = []
     for edge, (a, b) in ((0, (far, near)), (size - 1, (near, far))):
         strip = jnp.where(index == edge, 0.0, jnp.where(swap, a[...], b[...]))
-        strips.append(unfolded(strip, parts * rows, 4 * depth))
+        strips.append(strip)
 
     def reader(first):
         def read(plane, block):
-            low, high = (strip[first : first + rows, depth * plane : depth * plane + depth] for strip in strips)
+            low, high = (unfolded(strip, first, rows, plane, depth, parts * rows) for strip in strips)
             own = window[plane, pl.ds(first, rows), :]
             cuts = [own[:, : halo - depth], low, own[:, halo : width - halo], high, own[:, width - halo + depth :]]
             whole = jnp.concatenate([cut for cut in cuts if cut.shape[1]], axis=1)
@@ -576,54 +572,72 @@
         copy.wait()
 
 
-def folds(rows, lanes):
-    return 8 * -(-(rows // 8 * lanes) // 128) if lanes < 128 else rows
-
-
-def folded(strip):
-    rows, lanes = strip.shape
-    kept, spare = folds(rows, lanes), 128 - lanes
-    if lanes >= 128:
+def folds(rows, columns):
+    tiles, spare = rows // 8, max(128 // columns - 4, 0)
+    return (-(-4 * tiles // (spare + 4)), spare) if spare else (tiles, 0)
+
+
+def folded(strip, columns):
+    rows = strip.shape[0]
+    kept, spare = folds(rows, columns)
+    if not spare:
         return strip
-    stream = [strip[at : at + 8] for at in range(kept, rows, 8)]
-    missing = kept // 8 * spare - (rows - kept) // 8 * lanes
-    stream = jnp.concatenate(stream + [jnp.zeros((8, missing), F32)] * (missing > 0), axis=1)
-    groups = []
-    for k in range(kept // 8):
-        groups.append(jnp.concatenate([strip[8 * k : 8 * k + 8], stream[:, k * spare : (k + 1) * spare]], axis=1))
-    return jnp.concatenate(groups, axis=0)
-
-
-def unfolded(value, rows, lanes):
-    kept = folds(rows, lanes)
-    if lanes >= 128:
-        return value
-    stream = jnp.concatenate([value[at : at + 8, lanes:] for at in range(0, kept, 8)], axis=1)
-    tail = [stream[:, k * lanes : (k + 1) * lanes] for k in range((rows - kept) // 8)]
-    return jnp.concatenate([value[:, :lanes], *tail], axis=0)
+    tail = [(row, plane) for row in range(8 * kept, rows, 8) for plane in range(4)]
+    tiles = []
+    for k in range(kept):
+        beside = [strip[row : row + 8, p * columns : (p + 1) * columns] for row, p in tail[k * spare : (k + 1) * spare]]
+        blank = jnp.zeros((8, 128 - (4 + len(beside)) * columns), F32)
+        cuts = [strip[8 * k : 8 * k + 8], *beside, blank]
+        tiles.append(jnp.concatenate([cut for cut in cuts if cut.shape[1]], axis=1))
+    return jnp.concatenate(tiles, axis=0)
+
+
+def unfolded(value, first, rows, plane, columns, total):
+    kept, spare = folds(total, columns)
+    tiles = []
+    for row in range(first, first + rows, 8):
+        at, lane = row, plane * columns
+        if spare and row >= 8 * kept:
+            index = (row // 8 - kept) * 4 + plane
+            at, lane = index // spare * 8, (4 + index % spare) * columns
+        tiles.append(value[at : at + 8, lane : lane + columns])
+    return jnp.concatenate(tiles, axis=0)
 
 
 def pack_kernel(parts, rows, depth, *refs):
     count = 7 if parts == 2 else 3
     ins, outs = refs[:count], refs[count:]
     even = lax.rem(lax.axis_index("gy"), 2) == 0
-    if parts == 2:
-        even = even == (lax.axis_index("gx") == 0)
+    sources = source_list(ins, rows, parts)
+    total, tile = ins[-1].shape[-1], round_up(depth, 128)
+    if parts == 2 and depth <= 32:
+        first = lax.axis_index("gx") == 0
+        upper = even == first
+        column = pl.multiple_of(jnp.where(upper, total - tile, 0), 128)
+        offset = jnp.where(upper, tile - depth, 0)
+        lane = lax.broadcasted_iota(jnp.int32, (1, 128), 1)
+        strip = jnp.zeros((2 * rows, 128), F32)
+        for plane in range(4):
+            own, other = (planes[plane][:, pl.ds(column, tile)] for planes, _ in sources)
+            value = jnp.concatenate([jnp.where(first, own, other), jnp.where(first, other, own)], axis=0)
+            value = pltpu.roll(value, lax.rem(plane * depth + 128 - offset, 128), 1)
+            strip = jnp.where((lane >= plane * depth) & (lane < (plane + 1) * depth), value, strip)
+        outs[0][...] = folded(strip[:, : 4 * depth], depth)
+        return
     strips = []
-    for planes, _ in source_list(ins, rows, parts):
-        total = planes[0].shape[-1]
-        tile = round_up(depth, 128)
+    for planes, _ in sources:
         low = jnp.concatenate([ref[:, pl.ds(0, tile)][:, :depth] for ref in planes], axis=1)
         high = jnp.concatenate([ref[:, pl.ds(total - tile, tile)][:, tile - depth :] for ref in planes], axis=1)
         strips.append((jnp.where(even, high, low), jnp.where(even, low, high)))
     if parts == 2:
-        (own, _), (other, _) = strips
         first = lax.axis_index("gx") == 0
+        (own_a, own_b), (other_a, other_b) = strips
+        own, other = jnp.where(first, own_a, own_b), jnp.where(first, other_a, other_b)
         whole = [jnp.concatenate([jnp.where(first, own, other), jnp.where(first, other, own)], axis=0)]
     else:
         whole = [jnp.concatenate(each, axis=0) for each in zip(*strips)]
     for out, strip in zip(outs, whole):
-        out[...] = folded(strip)
+        out[...] = folded(strip, depth)
 
 
 def fetch_kernel(state, feed, kill, *refs):
@@ -695,7 +709,8 @@
     else:
         fields = [lax.all_gather(value, "gx") for value in given]
     pack = functools.partial(pack_kernel, parts, rows, depth)
-    strips = arrays([(folds(every, 4 * depth), max(4 * depth, 128))] * (1 if parts == 2 else 2))
+    kept, spare = folds(every, depth)
+    strips = arrays([(8 * kept, 128 if spare else 4 * depth)] * (1 if parts == 2 else 2))
     sent = called("pack", pack, strips, [], 8 * plane_bytes + 2**22, fields)
     if parts == 2:
         pairs = []
@@ -712,30 +727,31 @@
         near = lax.ppermute(sent[0], "gy", low_pairs)
         far = lax.ppermute(sent[1], "gy", high_pairs)
 
-    state, late = state_shapes(every // 2, here // 2), late_shapes(every // 2, here // 2)
     natural = natural_shape(every // 2, here // 2)
-    limit = size_of(state + late + [natural]) + 32 * every * (columns + width) + 2**22
+    everything = shapes_of(PLANES, every // 2, here // 2) + [natural]
+    limit = size_of(everything) + 32 * every * (columns + width) + 2**22
     interior = functools.partial(interior_kernel, parts, rows, columns, halo, depth, width)
     window_shape = (4, every, width)
     result_shape = (2, rows, here)
     if parts == 2:
         first = functools.partial(interior, True, False)
-        made = called("interior", first, arrays([window_shape] + state), buffers([natural]), limit, fields, flops=2**24)
+        handed = shapes_of(HANDED, every // 2, here // 2)
+        scratch = buffers(shapes_of([name for name in PLANES if name not in HANDED], every // 2, here // 2) + [natural])
+        made = called("interior", first, arrays([window_shape] + handed), scratch, limit, fields, flops=2**24)
         near, window, *made = lax.optimization_barrier((near, *made))
         far = crossed(near)
         last = functools.partial(interior, False, True)
-        keep, give = called("own", last, arrays([result_shape] * 2), buffers(late + [natural]), limit, made, flops=2**23)
-        far, give = lax.optimization_barrier((far, give))
+        scratch = buffers(shapes_of(["ends"], every // 2, here // 2) + [natural])
+        keep, give = called("own", last, arrays([result_shape] * 2), scratch, limit, made, flops=2**34)
         inner = [keep, crossed(give)]
     else:
         whole = functools.partial(interior, True, True)
-        scratch = buffers(state + late + [natural])
-        window, *inner = called("interior", whole, arrays([window_shape, result_shape]), scratch, limit, fields, flops=2**24)
-    work = state_shapes(every // 2, width // 2) + late_shapes(every // 2, width // 2)
-    work.append(natural_shape(every // 2, width // 2))
+        shapes = [window_shape, result_shape]
+        window, *inner = called("interior", whole, arrays(shapes), buffers(everything), limit, fields, flops=2**24)
+    work = shapes_of(PLANES, every // 2, width // 2) + [natural_shape(every // 2, width // 2)]
     limit = size_of(work) + 32 * every * width + 2**23
     border = functools.partial(border_kernel, parts, rows, halo, depth, width)
-    (edges,) = called("border", border, arrays([(2, rows, width)]), buffers(work), limit, (window, near, far), flops=2**23)
+    (edges,) = called("border", border, arrays([(2, rows, width)]), buffers(work), limit, (window, near, far), flops=2**34)
     result = arrays([(1, 2, rows, columns)])
     if parts == 2:
         tile = round_up(depth, 128)

time: 11 us -> 10.6 us (0.964)
  Pallas kernels: 7.01 us -> 6.8 us
  starting transfers between devices: 3.23 us -> 3.11 us
    ppermute x1, waiting for transfers between devices: 0.44 us -> 0.16 us  [per_device(): near = lax.ppermute(sent[0], ('ta', 'gx', 'gy'), pairs)]
    pallas_call x6, Pallas kernels: 7.01 us -> 6.8 us  [called(): pl.pallas_call(kernel, out_shape=outs, in_specs=[specs] * len(inputs), ou...]
    ppermute x5, waiting for transfers between devices: 0.1 us -> 0.3 us  [crossed(): return lax.ppermute(value, 'gx', [(0, 1), (1, 0)])]
    ppermute x5, starting transfers between devices: 3.04 us -> 2.92 us  [crossed(): return lax.ppermute(value, 'gx', [(0, 1), (1, 0)])]
  transfers between devices with their start and end apart: 6 -> 6, of which waited for: 2 -> 3; matrix products, arithmetic and copies ran while one was open for 0% -> 0% of each run, Pallas kernels for 56% -> 56%
where the time goes in v7:
time: 10.6 us; the launch traced here: 10.4 us
  Pallas kernels  6.8 us (64%)
  starting transfers between devices  3.11 us (29%)
  waiting for transfers between devices  0.46 us (4%)
    pallas_call x6, Pallas kernels, called(): pl.pallas_call(kernel, out_shape=outs, in_specs=[specs] * len(inputs), ou...  6.8 us
    ppermute x5, starting transfers between devices, crossed(): return lax.ppermute(value, 'gx', [(0, 1), (1, 0)])  2.92 us
    ppermute x5, waiting for transfers between devices, crossed(): return lax.ppermute(value, 'gx', [(0, 1), (1, 0)])  0.3 us
  transfers between devices with their start and end apart: 6, of which 3 were waited for; matrix products, arithmetic and copies ran while one was open for 0% of the time, Pallas kernels for 56%

profile of v7, /device:TPU:25, one launch (start us, length us, event | category | flops | bytes accessed | tf_op | source)
XLA Modules:
  0.0 10.4 jit_solution(11067177567707158567)
XLA Ops:
  0.0 0.7 %collective-permute-start = (f32[2,32,1024]{2,1,0:T(8,128)}, f32[2,32,1024]{2,1,0:T(8,128)S(1)}, u32[]{:S(2)}, u32[]{:S(2)}) collective-permute-start(f32[2,32,1024]{2,1,0:T(8,128)} %state.1), channel_id=1, source_target_pairs={{0,4},{4,0},{1,5},{5,1},{2,6},{6,2},{3,7},{7,3},{8,12},{12,8},{9,1... | collective-permute-start | bytes 786440 | tf_op jit(solution)/shard_map/ppermute | solution.py:702
  0.7 0.0 collective-permute-start.1
  0.7 0.5 %collective-permute-start.2 = (f32[32,1024]{1,0:T(8,128)}, f32[32,1024]{1,0:T(8,128)S(1)}, u32[]{:S(2)}, u32[]{:S(2)}) collective-permute-start(f32[32,1024]{1,0:T(8,128)} %kill.1), channel_id=1, source_target_pairs={{0,4},{4,0},{1,5},{5,1},{2,6},{6,2},{3,7},{7,3},{8,12},{12,8},{9,1... | collective-permute-start | bytes 393224 | tf_op jit(solution)/shard_map/ppermute | solution.py:702
  1.2 1.1 %fetch.1 = (f32[32,1024]{1,0:T(8,128)S(1)}, f32[32,1024]{1,0:T(8,128)S(1)}, f32[32,1024]{1,0:T(8,128)S(1)}, f32[32,1024]{1,0:T(8,128)S(1)}) custom-call(f32[2,32,1024]{2,1,0:T(8,128)} %state.1, f32[32,1024]{1,0:T(8,128)} %feed.1, f32[32,1024]{1,0:T(8,128)} %kill.1), custom_call_target="tpu_custom_call" | custom-call | tf_op jit(solution)/shard_map/fetch/pallas_call | solution.py:674
  2.3 0.0 collective-permute-done.1.refs_5_
  2.3 0.1 collective-permute-done.2.refs_6_
  2.4 0.0 collective-permute-done.refs_4_
  2.4 0.1 %pack.1 = f32[48,128]{1,0:T(8,128)S(1)} custom-call(f32[32,1024]{1,0:T(8,128)S(1)} %get-tuple-element.22.refs_0_, f32[32,1024]{1,0:T(8,128)S(1)} %get-tuple-element.23.refs_1_, f32[32,1024]{1,0:T(8,128)S(1)} %get-tuple-element.24.refs_2_, f32[32,1024]{1,0:T(8,128)S(1)} %get-tuple-element.25.refs_3_, f32[2,32,1024]{2,1,0:T(8,128)S(1)} %collective-permute-done.refs_4_, ...), custom_call_target="tpu_custom_call" | custom-call | tf_op jit(solution)/shard_map/pack/pallas_call | solution.py:674
  2.6 0.2 %collective-permute-start.3 = (f32[48,128]{1,0:T(8,128)S(1)}, f32[48,128]{1,0:T(8,128)S(1)}, u32[]{:S(2)}, u32[]{:S(2)}) collective-permute-start(f32[48,128]{1,0:T(8,128)S(1)} %pack.1), channel_id=1, source_target_pairs={{0,1},{1,0},{2,3},{3,2},{5,6},{6,5},{4,12},{7,15},{8,9},{9,8},{10,... | collective-permute-start | bytes 73736 | tf_op jit(solution)/shard_map/ppermute | solution.py:725
  2.8 2.3 %interior.1 = (f32[4,64,256]{2,1,0:T(8,128)S(1)}, f32[8,32,256]{2,1,0:T(8,128)S(1)}, f32[8,32,256]{2,1,0:T(8,128)S(1)}, f32[8,32,256]{2,1,0:T(8,128)S(1)}, f32[20,32,256]{2,1,0:T(8,128)S(1)}) custom-call(f32[32,1024]{1,0:T(8,128)S(1)} %get-tuple-element.22.refs_0_, f32[32,1024]{1,0:T(8,128)S(1)} %get-tuple-element.23.refs_1_, ...), custom_call_target="tpu_custom_call" | custom-call | flops 16777216 | bytes 8388608 | tf_op jit(solution)/shard_map/interior/pallas_call | solution.py:674
  5.1 0.2 %collective-permute-done.3.near = f32[48,128]{1,0:T(8,128)S(1)} collective-permute-done((f32[48,128]{1,0:T(8,128)S(1)}, f32[48,128]{1,0:T(8,128)S(1)}, u32[]{:S(2)}, u32[]{:S(2)}) %collective-permute-start.3) | collective-permute-done | bytes 24608 | tf_op jit(solution)/shard_map/ppermute | solution.py:725
  5.3 1.7 %collective-permute-start.5 = (f32[48,128]{1,0:T(8,128)S(1)}, f32[48,128]{1,0:T(8,128)S(1)}, u32[]{:S(2)}, u32[]{:S(2)}) collective-permute-start(f32[48,128]{1,0:T(8,128)S(1)} %collective-permute-done.3.near), channel_id=1, source_target_pairs={{0,4},{4,0},{1,5},{5,1},{2,6},{6,2},{3,7},{7,3},{8,12},{12,8},{9,1... | collective-permute-start | bytes 73736 | tf_op jit(solution)/shard_map/ppermute | solution.py:702
  6.9 0.6 %own.1 = (f32[2,32,512]{2,1,0:T(8,128)S(1)}, f32[2,32,512]{2,1,0:T(8,128)S(1)}) custom-call(f32[8,32,256]{2,1,0:T(8,128)S(1)} %get-tuple-element.31.refs_0_, f32[8,32,256]{2,1,0:T(8,128)S(1)} %get-tuple-element.32.refs_1_, f32[8,32,256]{2,1,0:T(8,128)S(1)} %get-tuple-element.33.refs_2_, f32[20,32,256]{2,1,0:T(8,128)S(1)} %get-tuple-element.34.refs_3_), custom_call_target="tpu_custom_call" | custom-call | flops 17179869184 | bytes 8589934592 | tf_op jit(solution)/shard_map/own/pallas_call | solution.py:674
  7.5 0.1 collective-permute-start.4
  7.6 0.2 %collective-permute-done.5.far = f32[48,128]{1,0:T(8,128)S(1)} collective-permute-done((f32[48,128]{1,0:T(8,128)S(1)}, f32[48,128]{1,0:T(8,128)S(1)}, u32[]{:S(2)}, u32[]{:S(2)}) %collective-permute-start.5) | collective-permute-done | bytes 24608 | tf_op jit(solution)/shard_map/ppermute | solution.py:702
  7.8 1.8 %border.1 = f32[2,32,256]{2,1,0:T(8,128)S(1)} custom-call(f32[4,64,256]{2,1,0:T(8,128)S(1)} %get-tuple-element.37.window, f32[48,128]{1,0:T(8,128)S(1)} %collective-permute-done.3.near, f32[48,128]{1,0:T(8,128)S(1)} %collective-permute-done.5.far), custom_call_target="tpu_custom_call" | custom-call | flops 17179869184 | bytes 8589934592 | tf_op jit(solution)/shard_map/border/pallas_call | solution.py:674
  9.6 0.0 collective-permute-done.4.got
  9.6 0.8 %final.1 = f32[1,2,32,1024]{3,2,1,0:T(8,128)} custom-call(f32[2,32,512]{2,1,0:T(8,128)S(1)} %get-tuple-element.35.keep, f32[2,32,512]{2,1,0:T(8,128)S(1)} %collective-permute-done.4.got, f32[2,32,256]{2,1,0:T(8,128)S(1)} %border.1), custom_call_target="tpu_custom_call" | custom-call | tf_op jit(solution)/shard_map/final/pallas_call | solution.py:674
Async XLA Ops:
  0.0 2.4 %collective-permute-start = (f32[2,32,1024]{2,1,0:T(8,128)}, f32[2,32,1024]{2,1,0:T(8,128)S(1)}, u32[]{:S(2)}, u32[]{:S(2)}) collective-permute-start(f32[2,32,1024]{2,1,0:T(8,128)} %state.1), channel_id=1, source_target_pairs={{0,4},{4,0},{1,5},{5,1},{2,6},{6,2},{3,7},{7,3},{8,12},{12,8},{9,1... | collective-permute-start | bytes 786440 | tf_op jit(solution)/shard_map/ppermute | solution.py:702
  0.7 1.6 %collective-permute-start.1 = (f32[32,1024]{1,0:T(8,128)}, f32[32,1024]{1,0:T(8,128)S(1)}, u32[]{:S(2)}, u32[]{:S(2)}) collective-permute-start(f32[32,1024]{1,0:T(8,128)} %feed.1), channel_id=1, source_target_pairs={{0,4},{4,0},{1,5},{5,1},{2,6},{6,2},{3,7},{7,3},{8,12},{12,8},{9,1... | collective-permute-start | bytes 393224 | tf_op jit(solution)/shard_map/ppermute | solution.py:702
  0.7 1.7 %collective-permute-start.2 = (f32[32,1024]{1,0:T(8,128)}, f32[32,1024]{1,0:T(8,128)S(1)}, u32[]{:S(2)}, u32[]{:S(2)}) collective-permute-start(f32[32,1024]{1,0:T(8,128)} %kill.1), channel_id=1, source_target_pairs={{0,4},{4,0},{1,5},{5,1},{2,6},{6,2},{3,7},{7,3},{8,12},{12,8},{9,1... | collective-permute-start | bytes 393224 | tf_op jit(solution)/shard_map/ppermute | solution.py:702
  2.6 2.7 %collective-permute-start.3 = (f32[48,128]{1,0:T(8,128)S(1)}, f32[48,128]{1,0:T(8,128)S(1)}, u32[]{:S(2)}, u32[]{:S(2)}) collective-permute-start(f32[48,128]{1,0:T(8,128)S(1)} %pack.1), channel_id=1, source_target_pairs={{0,1},{1,0},{2,3},{3,2},{5,6},{6,5},{4,12},{7,15},{8,9},{9,8},{10,... | collective-permute-start | bytes 73736 | tf_op jit(solution)/shard_map/ppermute | solution.py:725
  5.3 2.5 %collective-permute-start.5 = (f32[48,128]{1,0:T(8,128)S(1)}, f32[48,128]{1,0:T(8,128)S(1)}, u32[]{:S(2)}, u32[]{:S(2)}) collective-permute-start(f32[48,128]{1,0:T(8,128)S(1)} %collective-permute-done.3.near), channel_id=1, source_target_pairs={{0,4},{4,0},{1,5},{5,1},{2,6},{6,2},{3,7},{7,3},{8,12},{12,8},{9,1... | collective-permute-start | bytes 73736 | tf_op jit(solution)/shard_map/ppermute | solution.py:702
  7.5 2.1 %collective-permute-start.4 = (f32[2,32,512]{2,1,0:T(8,128)S(1)}, f32[2,32,512]{2,1,0:T(8,128)S(1)}, u32[]{:S(2)}, u32[]{:S(2)}) collective-permute-start(f32[2,32,512]{2,1,0:T(8,128)S(1)} %get-tuple-element.36), channel_id=1, source_target_pairs={{0,4},{4,0},{1,5},{5,1},{2,6},{6,2},{3,7},{7,3},{8,12},{12,8},{9,1... | collective-permute-start | bytes 393224 | tf_op jit(solution)/shard_map/ppermute | solution.py:702

commit v8 on v7

--- a/solution.py
+++ b/solution.py
@@ -100,11 +100,13 @@
 
 
 class Level:
-    def __init__(self, refs, rows, lanes, mask):
+    def __init__(self, refs, rows, lanes, mask, slices=0):
+        self.slices = slices
         for name, ref in refs.items():
             setattr(self, name, ref)
         self.rows, self.lanes, self.mask = rows, lanes, mask
         self.chunks = rows // 8
+        self.recent = {}
 
     def each(self, body):
         if self.chunks <= 4:
@@ -128,13 +130,20 @@
             return factor * value
         return (factor * self.mask) * value
 
+    def known(self, ref, plane, row):
+        return self.recent.get((id(ref), plane, row)) if self.slices else None
+
+    def note(self, ref, plane, row, value):
+        if self.slices:
+            self.recent[id(ref), plane, row] = value
+
     def at(self, ref, plane, row, shift=0):
         target = row + 8 * shift
         if isinstance(row, int) and 0 <= target < self.rows:
-            return ref[plane, pl.ds(target, 8), :]
+            return self.get(ref, plane, target)
         sublane = lax.broadcasted_iota(jnp.int32, (8, 1), 0)
         if isinstance(row, int):
-            value = ref[plane, pl.ds(target % self.rows, 8), :]
+            value = self.get(ref, plane, target % self.rows)
             return jnp.where(sublane == (0 if shift < 0 else 7), 0.0, pltpu.roll(value, 1 if shift < 0 else 7, 0))
         if shift == 0:
             return ref[plane, pl.ds(row, 8), :]
@@ -145,12 +154,15 @@
 
     def put(self, ref, plane, row, value, lane=slice(None)):
         ref[plane, pl.ds(row, 8), lane] = value
+        if isinstance(row, int) and (lane == slice(None) or self.lanes == 128):
+            self.note(ref, plane, row, value)
 
     def get(self, ref, plane, row):
-        return ref[plane, pl.ds(row, 8), :]
+        value = self.known(ref, plane, row)
+        return ref[plane, pl.ds(row, 8), :] if value is None else value
 
     def set(self, ref, plane, row, value):
-        ref[plane, pl.ds(row, 8), :] = value
+        self.put(ref, plane, row, value)
 
     def fine_rates(self, base, row):
         ref, base = (self.fresh, 0) if base == 3 else (self.fine, base)
@@ -335,18 +347,22 @@
                 for t in range(0, lv.lanes, 128):
                     lane = pl.ds(t, 128)
                     tile = pl.ds(row, 8)
-                    feed, both = lv.coef[p, tile, lane], lv.coef[4 + p, tile, lane]
+                    if lv.lanes == 128:
+                        take = lambda ref, plane: lv.get(ref, plane, row)
+                    else:
+                        take = lambda ref, plane, lane=lane: ref[plane, tile, lane]
+                    feed, both = take(lv.coef, p), take(lv.coef, 4 + p)
                     rates, start = [], None
                     for k, (base, d) in enumerate(zip((origin, 1, 2), starts)):
-                        pair = [lv.fine[base * 8 + s * 4 + p, tile, lane] + cs[d + s, tile, lane] for s in range(2)]
-                        lin = [lv.lin[base * 8 + s * 4 + p, tile, lane] + lv.tl[k * 8 + s * 4 + p, tile, lane] for s in range(2)]
+                        pair = [take(lv.fine, base * 8 + s * 4 + p) + take(cs, d + s) for s in range(2)]
+                        lin = [take(lv.lin, base * 8 + s * 4 + p) + take(lv.tl, k * 8 + s * 4 + p) for s in range(2)]
                         rates.append(lv.reacted(pair[0], pair[1], lin[0], lin[1], feed, both))
                         start = pair if k == 0 else start
                     for s in range(2):
                         f0, f1, f2 = (r[s] for r in rates)
                         second = start[s] + (W0[0] * f0 + W0[1] * f1 + W0[2] * f2)
                         lv.put(lv.fresh, s * 4 + p, row, second, lane)
-                        lv.rest[s * 4 + p, tile, lane] = second + (W1[0] * f0 + (W1[1] - HALF_STEP) * f1 + W1[2] * f2)
+                        lv.put(lv.rest, s * 4 + p, row, second + (W1[0] * f0 + (W1[1] - HALF_STEP) * f1 + W1[2] * f2), lane)
 
         def last_node(row):
             _, _, rates = lv.fine_rates(3, row)
@@ -356,10 +372,29 @@
                 for p in range(4):
                     lv.set(lv.ends, s * 4 + p, row, ends[p] + fix)
 
-        if start:
+        def sweeps():
             lv.each(first_sweep)
             lv.each(second_sweep)
             lv.each(third_sweep)
+
+        def written_out(count):
+            nonlocal origin
+            origin = 0 if count == 0 else 2
+            self.recent = {}
+            sweeps()
+            for n in range(1, count + 1):
+                one_slice(n, 0)
+            lv.each(corrections(starts))
+            lv.each(own_nodes)
+            if finish:
+                lv.each(last_node)
+
+        if start and self.slices:
+            for count in range(self.slices):
+                pl.when(own == count)(functools.partial(written_out, count))
+            return
+        if start:
+            sweeps()
             lax.fori_loop(1, own + 1, one_slice, 0)
             lv.each(corrections(starts))
             lv.each(own_nodes)
@@ -492,6 +527,10 @@
                     target[s, :, pl.ds(256 * k, 256)] = block
 
 
+def few(count):
+    return count if count <= 4 else 0
+
+
 def border_kernel(parts, rows, halo, depth, width, window, near, far, out, *work):
     lanes = width // 2
     index, size = lax.axis_index("gy"), lax.axis_size("gy")
@@ -502,7 +541,7 @@
     at = lax.broadcasted_iota(jnp.int32, (1, lanes), 1)
     at = tiles * (at % 128) + at // 128
     outside = ((at < halo // 2) & (index == 0)) | ((at >= lanes - halo // 2) & (index == size - 1))
-    level = Level(dict(zip(PLANES, work)), parts * rows // 2, lanes, jnp.where(outside, 0.0, 1.0))
+    level = Level(dict(zip(PLANES, work)), parts * rows // 2, lanes, jnp.where(outside, 0.0, 1.0), few(lax.axis_size("ta")))
 
     strips = []
     for edge, (a, b) in ((0, (far, near)), (size - 1, (near, far))):

time: 10.6 us -> 10.3 us (0.972)
  the two profiles are of different devices: /device:TPU:25 before, /device:TPU:0 now
where the time goes in v8:
time: 10.3 us; the launch traced here: 10.2 us
  Pallas kernels  5.36 us (52%)
  starting transfers between devices  4.43 us (43%)
  waiting for transfers between devices  0.37 us (4%)
    pallas_call x6, Pallas kernels, called(): pl.pallas_call(kernel, out_shape=outs, in_specs=[specs] * len(inputs), ou...  5.36 us
    ppermute x1, starting transfers between devices, per_device(): near = lax.ppermute(sent[0], ('ta', 'gx', 'gy'), pairs)  2.89 us
    ppermute x5, starting transfers between devices, crossed(): return lax.ppermute(value, 'gx', [(0, 1), (1, 0)])  1.54 us
    ppermute x1, waiting for transfers between devices, per_device(): near = lax.ppermute(sent[0], ('ta', 'gx', 'gy'), pairs)  0.22 us
  transfers between devices with their start and end apart: 6, of which 2 were waited for; matrix products, arithmetic and copies ran while one was open for 0% of the time, Pallas kernels for 43%

profile of v8, /device:TPU:0, one launch (start us, length us, event | category | flops | bytes accessed | tf_op | source)
XLA Modules:
  0.0 10.2 jit_solution(15684270295402535107)
XLA Ops:
  0.0 0.5 %collective-permute-start = (f32[2,32,1024]{2,1,0:T(8,128)}, f32[2,32,1024]{2,1,0:T(8,128)S(1)}, u32[]{:S(2)}, u32[]{:S(2)}) collective-permute-start(f32[2,32,1024]{2,1,0:T(8,128)} %state.1), channel_id=1, source_target_pairs={{0,4},{4,0},{1,5},{5,1},{2,6},{6,2},{3,7},{7,3},{8,12},{12,8},{9,1... | collective-permute-start | bytes 786440 | tf_op jit(solution)/shard_map/ppermute | solution.py:741
  0.5 0.1 collective-permute-start.1
  0.5 0.5 %collective-permute-start.2 = (f32[32,1024]{1,0:T(8,128)}, f32[32,1024]{1,0:T(8,128)S(1)}, u32[]{:S(2)}, u32[]{:S(2)}) collective-permute-start(f32[32,1024]{1,0:T(8,128)} %kill.1), channel_id=1, source_target_pairs={{0,4},{4,0},{1,5},{5,1},{2,6},{6,2},{3,7},{7,3},{8,12},{12,8},{9,1... | collective-permute-start | bytes 393224 | tf_op jit(solution)/shard_map/ppermute | solution.py:741
  1.0 1.1 %fetch.1 = (f32[32,1024]{1,0:T(8,128)S(1)}, f32[32,1024]{1,0:T(8,128)S(1)}, f32[32,1024]{1,0:T(8,128)S(1)}, f32[32,1024]{1,0:T(8,128)S(1)}) custom-call(f32[2,32,1024]{2,1,0:T(8,128)} %state.1, f32[32,1024]{1,0:T(8,128)} %feed.1, f32[32,1024]{1,0:T(8,128)} %kill.1), custom_call_target="tpu_custom_call" | custom-call | tf_op jit(solution)/shard_map/fetch/pallas_call | solution.py:713
  2.1 0.0 collective-permute-done.1.refs_5_
  2.1 0.1 collective-permute-done.2.refs_6_
  2.2 0.0 collective-permute-done.refs_4_
  2.2 0.1 %pack.1 = f32[48,128]{1,0:T(8,128)S(1)} custom-call(f32[32,1024]{1,0:T(8,128)S(1)} %get-tuple-element.22.refs_0_, f32[32,1024]{1,0:T(8,128)S(1)} %get-tuple-element.23.refs_1_, f32[32,1024]{1,0:T(8,128)S(1)} %get-tuple-element.24.refs_2_, f32[32,1024]{1,0:T(8,128)S(1)} %get-tuple-element.25.refs_3_, f32[2,32,1024]{2,1,0:T(8,128)S(1)} %collective-permute-done.refs_4_, ...), custom_call_target="tpu_custom_call" | custom-call | tf_op jit(solution)/shard_map/pack/pallas_call | solution.py:713
  2.4 2.9 %collective-permute-start.3 = (f32[48,128]{1,0:T(8,128)S(1)}, f32[48,128]{1,0:T(8,128)S(1)}, u32[]{:S(2)}, u32[]{:S(2)}) collective-permute-start(f32[48,128]{1,0:T(8,128)S(1)} %pack.1), channel_id=1, source_target_pairs={{0,1},{1,0},{2,3},{3,2},{5,6},{6,5},{4,12},{7,15},{8,9},{9,8},{10,... | collective-permute-start | bytes 73736 | tf_op jit(solution)/shard_map/ppermute | solution.py:764
  5.2 1.6 %interior.1 = (f32[4,64,256]{2,1,0:T(8,128)S(1)}, f32[8,32,256]{2,1,0:T(8,128)S(1)}, f32[8,32,256]{2,1,0:T(8,128)S(1)}, f32[8,32,256]{2,1,0:T(8,128)S(1)}, f32[20,32,256]{2,1,0:T(8,128)S(1)}) custom-call(f32[32,1024]{1,0:T(8,128)S(1)} %get-tuple-element.22.refs_0_, f32[32,1024]{1,0:T(8,128)S(1)} %get-tuple-element.23.refs_1_, ...), custom_call_target="tpu_custom_call" | custom-call | flops 16777216 | bytes 8388608 | tf_op jit(solution)/shard_map/interior/pallas_call | solution.py:713
  6.8 0.2 %collective-permute-done.3.near = f32[48,128]{1,0:T(8,128)S(1)} collective-permute-done((f32[48,128]{1,0:T(8,128)S(1)}, f32[48,128]{1,0:T(8,128)S(1)}, u32[]{:S(2)}, u32[]{:S(2)}) %collective-permute-start.3) | collective-permute-done | bytes 24608 | tf_op jit(solution)/shard_map/ppermute | solution.py:764
  7.0 0.0 collective-permute-start.5
  7.1 0.6 %own.1 = (f32[2,32,512]{2,1,0:T(8,128)S(1)}, f32[2,32,512]{2,1,0:T(8,128)S(1)}) custom-call(f32[8,32,256]{2,1,0:T(8,128)S(1)} %get-tuple-element.31.refs_0_, f32[8,32,256]{2,1,0:T(8,128)S(1)} %get-tuple-element.32.refs_1_, f32[8,32,256]{2,1,0:T(8,128)S(1)} %get-tuple-element.33.refs_2_, f32[20,32,256]{2,1,0:T(8,128)S(1)} %get-tuple-element.34.refs_3_), custom_call_target="tpu_custom_call" | custom-call | flops 17179869184 | bytes 8589934592 | tf_op jit(solution)/shard_map/own/pallas_call | solution.py:713
  7.6 0.6 %collective-permute-start.4 = (f32[2,32,512]{2,1,0:T(8,128)S(1)}, f32[2,32,512]{2,1,0:T(8,128)S(1)}, u32[]{:S(2)}, u32[]{:S(2)}) collective-permute-start(f32[2,32,512]{2,1,0:T(8,128)S(1)} %get-tuple-element.36), channel_id=1, source_target_pairs={{0,4},{4,0},{1,5},{5,1},{2,6},{6,2},{3,7},{7,3},{8,12},{12,8},{9,1... | collective-permute-start | bytes 393224 | tf_op jit(solution)/shard_map/ppermute | solution.py:741
  8.2 0.0 collective-permute-done.5.far
  8.2 1.2 %border.1 = f32[2,32,256]{2,1,0:T(8,128)S(1)} custom-call(f32[4,64,256]{2,1,0:T(8,128)S(1)} %get-tuple-element.37.window, f32[48,128]{1,0:T(8,128)S(1)} %collective-permute-done.3.near, f32[48,128]{1,0:T(8,128)S(1)} %collective-permute-done.5.far), custom_call_target="tpu_custom_call" | custom-call | flops 17179869184 | bytes 8589934592 | tf_op jit(solution)/shard_map/border/pallas_call | solution.py:713
  9.4 0.0 collective-permute-done.4.got
  9.4 0.8 %final.1 = f32[1,2,32,1024]{3,2,1,0:T(8,128)} custom-call(f32[2,32,512]{2,1,0:T(8,128)S(1)} %get-tuple-element.35.keep, f32[2,32,512]{2,1,0:T(8,128)S(1)} %collective-permute-done.4.got, f32[2,32,256]{2,1,0:T(8,128)S(1)} %border.1), custom_call_target="tpu_custom_call" | custom-call | tf_op jit(solution)/shard_map/final/pallas_call | solution.py:713
Async XLA Ops:
  0.0 2.2 %collective-permute-start = (f32[2,32,1024]{2,1,0:T(8,128)}, f32[2,32,1024]{2,1,0:T(8,128)S(1)}, u32[]{:S(2)}, u32[]{:S(2)}) collective-permute-start(f32[2,32,1024]{2,1,0:T(8,128)} %state.1), channel_id=1, source_target_pairs={{0,4},{4,0},{1,5},{5,1},{2,6},{6,2},{3,7},{7,3},{8,12},{12,8},{9,1... | collective-permute-start | bytes 786440 | tf_op jit(solution)/shard_map/ppermute | solution.py:741
  0.5 1.6 %collective-permute-start.1 = (f32[32,1024]{1,0:T(8,128)}, f32[32,1024]{1,0:T(8,128)S(1)}, u32[]{:S(2)}, u32[]{:S(2)}) collective-permute-start(f32[32,1024]{1,0:T(8,128)} %feed.1), channel_id=1, source_target_pairs={{0,4},{4,0},{1,5},{5,1},{2,6},{6,2},{3,7},{7,3},{8,12},{12,8},{9,1... | collective-permute-start | bytes 393224 | tf_op jit(solution)/shard_map/ppermute | solution.py:741
  0.5 1.7 %collective-permute-start.2 = (f32[32,1024]{1,0:T(8,128)}, f32[32,1024]{1,0:T(8,128)S(1)}, u32[]{:S(2)}, u32[]{:S(2)}) collective-permute-start(f32[32,1024]{1,0:T(8,128)} %kill.1), channel_id=1, source_target_pairs={{0,4},{4,0},{1,5},{5,1},{2,6},{6,2},{3,7},{7,3},{8,12},{12,8},{9,1... | collective-permute-start | bytes 393224 | tf_op jit(solution)/shard_map/ppermute | solution.py:741
  2.4 4.7 %collective-permute-start.3 = (f32[48,128]{1,0:T(8,128)S(1)}, f32[48,128]{1,0:T(8,128)S(1)}, u32[]{:S(2)}, u32[]{:S(2)}) collective-permute-start(f32[48,128]{1,0:T(8,128)S(1)} %pack.1), channel_id=1, source_target_pairs={{0,1},{1,0},{2,3},{3,2},{5,6},{6,5},{4,12},{7,15},{8,9},{9,8},{10,... | collective-permute-start | bytes 73736 | tf_op jit(solution)/shard_map/ppermute | solution.py:764
  7.0 1.2 %collective-permute-start.5 = (f32[48,128]{1,0:T(8,128)S(1)}, f32[48,128]{1,0:T(8,128)S(1)}, u32[]{:S(2)}, u32[]{:S(2)}) collective-permute-start(f32[48,128]{1,0:T(8,128)S(1)} %collective-permute-done.3.near), channel_id=1, source_target_pairs={{0,4},{4,0},{1,5},{5,1},{2,6},{6,2},{3,7},{7,3},{8,12},{12,8},{9,1... | collective-permute-start | bytes 73736 | tf_op jit(solution)/shard_map/ppermute | solution.py:741
  7.6 1.8 %collective-permute-start.4 = (f32[2,32,512]{2,1,0:T(8,128)S(1)}, f32[2,32,512]{2,1,0:T(8,128)S(1)}, u32[]{:S(2)}, u32[]{:S(2)}) collective-permute-start(f32[2,32,512]{2,1,0:T(8,128)S(1)} %get-tuple-element.36), channel_id=1, source_target_pairs={{0,4},{4,0},{1,5},{5,1},{2,6},{6,2},{3,7},{7,3},{8,12},{12,8},{9,1... | collective-permute-start | bytes 393224 | tf_op jit(solution)/shard_map/ppermute | solution.py:741

commit v9 on v8

--- a/solution.py
+++ b/solution.py
@@ -101,7 +101,7 @@
 
 class Level:
     def __init__(self, refs, rows, lanes, mask, slices=0):
-        self.slices = slices
+        self.slices = slices if rows <= 32 else 0
         for name, ref in refs.items():
             setattr(self, name, ref)
         self.rows, self.lanes, self.mask = rows, lanes, mask
@@ -175,32 +175,34 @@
                 along = state[s][2 * (1 - a) + b]
                 moved = self.at(ref, base * 8 + s * 4 + 2 * (1 - a) + b, row, 1 if a else -1)
                 side = self.right(across) if b else self.left(across)
-                laps.append((along + moved) + (across + side) - 4.0 * state[s][p])
+                laps.append((((along + moved) + across) - 4.0 * state[s][p]) + side)
             u, v = state[0][p], state[1][p]
             feed = self.get(self.coef, p, row)
             both = self.get(self.coef, 4 + p, row)
-            lin_u = self.scaled(laps[0], DIFF_U) + feed
-            lin_v = self.scaled(laps[1], DIFF_V)
-            linear.append((lin_u, lin_v))
-            rates.append(self.reacted(u, v, lin_u, lin_v, feed, both))
+            rest_u, rest_v = self.reacted(u, v, feed, 0.0, feed, both)
+            scaled_u, scaled_v = self.scaled(laps[0], DIFF_U), self.scaled(laps[1], DIFF_V)
+            linear.append((scaled_u + feed, scaled_v))
+            rates.append((scaled_u + rest_u, scaled_v + rest_v))
         return state, linear, rates
 
     def reacted(self, u, v, lin_u, lin_v, feed, both):
         return lin_u - u * (feed + v * v), lin_v + v * (u * v - both)
 
-    def neighbours(self, plane, row, value):
-        rows = self.at(self.cs, plane, row, -1) + self.at(self.cs, plane, row, 1)
-        return rows + (self.left(value) + self.right(value))
-
     def laplacians(self, first, row):
-        pair = [self.at(self.cs, first + s, row) for s in range(2)]
-        return pair, [self.neighbours(first + s, row, pair[s]) - 4.0 * pair[s] for s in range(2)]
+        pair, laps = [], []
+        for plane in (first, first + 1):
+            value = self.at(self.cs, plane, row)
+            rows = self.at(self.cs, plane, row, -1) + self.at(self.cs, plane, row, 1)
+            pair.append(value)
+            laps.append((rows - 4.0 * value) + (self.left(value) + self.right(value)))
+        return pair, laps
 
     def coarse_rates(self, first, row):
         (u, v), laps = self.laplacians(first, row)
         scaled = [self.scaled(laps[s], 0.25 * (DIFF_U, DIFF_V)[s]) for s in range(2)]
         feed, both = self.get(self.cc, 0, row), self.get(self.cc, 1, row)
-        return (u, v), scaled, self.reacted(u, v, scaled[0] + feed, scaled[1], feed, both)
+        rest_u, rest_v = self.reacted(u, v, feed, 0.0, feed, both)
+        return (u, v), scaled, (scaled[0] + rest_u, scaled[1] + rest_v)
 
     def moved_rates(self, shift, scaled, which, base, row):
         a, b = shift
@@ -317,11 +319,11 @@
                 j1s.append(j1)
             feed, both = lv.get(lv.cc, 0, row), lv.get(lv.cc, 1, row)
             lin = [lv.scaled(laps[s], 0.25 * (DIFF_U, DIFF_V)[s]) for s in range(2)]
-            rate_new = lv.reacted(new[0], new[1], lin[0], lin[1], feed, both)
+            rate_new = lv.reacted(new[0], new[1], 0.0, 0.0, feed, both)
             rate_old = lv.reacted(old[0], old[1], 0.0, 0.0, feed, both)
             for s in range(2):
                 total = new[s] + j1s[s] + HALF_STEP * (rate_new[s] - rate_old[s])
-                lv.put(cs, C_NEW + s, row, total)
+                lv.put(cs, C_NEW + s, row, total + HALF_STEP * lin[s])
 
         def corrections(starts):
             def body(row):
@@ -452,22 +454,6 @@
     return [[block[s * rows : (s + 1) * rows] for block in blocks] for s in range(2)]
 
 
-def woven(natural, first, rows):
-    lane = lax.broadcasted_iota(jnp.int32, (8, 128), 1)
-    results = []
-    for s in range(2):
-        blocks = []
-        for at in range(0, rows, 8):
-            pair = [natural[s, b, pl.ds(pl.multiple_of(first + at, 8), 8), :] for b in range(2)]
-            halves = []
-            for k in range(2):
-                even, odd = (jnp.take_along_axis(x, (lane >> 1) + 64 * k, axis=1) for x in pair)
-                halves.append(jnp.where((lane & 1) == 0, even, odd))
-            blocks.append(jnp.concatenate(halves, axis=1))
-        results.append([jnp.concatenate(blocks, axis=0)])
-    return results
-
-
 def own_first(rows):
     return pl.multiple_of(lax.axis_index("gx") * rows, rows)
 
@@ -531,6 +517,11 @@
     return count if count <= 4 else 0
 
 
+def places(halo, depth, width):
+    last = -depth % 128
+    return (halo, 0), (width // 2 - depth, last), (width // 2, 0), (width - halo - depth, last)
+
+
 def border_kernel(parts, rows, halo, depth, width, window, near, far, out, *work):
     lanes = width // 2
     index, size = lax.axis_index("gy"), lax.axis_size("gy")
@@ -561,8 +552,17 @@
     load_planes(level, [(reader(g * rows), g * rows) for g in range(parts)], width, work[-1])
     level.run(lax.axis_index("ta"))
     spread(level, work[-1])
-    natural = woven(work[-1], own_first(rows), rows) if tiles == 1 else None
-    natural = natural or merged(level, own_first(rows), rows, work[-1], group_matrix(tiles, True))
+    if parts == 2 and tiles == 1:
+        mine = own_first(rows)
+        for k, (start, at) in enumerate(places(halo, depth, width)):
+            source = lax.broadcasted_iota(jnp.int32, (8, 128), 1) + (start - at)
+            for s in range(2):
+                for row in range(0, rows, 8):
+                    pair = [work[-1][s, b, pl.ds(pl.multiple_of(mine + row, 8), 8), :] for b in range(2)]
+                    even, odd = (jnp.take_along_axis(x, (source >> 1) & 127, axis=1) for x in pair)
+                    out[k, s, pl.ds(row, 8), :] = jnp.where((source & 1) == 0, even, odd)
+        return
+    natural = merged(level, own_first(rows), rows, work[-1], group_matrix(tiles, True))
     for s in range(2):
         for k, block in enumerate(natural[s]):
             out[s, :, pl.ds(256 * k, 256)] = block
@@ -594,11 +594,16 @@
         copies[-1].start()
     first = core == 0
     low, high = pl.ds(0, tile), pl.ds(half - tile, tile)
+    starts = [start for start, _ in places(halo, depth, width)]
+    lane = lax.broadcasted_iota(jnp.int32, (1, tile), 1)
     for s in range(2):
         old = [jnp.where(first, a[s, :, at], b[s, :, at]) for a, b in ((keep, got), (got, keep)) for at in (low, high)]
-        new = border[s]
-        starts = (halo, width // 2 - depth, width // 2, width - halo - depth)
-        new = [new[:, at : at + depth] for at in starts]
+        if border.ndim == 4:
+            targets = (ends.at[0, s], middle.at[s, :, pl.ds(0, tile)], middle.at[s, :, pl.ds(tile, tile)], ends.at[1, s])
+            for k, (target, (_, at)) in enumerate(zip(targets, places(halo, depth, width))):
+                target[...] = jnp.where((lane >= at) & (lane < at + depth), border[k, s], old[k])
+            continue
+        new = [border[s][:, at : at + depth] for at in starts]
         ends[0, s] = jnp.concatenate([new[0], old[0][:, depth:]], axis=1)
         ends[1, s] = jnp.concatenate([old[3][:, : tile - depth], new[3]], axis=1)
         middle[s] = jnp.concatenate([old[1][:, : tile - depth], new[1], new[2], old[2][:, depth:]], axis=1)
@@ -789,8 +794,9 @@
         window, *inner = called("interior", whole, arrays(shapes), buffers(everything), limit, fields, flops=2**24)
     work = shapes_of(PLANES, every // 2, width // 2) + [natural_shape(every // 2, width // 2)]
     limit = size_of(work) + 32 * every * width + 2**23
+    shape = (4, 2, rows, 128) if parts == 2 and width == 256 else (2, rows, width)
     border = functools.partial(border_kernel, parts, rows, halo, depth, width)
-    (edges,) = called("border", border, arrays([(2, rows, width)]), buffers(work), limit, (window, near, far), flops=2**34)
+    (edges,) = called("border", border, arrays([shape]), buffers(work), limit, (window, near, far), flops=2**34)
     result = arrays([(1, 2, rows, columns)])
     if parts == 2:
         tile = round_up(depth, 128)

time: 10.3 us -> 10.4 us (level)
  transfers between devices with their start and end apart: 6 -> 6, of which waited for: 2 -> 3; matrix products, arithmetic and copies ran while one was open for 0% -> 0% of each run, Pallas kernels for 43% -> 44%
where the time goes in v9:
time: 10.4 us; the launch traced here: 10.2 us
  Pallas kernels  5.38 us (52%)
  starting transfers between devices  4.43 us (43%)
  waiting for transfers between devices  0.37 us (4%)
    pallas_call x6, Pallas kernels, called(): pl.pallas_call(kernel, out_shape=outs, in_specs=[specs] * len(inputs), ou...  5.38 us
    ppermute x1, starting transfers between devices, per_device(): near = lax.ppermute(sent[0], ('ta', 'gx', 'gy'), pairs)  2.89 us
    ppermute x5, starting transfers between devices, crossed(): return lax.ppermute(value, 'gx', [(0, 1), (1, 0)])  1.54 us
    ppermute x1, waiting for transfers between devices, per_device(): near = lax.ppermute(sent[0], ('ta', 'gx', 'gy'), pairs)  0.21 us
  transfers between devices with their start and end apart: 6, of which 3 were waited for; matrix products, arithmetic and copies ran while one was open for 0% of the time, Pallas kernels for 44%

profile of v9, /device:TPU:0, one launch (start us, length us, event | category | flops | bytes accessed | tf_op | source)
XLA Modules:
  0.0 10.2 jit_solution(17492616140315366514)
XLA Ops:
  0.0 0.5 %collective-permute-start = (f32[2,32,1024]{2,1,0:T(8,128)}, f32[2,32,1024]{2,1,0:T(8,128)S(1)}, u32[]{:S(2)}, u32[]{:S(2)}) collective-permute-start(f32[2,32,1024]{2,1,0:T(8,128)} %state.1), channel_id=1, source_target_pairs={{0,4},{4,0},{1,5},{5,1},{2,6},{6,2},{3,7},{7,3},{8,12},{12,8},{9,1... | collective-permute-start | bytes 786440 | tf_op jit(solution)/shard_map/ppermute | solution.py:746
  0.5 0.1 collective-permute-start.1
  0.5 0.5 %collective-permute-start.2 = (f32[32,1024]{1,0:T(8,128)}, f32[32,1024]{1,0:T(8,128)S(1)}, u32[]{:S(2)}, u32[]{:S(2)}) collective-permute-start(f32[32,1024]{1,0:T(8,128)} %kill.1), channel_id=1, source_target_pairs={{0,4},{4,0},{1,5},{5,1},{2,6},{6,2},{3,7},{7,3},{8,12},{12,8},{9,1... | collective-permute-start | bytes 393224 | tf_op jit(solution)/shard_map/ppermute | solution.py:746
  1.0 1.1 %fetch.1 = (f32[32,1024]{1,0:T(8,128)S(1)}, f32[32,1024]{1,0:T(8,128)S(1)}, f32[32,1024]{1,0:T(8,128)S(1)}, f32[32,1024]{1,0:T(8,128)S(1)}) custom-call(f32[2,32,1024]{2,1,0:T(8,128)} %state.1, f32[32,1024]{1,0:T(8,128)} %feed.1, f32[32,1024]{1,0:T(8,128)} %kill.1), custom_call_target="tpu_custom_call" | custom-call | tf_op jit(solution)/shard_map/fetch/pallas_call | solution.py:718
  2.1 0.0 collective-permute-done.1.refs_5_
  2.1 0.1 collective-permute-done.2.refs_6_
  2.2 0.0 collective-permute-done.refs_4_
  2.2 0.1 %pack.1 = f32[48,128]{1,0:T(8,128)S(1)} custom-call(f32[32,1024]{1,0:T(8,128)S(1)} %get-tuple-element.22.refs_0_, f32[32,1024]{1,0:T(8,128)S(1)} %get-tuple-element.23.refs_1_, f32[32,1024]{1,0:T(8,128)S(1)} %get-tuple-element.24.refs_2_, f32[32,1024]{1,0:T(8,128)S(1)} %get-tuple-element.25.refs_3_, f32[2,32,1024]{2,1,0:T(8,128)S(1)} %collective-permute-done.refs_4_, ...), custom_call_target="tpu_custom_call" | custom-call | tf_op jit(solution)/shard_map/pack/pallas_call | solution.py:718
  2.4 2.9 %collective-permute-start.3 = (f32[48,128]{1,0:T(8,128)S(1)}, f32[48,128]{1,0:T(8,128)S(1)}, u32[]{:S(2)}, u32[]{:S(2)}) collective-permute-start(f32[48,128]{1,0:T(8,128)S(1)} %pack.1), channel_id=1, source_target_pairs={{0,1},{1,0},{2,3},{3,2},{5,6},{6,5},{4,12},{7,15},{8,9},{9,8},{10,... | collective-permute-start | bytes 73736 | tf_op jit(solution)/shard_map/ppermute | solution.py:769
  5.2 1.6 %interior.1 = (f32[4,64,256]{2,1,0:T(8,128)S(1)}, f32[8,32,256]{2,1,0:T(8,128)S(1)}, f32[8,32,256]{2,1,0:T(8,128)S(1)}, f32[8,32,256]{2,1,0:T(8,128)S(1)}, f32[20,32,256]{2,1,0:T(8,128)S(1)}) custom-call(f32[32,1024]{1,0:T(8,128)S(1)} %get-tuple-element.22.refs_0_, f32[32,1024]{1,0:T(8,128)S(1)} %get-tuple-element.23.refs_1_, ...), custom_call_target="tpu_custom_call" | custom-call | flops 16777216 | bytes 8388608 | tf_op jit(solution)/shard_map/interior/pallas_call | solution.py:718
  6.8 0.2 %collective-permute-done.3.near = f32[48,128]{1,0:T(8,128)S(1)} collective-permute-done((f32[48,128]{1,0:T(8,128)S(1)}, f32[48,128]{1,0:T(8,128)S(1)}, u32[]{:S(2)}, u32[]{:S(2)}) %collective-permute-start.3) | collective-permute-done | bytes 24608 | tf_op jit(solution)/shard_map/ppermute | solution.py:769
  7.0 0.0 collective-permute-start.5
  7.1 0.6 %own.1 = (f32[2,32,512]{2,1,0:T(8,128)S(1)}, f32[2,32,512]{2,1,0:T(8,128)S(1)}) custom-call(f32[8,32,256]{2,1,0:T(8,128)S(1)} %get-tuple-element.31.refs_0_, f32[8,32,256]{2,1,0:T(8,128)S(1)} %get-tuple-element.32.refs_1_, f32[8,32,256]{2,1,0:T(8,128)S(1)} %get-tuple-element.33.refs_2_, f32[20,32,256]{2,1,0:T(8,128)S(1)} %get-tuple-element.34.refs_3_), custom_call_target="tpu_custom_call" | custom-call | flops 17179869184 | bytes 8589934592 | tf_op jit(solution)/shard_map/own/pallas_call | solution.py:718
  7.6 0.6 %collective-permute-start.4 = (f32[2,32,512]{2,1,0:T(8,128)S(1)}, f32[2,32,512]{2,1,0:T(8,128)S(1)}, u32[]{:S(2)}, u32[]{:S(2)}) collective-permute-start(f32[2,32,512]{2,1,0:T(8,128)S(1)} %get-tuple-element.36), channel_id=1, source_target_pairs={{0,4},{4,0},{1,5},{5,1},{2,6},{6,2},{3,7},{7,3},{8,12},{12,8},{9,1... | collective-permute-start | bytes 393224 | tf_op jit(solution)/shard_map/ppermute | solution.py:746
  8.2 0.1 collective-permute-done.5.far
  8.2 1.2 %border.1 = f32[4,2,32,128]{3,2,1,0:T(8,128)S(1)} custom-call(f32[4,64,256]{2,1,0:T(8,128)S(1)} %get-tuple-element.37.window, f32[48,128]{1,0:T(8,128)S(1)} %collective-permute-done.3.near, f32[48,128]{1,0:T(8,128)S(1)} %collective-permute-done.5.far), custom_call_target="tpu_custom_call" | custom-call | flops 17179869184 | bytes 8589934592 | tf_op jit(solution)/shard_map/border/pallas_call | solution.py:718
  9.5 0.0 collective-permute-done.4.got
  9.5 0.7 %final.1 = f32[1,2,32,1024]{3,2,1,0:T(8,128)} custom-call(f32[2,32,512]{2,1,0:T(8,128)S(1)} %get-tuple-element.35.keep, f32[2,32,512]{2,1,0:T(8,128)S(1)} %collective-permute-done.4.got, f32[4,2,32,128]{3,2,1,0:T(8,128)S(1)} %border.1), custom_call_target="tpu_custom_call" | custom-call | tf_op jit(solution)/shard_map/final/pallas_call | solution.py:718
Async XLA Ops:
  0.0 2.2 %collective-permute-start = (f32[2,32,1024]{2,1,0:T(8,128)}, f32[2,32,1024]{2,1,0:T(8,128)S(1)}, u32[]{:S(2)}, u32[]{:S(2)}) collective-permute-start(f32[2,32,1024]{2,1,0:T(8,128)} %state.1), channel_id=1, source_target_pairs={{0,4},{4,0},{1,5},{5,1},{2,6},{6,2},{3,7},{7,3},{8,12},{12,8},{9,1... | collective-permute-start | bytes 786440 | tf_op jit(solution)/shard_map/ppermute | solution.py:746
  0.5 1.6 %collective-permute-start.1 = (f32[32,1024]{1,0:T(8,128)}, f32[32,1024]{1,0:T(8,128)S(1)}, u32[]{:S(2)}, u32[]{:S(2)}) collective-permute-start(f32[32,1024]{1,0:T(8,128)} %feed.1), channel_id=1, source_target_pairs={{0,4},{4,0},{1,5},{5,1},{2,6},{6,2},{3,7},{7,3},{8,12},{12,8},{9,1... | collective-permute-start | bytes 393224 | tf_op jit(solution)/shard_map/ppermute | solution.py:746
  0.5 1.7 %collective-permute-start.2 = (f32[32,1024]{1,0:T(8,128)}, f32[32,1024]{1,0:T(8,128)S(1)}, u32[]{:S(2)}, u32[]{:S(2)}) collective-permute-start(f32[32,1024]{1,0:T(8,128)} %kill.1), channel_id=1, source_target_pairs={{0,4},{4,0},{1,5},{5,1},{2,6},{6,2},{3,7},{7,3},{8,12},{12,8},{9,1... | collective-permute-start | bytes 393224 | tf_op jit(solution)/shard_map/ppermute | solution.py:746
  2.4 4.7 %collective-permute-start.3 = (f32[48,128]{1,0:T(8,128)S(1)}, f32[48,128]{1,0:T(8,128)S(1)}, u32[]{:S(2)}, u32[]{:S(2)}) collective-permute-start(f32[48,128]{1,0:T(8,128)S(1)} %pack.1), channel_id=1, source_target_pairs={{0,1},{1,0},{2,3},{3,2},{5,6},{6,5},{4,12},{7,15},{8,9},{9,8},{10,... | collective-permute-start | bytes 73736 | tf_op jit(solution)/shard_map/ppermute | solution.py:769
  7.0 1.2 %collective-permute-start.5 = (f32[48,128]{1,0:T(8,128)S(1)}, f32[48,128]{1,0:T(8,128)S(1)}, u32[]{:S(2)}, u32[]{:S(2)}) collective-permute-start(f32[48,128]{1,0:T(8,128)S(1)} %collective-permute-done.3.near), channel_id=1, source_target_pairs={{0,4},{4,0},{1,5},{5,1},{2,6},{6,2},{3,7},{7,3},{8,12},{12,8},{9,1... | collective-permute-start | bytes 73736 | tf_op jit(solution)/shard_map/ppermute | solution.py:746
  7.6 1.9 %collective-permute-start.4 = (f32[2,32,512]{2,1,0:T(8,128)S(1)}, f32[2,32,512]{2,1,0:T(8,128)S(1)}, u32[]{:S(2)}, u32[]{:S(2)}) collective-permute-start(f32[2,32,512]{2,1,0:T(8,128)S(1)} %get-tuple-element.36), channel_id=1, source_target_pairs={{0,4},{4,0},{1,5},{5,1},{2,6},{6,2},{3,7},{7,3},{8,12},{12,8},{9,1... | collective-permute-start | bytes 393224 | tf_op jit(solution)/shard_map/ppermute | solution.py:746

commit v10 on v9

--- a/solution.py
+++ b/solution.py
@@ -220,10 +220,14 @@
         lv = self
         cs, cp = self.cs, getattr(self, "cp", None)
 
+        made = {}
+
         def first_sweep(row):
             for k in range(2):
                 lv.set(lv.cc, k, row, lv.block_mean([lv.get(lv.coef, 4 * k + p, row) for p in range(4)]))
             state, linear, rates = lv.fine_rates(0, row)
+            if isinstance(row, int):
+                made[0, row] = state, rates
             for s in range(2):
                 for p in range(4):
                     lv.set(lv.lin, s * 4 + p, row, linear[p][s])
@@ -246,6 +250,8 @@
 
         def second_sweep(row):
             state, linear, rates = lv.fine_rates(1, row)
+            if isinstance(row, int):
+                made[1, row] = state, rates
             _, _, g0 = lv.coarse_rates(C_X0, row)
             first, scaled, g1 = lv.coarse_rates(C_X1, row)
             for s in range(2):
@@ -328,6 +334,8 @@
         def corrections(starts):
             def body(row):
                 for k, first in enumerate(starts):
+                    if taken and k < 2:
+                        continue
                     for s in range(2):
                         d = lv.at(cs, first + s, row)
                         ring = [lv.at(cs, first + s, row, -1), lv.at(cs, first + s, row, 1), lv.left(d), lv.right(d)]
@@ -344,6 +352,7 @@
 
         origin = jnp.where(own == 0, 0, 2)
         starts = (C_D2_BEFORE, C_D1, C_D2)
+        taken = False
         def own_nodes(row):
             for p in range(4):
                 for t in range(0, lv.lanes, 128):
@@ -355,7 +364,12 @@
                         take = lambda ref, plane, lane=lane: ref[plane, tile, lane]
                     feed, both = take(lv.coef, p), take(lv.coef, 4 + p)
                     rates, start = [], None
-                    for k, (base, d) in enumerate(zip((origin, 1, 2), starts)):
+                    cases = list(enumerate(zip((origin, 1, 2), starts)))
+                    if taken:
+                        rates = [made[k, row][1][p] for k in range(2)]
+                        start = [made[0, row][0][s][p] for s in range(2)]
+                        cases = cases[2:]
+                    for k, (base, d) in cases:
                         pair = [take(lv.fine, base * 8 + s * 4 + p) + take(cs, d + s) for s in range(2)]
                         lin = [take(lv.lin, base * 8 + s * 4 + p) + take(lv.tl, k * 8 + s * 4 + p) for s in range(2)]
                         rates.append(lv.reacted(pair[0], pair[1], lin[0], lin[1], feed, both))
@@ -380,8 +394,9 @@
             lv.each(third_sweep)
 
         def written_out(count):
-            nonlocal origin
-            origin = 0 if count == 0 else 2
+            nonlocal origin, taken
+            origin, taken = 0 if count == 0 else 2, count == 0 and lv.lanes == 128
+            made.clear()
             self.recent = {}
             sweeps()
             for n in range(1, count + 1):

time: 10.4 us -> 10.3 us (level)
  no operation moved by 1% of the time
where the time goes in v10:
time: 10.3 us; the launch traced here: 10.1 us
  Pallas kernels  5.3 us (51%)
  starting transfers between devices  4.43 us (43%)
  waiting for transfers between devices  0.37 us (4%)
    pallas_call x6, Pallas kernels, called(): pl.pallas_call(kernel, out_shape=outs, in_specs=[specs] * len(inputs), ou...  5.3 us
    ppermute x1, starting transfers between devices, per_device(): near = lax.ppermute(sent[0], ('ta', 'gx', 'gy'), pairs)  2.89 us
    ppermute x5, starting transfers between devices, crossed(): return lax.ppermute(value, 'gx', [(0, 1), (1, 0)])  1.54 us
    ppermute x1, waiting for transfers between devices, per_device(): near = lax.ppermute(sent[0], ('ta', 'gx', 'gy'), pairs)  0.21 us
  transfers between devices with their start and end apart: 6, of which 3 were waited for; matrix products, arithmetic and copies ran while one was open for 0% of the time, Pallas kernels for 44%

profile of v10, /device:TPU:0, one launch (start us, length us, event | category | flops | bytes accessed | tf_op | source)
XLA Modules:
  0.0 10.1 jit_solution(2587809279122533139)
XLA Ops:
  0.0 0.5 %collective-permute-start = (f32[2,32,1024]{2,1,0:T(8,128)}, f32[2,32,1024]{2,1,0:T(8,128)S(1)}, u32[]{:S(2)}, u32[]{:S(2)}) collective-permute-start(f32[2,32,1024]{2,1,0:T(8,128)} %state.1), channel_id=1, source_target_pairs={{0,4},{4,0},{1,5},{5,1},{2,6},{6,2},{3,7},{7,3},{8,12},{12,8},{9,1... | collective-permute-start | bytes 786440 | tf_op jit(solution)/shard_map/ppermute | solution.py:761
  0.5 0.1 collective-permute-start.1
  0.5 0.5 %collective-permute-start.2 = (f32[32,1024]{1,0:T(8,128)}, f32[32,1024]{1,0:T(8,128)S(1)}, u32[]{:S(2)}, u32[]{:S(2)}) collective-permute-start(f32[32,1024]{1,0:T(8,128)} %kill.1), channel_id=1, source_target_pairs={{0,4},{4,0},{1,5},{5,1},{2,6},{6,2},{3,7},{7,3},{8,12},{12,8},{9,1... | collective-permute-start | bytes 393224 | tf_op jit(solution)/shard_map/ppermute | solution.py:761
  1.0 1.1 %fetch.1 = (f32[32,1024]{1,0:T(8,128)S(1)}, f32[32,1024]{1,0:T(8,128)S(1)}, f32[32,1024]{1,0:T(8,128)S(1)}, f32[32,1024]{1,0:T(8,128)S(1)}) custom-call(f32[2,32,1024]{2,1,0:T(8,128)} %state.1, f32[32,1024]{1,0:T(8,128)} %feed.1, f32[32,1024]{1,0:T(8,128)} %kill.1), custom_call_target="tpu_custom_call" | custom-call | tf_op jit(solution)/shard_map/fetch/pallas_call | solution.py:733
  2.1 0.0 collective-permute-done.1.refs_5_
  2.1 0.1 collective-permute-done.2.refs_6_
  2.2 0.0 collective-permute-done.refs_4_
  2.2 0.1 %pack.1 = f32[48,128]{1,0:T(8,128)S(1)} custom-call(f32[32,1024]{1,0:T(8,128)S(1)} %get-tuple-element.22.refs_0_, f32[32,1024]{1,0:T(8,128)S(1)} %get-tuple-element.23.refs_1_, f32[32,1024]{1,0:T(8,128)S(1)} %get-tuple-element.24.refs_2_, f32[32,1024]{1,0:T(8,128)S(1)} %get-tuple-element.25.refs_3_, f32[2,32,1024]{2,1,0:T(8,128)S(1)} %collective-permute-done.refs_4_, ...), custom_call_target="tpu_custom_call" | custom-call | tf_op jit(solution)/shard_map/pack/pallas_call | solution.py:733
  2.4 2.9 %collective-permute-start.3 = (f32[48,128]{1,0:T(8,128)S(1)}, f32[48,128]{1,0:T(8,128)S(1)}, u32[]{:S(2)}, u32[]{:S(2)}) collective-permute-start(f32[48,128]{1,0:T(8,128)S(1)} %pack.1), channel_id=1, source_target_pairs={{0,1},{1,0},{2,3},{3,2},{5,6},{6,5},{4,12},{7,15},{8,9},{9,8},{10,... | collective-permute-start | bytes 73736 | tf_op jit(solution)/shard_map/ppermute | solution.py:784
  5.2 1.6 %interior.1 = (f32[4,64,256]{2,1,0:T(8,128)S(1)}, f32[8,32,256]{2,1,0:T(8,128)S(1)}, f32[8,32,256]{2,1,0:T(8,128)S(1)}, f32[8,32,256]{2,1,0:T(8,128)S(1)}, f32[20,32,256]{2,1,0:T(8,128)S(1)}) custom-call(f32[32,1024]{1,0:T(8,128)S(1)} %get-tuple-element.22.refs_0_, f32[32,1024]{1,0:T(8,128)S(1)} %get-tuple-element.23.refs_1_, ...), custom_call_target="tpu_custom_call" | custom-call | flops 16777216 | bytes 8388608 | tf_op jit(solution)/shard_map/interior/pallas_call | solution.py:733
  6.8 0.2 %collective-permute-done.3.near = f32[48,128]{1,0:T(8,128)S(1)} collective-permute-done((f32[48,128]{1,0:T(8,128)S(1)}, f32[48,128]{1,0:T(8,128)S(1)}, u32[]{:S(2)}, u32[]{:S(2)}) %collective-permute-start.3) | collective-permute-done | bytes 24608 | tf_op jit(solution)/shard_map/ppermute | solution.py:784
  7.0 0.0 collective-permute-start.5
  7.1 0.6 %own.1 = (f32[2,32,512]{2,1,0:T(8,128)S(1)}, f32[2,32,512]{2,1,0:T(8,128)S(1)}) custom-call(f32[8,32,256]{2,1,0:T(8,128)S(1)} %get-tuple-element.31.refs_0_, f32[8,32,256]{2,1,0:T(8,128)S(1)} %get-tuple-element.32.refs_1_, f32[8,32,256]{2,1,0:T(8,128)S(1)} %get-tuple-element.33.refs_2_, f32[20,32,256]{2,1,0:T(8,128)S(1)} %get-tuple-element.34.refs_3_), custom_call_target="tpu_custom_call" | custom-call | flops 17179869184 | bytes 8589934592 | tf_op jit(solution)/shard_map/own/pallas_call | solution.py:733
  7.6 0.6 %collective-permute-start.4 = (f32[2,32,512]{2,1,0:T(8,128)S(1)}, f32[2,32,512]{2,1,0:T(8,128)S(1)}, u32[]{:S(2)}, u32[]{:S(2)}) collective-permute-start(f32[2,32,512]{2,1,0:T(8,128)S(1)} %get-tuple-element.36), channel_id=1, source_target_pairs={{0,4},{4,0},{1,5},{5,1},{2,6},{6,2},{3,7},{7,3},{8,12},{12,8},{9,1... | collective-permute-start | bytes 393224 | tf_op jit(solution)/shard_map/ppermute | solution.py:761
  8.2 0.1 collective-permute-done.5.far
  8.2 1.1 %border.1 = f32[4,2,32,128]{3,2,1,0:T(8,128)S(1)} custom-call(f32[4,64,256]{2,1,0:T(8,128)S(1)} %get-tuple-element.37.window, f32[48,128]{1,0:T(8,128)S(1)} %collective-permute-done.3.near, f32[48,128]{1,0:T(8,128)S(1)} %collective-permute-done.5.far), custom_call_target="tpu_custom_call" | custom-call | flops 17179869184 | bytes 8589934592 | tf_op jit(solution)/shard_map/border/pallas_call | solution.py:733
  9.4 0.0 collective-permute-done.4.got
  9.4 0.7 %final.1 = f32[1,2,32,1024]{3,2,1,0:T(8,128)} custom-call(f32[2,32,512]{2,1,0:T(8,128)S(1)} %get-tuple-element.35.keep, f32[2,32,512]{2,1,0:T(8,128)S(1)} %collective-permute-done.4.got, f32[4,2,32,128]{3,2,1,0:T(8,128)S(1)} %border.1), custom_call_target="tpu_custom_call" | custom-call | tf_op jit(solution)/shard_map/final/pallas_call | solution.py:733
Async XLA Ops:
  0.0 2.2 %collective-permute-start = (f32[2,32,1024]{2,1,0:T(8,128)}, f32[2,32,1024]{2,1,0:T(8,128)S(1)}, u32[]{:S(2)}, u32[]{:S(2)}) collective-permute-start(f32[2,32,1024]{2,1,0:T(8,128)} %state.1), channel_id=1, source_target_pairs={{0,4},{4,0},{1,5},{5,1},{2,6},{6,2},{3,7},{7,3},{8,12},{12,8},{9,1... | collective-permute-start | bytes 786440 | tf_op jit(solution)/shard_map/ppermute | solution.py:761
  0.5 1.6 %collective-permute-start.1 = (f32[32,1024]{1,0:T(8,128)}, f32[32,1024]{1,0:T(8,128)S(1)}, u32[]{:S(2)}, u32[]{:S(2)}) collective-permute-start(f32[32,1024]{1,0:T(8,128)} %feed.1), channel_id=1, source_target_pairs={{0,4},{4,0},{1,5},{5,1},{2,6},{6,2},{3,7},{7,3},{8,12},{12,8},{9,1... | collective-permute-start | bytes 393224 | tf_op jit(solution)/shard_map/ppermute | solution.py:761
  0.5 1.7 %collective-permute-start.2 = (f32[32,1024]{1,0:T(8,128)}, f32[32,1024]{1,0:T(8,128)S(1)}, u32[]{:S(2)}, u32[]{:S(2)}) collective-permute-start(f32[32,1024]{1,0:T(8,128)} %kill.1), channel_id=1, source_target_pairs={{0,4},{4,0},{1,5},{5,1},{2,6},{6,2},{3,7},{7,3},{8,12},{12,8},{9,1... | collective-permute-start | bytes 393224 | tf_op jit(solution)/shard_map/ppermute | solution.py:761
  2.4 4.7 %collective-permute-start.3 = (f32[48,128]{1,0:T(8,128)S(1)}, f32[48,128]{1,0:T(8,128)S(1)}, u32[]{:S(2)}, u32[]{:S(2)}) collective-permute-start(f32[48,128]{1,0:T(8,128)S(1)} %pack.1), channel_id=1, source_target_pairs={{0,1},{1,0},{2,3},{3,2},{5,6},{6,5},{4,12},{7,15},{8,9},{9,8},{10,... | collective-permute-start | bytes 73736 | tf_op jit(solution)/shard_map/ppermute | solution.py:784
  7.0 1.2 %collective-permute-start.5 = (f32[48,128]{1,0:T(8,128)S(1)}, f32[48,128]{1,0:T(8,128)S(1)}, u32[]{:S(2)}, u32[]{:S(2)}) collective-permute-start(f32[48,128]{1,0:T(8,128)S(1)} %collective-permute-done.3.near), channel_id=1, source_target_pairs={{0,4},{4,0},{1,5},{5,1},{2,6},{6,2},{3,7},{7,3},{8,12},{12,8},{9,1... | collective-permute-start | bytes 73736 | tf_op jit(solution)/shard_map/ppermute | solution.py:761
  7.6 1.8 %collective-permute-start.4 = (f32[2,32,512]{2,1,0:T(8,128)S(1)}, f32[2,32,512]{2,1,0:T(8,128)S(1)}, u32[]{:S(2)}, u32[]{:S(2)}) collective-permute-start(f32[2,32,512]{2,1,0:T(8,128)S(1)} %get-tuple-element.36), channel_id=1, source_target_pairs={{0,4},{4,0},{1,5},{5,1},{2,6},{6,2},{3,7},{7,3},{8,12},{12,8},{9,1... | collective-permute-start | bytes 393224 | tf_op jit(solution)/shard_map/ppermute | solution.py:761
